TPU v7x, 32 devices: a whole 2x2x4 slice. The times are simulated.
32 devices in a mesh: panel: 4 (over y, x), inc: 8 (over z, core).
Axes of the slice: x: 2, y: 2, z: 4, core: 2. Of those that a mesh axis runs over, the one named last changes fastest.
Arguments:
- surface_field: bfloat16 [2, 128, 2048], P(None, 'inc', 'panel'), may hold values from -6 to 6
- near_block: bfloat16 [16, 128, 8, 2, 128], P('panel', 'inc'), may hold values from -0.125 to 0.125
- near_index: int32 [16, 8], P('panel'), may hold values from 0 to 15, as said below
- source_basis: bfloat16 [16, 2, 16, 128], P('panel'), may hold values from -0.375 to 0.375
- coupling: bfloat16 [16, 2, 16, 256], P('panel'), may hold values from -0.375 to 0.375
- target_basis: bfloat16 [16, 2, 16, 128], P('panel'), may hold values from -1 to 1
- far_rank: int32 [16, 16], P('panel'), may hold values from 1 to 16, as said below
Outputs:
- applied_field: bfloat16 [2, 128, 2048], P(None, 'inc', 'panel')
Inputs may be any that keep to these rules, and one draw needn't show every extreme that they name: `near_index`: each row names 8 distinct blocks within 4 blocks of its own block i around the closed order of blocks (index modulo 16); slot 0 names i, slot 1 names i - 4 and slot 2 names i + 4. `far_rank`: entries of pairs named in near_index are not used; every block i has rank 16 toward block i + 8.
All inputs are finite; a program needn't handle non-finite values.
Results may differ from a plain program's by a relative error of at most 0.0042.
Values may be sent and summed in bfloat16 or wider, within the bound.
No kernel may reach another device: no remote copies, remote signals or barrier semaphores. Data moves between devices by JAX's collectives and lax.ppermute only.
A program may use at most 64 MiB of HBM per device.

v0:
```python
import jax
import jax.numpy as jnp
from jax import lax
from jax.sharding import PartitionSpec as P


def extended(block, sides, width):
    for axis, dim in sides:
        count = lax.axis_size(axis)
        forward = [(i, i + 1) for i in range(count - 1)]
        forward.append((count - 1, 0))
        backward = [(target, source) for source, target in forward]
        low = lax.ppermute(
            lax.slice_in_dim(block, block.shape[dim] - width, None, axis=dim), axis, forward
        )
        high = lax.ppermute(lax.slice_in_dim(block, 0, width, axis=dim), axis, backward)
        block = jnp.concatenate([low, block, high], axis=dim)
    return block


def near_product(coefficients, window, window_blocks):
    slots = coefficients.shape[2]
    running = None
    for near_slot in range(slots):
        source = jnp.take(window, window_blocks[:, near_slot], axis=2)
        part_a = jnp.einsum(
            "brs,pmbs->pmbr",
            coefficients[:, :, near_slot, 0],
            source,
            preferred_element_type=jnp.float32,
        )
        part_b = jnp.einsum(
            "brs,pmbs->pmbr",
            coefficients[:, :, near_slot, 1],
            source,
            preferred_element_type=jnp.float32,
        )
        addend = jnp.stack([part_a[0] - part_b[1], part_a[1] + part_b[0]])
        running = addend if running is None else running + addend
    return running


def local(surface_field, near_block, near_index, source_basis, coupling, target_basis, far_rank):
    own_blocks = near_index.shape[0]
    block_size = near_block.shape[4]
    inc_local = surface_field.shape[1]
    rank_most = source_basis.shape[2]
    block_count = own_blocks * lax.axis_size("panel")
    first_block = lax.axis_index("panel") * own_blocks
    local_ids = jnp.arange(own_blocks, dtype=jnp.int32)
    targets = first_block + local_ids
    offsets = (near_index - targets[:, None] + own_blocks) % block_count
    window_blocks = offsets + local_ids[:, None]
    everyone = lax.all_gather(surface_field, "inc", axis=1, tiled=True)
    window = extended(everyone, (("panel", 2),), own_blocks * block_size)
    window = window.reshape(2, everyone.shape[1], own_blocks + 2 * own_blocks, block_size)
    near_rows = near_product(near_block, window, window_blocks)
    near_local = lax.all_to_all(near_rows, "inc", split_axis=1, concat_axis=3, tiled=True)
    field_blocks = surface_field.reshape(2, inc_local, own_blocks, block_size)
    part_a = jnp.einsum(
        "bas,pmbs->pbam", source_basis[:, 0], field_blocks, preferred_element_type=jnp.float32
    )
    part_b = jnp.einsum(
        "bas,pmbs->pbam", source_basis[:, 1], field_blocks, preferred_element_type=jnp.float32
    )
    compressed = jnp.stack([part_a[0] - part_b[1], part_a[1] + part_b[0]]).astype(jnp.bfloat16)
    compressed = compressed.reshape(2, own_blocks * rank_most, inc_local)
    columns = jnp.arange(block_count * rank_most, dtype=jnp.int32)
    within = columns % rank_most
    block_ids = jnp.arange(block_count, dtype=jnp.int32)
    is_near = jnp.any(near_index[:, :, None] == block_ids[None, None, :], axis=1)
    rank_cols = jnp.repeat(far_rank, rank_most, axis=1)
    near_cols = jnp.repeat(is_near, rank_most, axis=1)
    rows_a = jnp.arange(rank_most, dtype=jnp.int32)
    keep = (
        (rows_a[None, :, None] < rank_cols[:, None, :])
        & (within[None, None, :] < rank_cols[:, None, :])
        & jnp.logical_not(near_cols[:, None, :])
    )
    masked = coupling * keep[:, None].astype(jnp.bfloat16)
    piece = lax.all_gather(compressed, "panel", axis=1, tiled=True)
    first_a = jnp.einsum("bac,pcn->pban", masked[:, 0], piece, preferred_element_type=jnp.float32)
    first_b = jnp.einsum("bac,pcn->pban", masked[:, 1], piece, preferred_element_type=jnp.float32)
    mixed = jnp.stack([first_a[0] - first_b[1], first_a[1] + first_b[0]]).astype(jnp.bfloat16)
    part_a = jnp.einsum(
        "bat,pban->pnbt", target_basis[:, 0], mixed, preferred_element_type=jnp.float32
    )
    part_b = jnp.einsum(
        "bat,pban->pnbt", target_basis[:, 1], mixed, preferred_element_type=jnp.float32
    )
    far = jnp.stack([part_a[0] - part_b[1], part_a[1] + part_b[0]])
    result = field_blocks.astype(jnp.float32) * 0.5 + near_local + far
    return result.reshape(2, inc_local, own_blocks * block_size).astype(jnp.bfloat16)


def solution(mesh):
    return jax.shard_map(
        local,
        mesh=mesh,
        in_specs=(
            P(None, "inc", "panel"),
            P("panel", "inc", None, None, None),
            P("panel", None),
            P("panel", None, None, None),
            P("panel", None, None, None),
            P("panel", None, None, None),
            P("panel", None),
        ),
        out_specs=P(None, "inc", "panel"),
        check_vma=False,
    )
```

profile of v0, /device:TPU:0, one launch (start us, length us, event | category | flops | bytes accessed | tf_op | source)
XLA Modules:
  0.0 61.8 jit_solution(2309359780913941923)
XLA Ops:
  0.0 0.9 %copy.171 = bf16[2,16,512]{2,0,1:T(2,128)(2,1)S(1)} copy(bf16[2,16,512]{2,1,0:T(8,128)(2,1)} %param.9) | data formatting | bytes 65536 | tf_op args[0]
  0.9 15.9 %all_gather.6 = bf16[2,128,512]{2,0,1:T(2,128)(2,1)S(1)} all-gather(bf16[2,16,512]{2,0,1:T(2,128)(2,1)S(1)} %copy.171), channel_id=1, replica_groups=mesh['panel'=4,'inc'=8] {'inc'}, dimensions={1}, use_global_device_ids=true | all-gather | bytes 294912 | tf_op jit(solution)/shard_map/all_gather | solution.py:54
  16.8 0.2 copy.172
  17.0 1.5 %collective-permute-start = (bf16[2,128,512]{1,2,0:T(8,128)(2,1)S(1)}, bf16[2,128,512]{1,2,0:T(8,128)(2,1)S(1)}, u32[]{:S(2)}, u32[]{:S(2)}) collective-permute-start(bf16[2,128,512]{1,2,0:T(8,128)(2,1)S(1)} %copy.172), channel_id=1, source_target_pairs={{0,8},{8,16},{16,24},{24,0},{1,9},{9,17},{17,25},{25,1},{2,10},{10... | collective-permute-start | bytes 786440 | tf_op jit(solution)/shard_map/ppermute | solution.py:13
  18.5 1.4 %collective-permute-start.1 = (bf16[2,128,512]{1,2,0:T(8,128)(2,1)S(1)}, bf16[2,128,512]{1,2,0:T(8,128)(2,1)S(1)}, u32[]{:S(2)}, u32[]{:S(2)}) collective-permute-start(bf16[2,128,512]{1,2,0:T(8,128)(2,1)S(1)} %copy.172), channel_id=1, source_target_pairs={{8,0},{16,8},{24,16},{0,24},{9,1},{17,9},{25,17},{1,25},{10,2},{18... | collective-permute-start | bytes 786440 | tf_op jit(solution)/shard_map/ppermute | solution.py:16
  20.0 0.1 fusion.46
  20.1 0.3 slice_reduce_fusion
  20.5 0.0 copy-start.4
  20.5 0.1 convolution_bitcast_fusion.4
  20.6 0.1 convolution_bitcast_fusion.5
  20.8 0.1 fusion.44
  20.8 0.0 copy-start
  20.9 0.1 stack.72
  21.0 0.1 stack.73
  21.1 0.1 copy.207
  21.2 13.8 %all_gather.7 = bf16[2,256,16]{2,0,1:T(2,128)(2,1)S(1)} all-gather(bf16[2,64,16]{2,0,1:T(2,128)(2,1)S(1)} %copy.207), channel_id=1, replica_groups=mesh['panel'=4,'inc'=8] {'panel'}, dimensions={1}, use_global_device_ids=true | all-gather | bytes 20480 | tf_op jit(solution)/shard_map/all_gather | solution.py:81
  35.0 0.1 copy.237
  35.0 0.1 broadcast_in_dim.13
  35.1 0.1 lt.49
  35.2 0.1 broadcast_in_dim.14
  35.3 0.1 not.13
  35.5 0.1 convolution_bitcast_fusion.3
  35.6 0.2 convolution_bitcast_fusion.2
  35.8 0.1 convolution_bitcast_fusion.1
  35.9 0.1 convolution_bitcast_fusion
  36.2 0.5 fusion.63
  36.7 0.0 collective-permute-done
  36.7 0.0 collective-permute-done.1
  36.7 0.1 pad_maximum_fusion
  36.8 0.4 copy.175
  37.1 0.6 gather_fusion.7
  37.8 0.2 convolution_bitcast_fusion.6
  38.0 0.3 convolution_bitcast_fusion.7
  38.3 0.6 gather_fusion.6
  38.9 0.2 convolution_bitcast_fusion.8
  39.1 0.3 convolution_bitcast_fusion.9
  39.4 0.6 gather_fusion.5
  40.0 0.2 convolution_bitcast_fusion.10
  40.2 0.3 convolution_bitcast_fusion.11
  40.5 0.6 gather_fusion.4
  41.1 0.2 convolution_bitcast_fusion.12
  41.4 0.3 convolution_bitcast_fusion.13
  41.6 0.6 gather_fusion.3
  42.2 0.2 convolution_bitcast_fusion.14
  42.5 0.3 convolution_bitcast_fusion.15
  42.7 0.6 gather_fusion.2
  43.4 0.2 convolution_bitcast_fusion.16
  43.6 0.3 convolution_bitcast_fusion.17
  43.9 0.6 gather_fusion.1
  44.5 0.2 convolution_bitcast_fusion.18
  44.7 0.3 convolution_bitcast_fusion.19
  45.0 0.6 gather_fusion
  45.6 0.2 convolution_bitcast_fusion.21
  45.8 0.3 convolution_bitcast_fusion.20
  46.3 0.3 copy.199
  46.7 1.3 %reshape.193 = f32[8,1,2048]{2,1,0:T(1,128)} reshape(f32[128,4,2,16]{3,2,1,0:T(2,128)S(1)} %bitcast.268) | data formatting | bytes 131072
  48.0 4.7 %all-to-all-start = ((f32[8,1,2048]{2,1,0:T(1,128)}), f32[8,1,2048]{2,1,0:T(1,128)S(1)}, u32[]{:S(2)}, u32[]{:S(2)}) async-start(f32[8,1,2048]{2,1,0:T(1,128)} %reshape.193), calls=%async_computation | async-start | bytes 131072 | tf_op jit(solution)/shard_map/all_to_all | solution.py:58
  52.8 5.8 %all-to-all-done = f32[8,1,2048]{2,1,0:T(1,128)S(1)} async-done(((f32[8,1,2048]{2,1,0:T(1,128)}), f32[8,1,2048]{2,1,0:T(1,128)S(1)}, u32[]{:S(2)}, u32[]{:S(2)}) %all-to-all-start) | async-done | bytes 65568 | tf_op jit(solution)/shard_map/all_to_all | solution.py:58
  58.6 0.5 broadcast.372
  59.1 0.8 %reduce.16 = f32[8,2048]{1,0:T(8,128)S(1)} reduce(f32[8,1,2048]{2,1,0:T(1,128)S(1)} %all-to-all-done, f32[]{:T(128)} %broadcast.372), dimensions={1}, to_apply=%all_to_all.13.reduce_sub_computation | reduce | bytes 131076 | tf_op jit(solution)/shard_map/all_to_all | solution.py:58
  59.9 0.7 %reshape.194 = f32[128,4,2,16]{3,2,1,0:T(2,128)S(1)} reshape(f32[8,2048]{1,0:T(8,128)S(1)} %reduce.16) | data formatting | bytes 131072
  60.6 0.3 copy.312
  61.0 0.3 all_to_all.16
  61.2 0.6 %fusion.22 = bf16[2,16,512]{2,1,0:T(8,128)(2,1)} fusion(f32[1,16,512]{2,1,0:T(8,128)S(1)} %copy.218, f32[1,16,512]{2,1,0:T(8,128)S(1)} %copy.217, f32[2,16,512]{2,1,0:T(8,128)S(1)} %all_to_all.16, bf16[2,16,512]{2,1,0:T(8,128)(2,1)S(1)} %copy-done.1), kind=kLoop, calls=%fused_computation.64 | loop fusion | flops 98304 | bytes 196608 | tf_op jit(solution)/shard_map/convert_element_type | solution.py:93
  (53 shorter events, 0.4 us)
Async XLA Ops:
  0.0 20.5 %copy-start.1 = (bf16[2,16,512]{2,1,0:T(8,128)(2,1)S(1)}, bf16[2,16,512]{2,1,0:T(8,128)(2,1)}, u32[]{:S(2)}) copy-start(bf16[2,16,512]{2,1,0:T(8,128)(2,1)} %param.9) | copy-start | bytes 98308
  0.0 20.0 %copy-start.5 = (s32[4,8]{1,0:T(4,128)S(1)}, s32[4,8]{1,0:T(4,128)}, u32[]{:S(2)}) copy-start(s32[4,8]{1,0:T(4,128)} %param.11) | copy-start | bytes 388
  0.0 20.5 %copy-start.3 = (bf16[4,2,16,128]{3,2,1,0:T(8,128)(2,1)S(1)}, bf16[4,2,16,128]{3,2,1,0:T(8,128)(2,1)}, u32[]{:S(2)}) copy-start(bf16[4,2,16,128]{3,2,1,0:T(8,128)(2,1)} %param.12) | copy-start | bytes 98308
  16.8 18.3 %copy-start.6 = (s32[4,16]{1,0:T(4,128)S(1)}, s32[4,16]{1,0:T(4,128)}, u32[]{:S(2)}) copy-start(s32[4,16]{1,0:T(4,128)} %param.15) | copy-start | bytes 772
  16.8 18.7 %copy-start.2 = (bf16[4,2,16,256]{3,2,1,0:T(8,128)(2,1)S(1)}, bf16[4,2,16,256]{3,2,1,0:T(8,128)(2,1)}, u32[]{:S(2)}) copy-start(bf16[4,2,16,256]{3,2,1,0:T(8,128)(2,1)} %param.13) | copy-start | bytes 196612
  17.0 19.7 %collective-permute-start = (bf16[2,128,512]{1,2,0:T(8,128)(2,1)S(1)}, bf16[2,128,512]{1,2,0:T(8,128)(2,1)S(1)}, u32[]{:S(2)}, u32[]{:S(2)}) collective-permute-start(bf16[2,128,512]{1,2,0:T(8,128)(2,1)S(1)} %copy.172), channel_id=1, source_target_pairs={{0,8},{8,16},{16,24},{24,0},{1,9},{9,17},{17,25},{25,1},{2,10},{10... | collective-permute-start | bytes 786440 | tf_op jit(solution)/shard_map/ppermute | solution.py:13
  18.5 18.2 %collective-permute-start.1 = (bf16[2,128,512]{1,2,0:T(8,128)(2,1)S(1)}, bf16[2,128,512]{1,2,0:T(8,128)(2,1)S(1)}, u32[]{:S(2)}, u32[]{:S(2)}) collective-permute-start(bf16[2,128,512]{1,2,0:T(8,128)(2,1)S(1)} %copy.172), channel_id=1, source_target_pairs={{8,0},{16,8},{24,16},{0,24},{9,1},{17,9},{25,17},{1,25},{10,2},{18... | collective-permute-start | bytes 786440 | tf_op jit(solution)/shard_map/ppermute | solution.py:16
  20.5 15.3 %copy-start.4 = (bf16[4,2,16,128]{3,2,1,0:T(8,128)(2,1)S(1)}, bf16[4,2,16,128]{3,2,1,0:T(8,128)(2,1)}, u32[]{:S(2)}) copy-start(bf16[4,2,16,128]{3,2,1,0:T(8,128)(2,1)} %param.14) | copy-start | bytes 98308
  20.8 15.3 %copy-start = (bf16[4,16,8,2,128]{4,3,2,1,0:T(2,128)(2,1)S(1)}, bf16[4,16,8,2,128]{4,3,2,1,0:T(2,128)(2,1)}, u32[]{:S(2)}) copy-start(bf16[4,16,8,2,128]{4,3,2,1,0:T(2,128)(2,1)} %param.10) | copy-start | bytes 786436
  48.0 10.6 %all-to-all-start = ((f32[8,1,2048]{2,1,0:T(1,128)}), f32[8,1,2048]{2,1,0:T(1,128)S(1)}, u32[]{:S(2)}, u32[]{:S(2)}) async-start(f32[8,1,2048]{2,1,0:T(1,128)} %reshape.193), calls=%async_computation | async-start | bytes 131072 | tf_op jit(solution)/shard_map/all_to_all | solution.py:58
where the time goes:
time: 62.1 us; the launch traced here: 61.8 us
  blocking collectives  29.6 us (48%)
  local copies, waits for them, and re-layouts  11.4 us (18%)
  starting transfers between devices  7.66 us (12%)
  waiting for transfers between devices  5.84 us (9%)
  matrix products  4.79 us (8%)
  other arithmetic  1.98 us (3%)
    all_gather x1, blocking collectives, local(): everyone = lax.all_gather(surface_field, 'inc', axis=1, tiled=True)  15.9 us
    all_gather x1, blocking collectives, local(): piece = lax.all_gather(compressed, 'panel', axis=1, tiled=True)  13.8 us
    all_to_all x1, waiting for transfers between devices, local(): lax.all_to_all(near_rows, 'inc', split_axis=1, concat_axis=3, tiled=True)  5.84 us
    gather x8, local copies, waits for them, and re-layouts, near_product(): source = jnp.take(window, window_blocks[:, near_slot], axis=2)  4.89 us
    all_to_all x1, starting transfers between devices, local(): lax.all_to_all(near_rows, 'inc', split_axis=1, concat_axis=3, tiled=True)  4.68 us
    unnamed x17, local copies, waits for them, and re-layouts  2.95 us
    dot_general x8, matrix products, near_product(): jnp.einsum('brs,pmbs->pmbr', coefficients[:, :, near_slot, 0], source, pr...  2.05 us
    dot_general x8, matrix products, near_product(): jnp.einsum('brs,pmbs->pmbr', coefficients[:, :, near_slot, 1], source, pr...  1.95 us
  transfers between devices with their start and end apart: 3, of which 1 were waited for; matrix products, arithmetic and copies ran while one was open for 4% of the time, Pallas kernels for 0%

commit v1 on v0

v1 whole, which is shorter than its diff:
```python
import functools

import jax
import jax.numpy as jnp
from jax import lax
from jax.experimental import pallas as pl
from jax.experimental.pallas import tpu as pltpu
from jax.sharding import PartitionSpec as P

F32 = jnp.float32
BF16 = jnp.bfloat16
LANES = 128
VMEM = pl.BlockSpec(memory_space=pltpu.VMEM)
SMEM = pl.BlockSpec(memory_space=pltpu.SMEM)
PARAMS = pltpu.CompilerParams(vmem_limit_bytes=8 * 1024 * 1024)


def nt_dot(left, right):
    return lax.dot_general(left, right, (((1,), (1,)), ((), ())), preferred_element_type=F32)


def tn_dot(left, right):
    return lax.dot_general(left, right, (((0,), (0,)), ((), ())), preferred_element_type=F32)


def times_i(pair_rows, width):
    return jnp.concatenate([-pair_rows[width:], pair_rows[:width]], axis=0)


def times_i_lanes(pair_lanes, width):
    return jnp.concatenate([-pair_lanes[:, width:], pair_lanes[:, :width]], axis=1)


def pack_kernel(own_ref, other_ref, basis_ref, payload_ref, packed_ref):
    _, inc, panels = own_ref.shape
    blocks, _, rank, block = basis_ref.shape
    for part in range(2):
        payload_ref[part * inc : (part + 1) * inc, :panels] = own_ref[part]
        payload_ref[(2 + part) * inc : (3 + part) * inc, :panels] = other_ref[part]
    if payload_ref.shape[0] > 4 * inc:
        payload_ref[4 * inc :, :panels] = jnp.zeros((payload_ref.shape[0] - 4 * inc, panels), BF16)
    pieces = []
    for j in range(blocks):
        basis = jnp.concatenate([basis_ref[j, 0], basis_ref[j, 1]], axis=0)
        field = jnp.concatenate(
            [own_ref[part][:, j * block : (j + 1) * block] for part in range(2)], axis=0
        )
        both = nt_dot(basis, field)
        pieces.append(both[:rank] + times_i_lanes(both[rank:], inc))
    compressed = jnp.concatenate(pieces, axis=0)
    pad = packed_ref.shape[1] - 2 * inc
    compressed = jnp.concatenate([compressed, jnp.zeros((blocks * rank, pad), F32)], axis=1)
    compressed = compressed.astype(BF16)
    packed_ref[...] = compressed
    payload_ref[: blocks * rank, panels:] = compressed
    if payload_ref.shape[0] > blocks * rank:
        payload_ref[blocks * rank :, panels:] = jnp.zeros(
            (payload_ref.shape[0] - blocks * rank, packed_ref.shape[1]), BF16
        )


def near_kernel(pieces, inc, block, slots, *refs):
    picks_ref = refs[0]
    window_refs = refs[1:4]
    coefs_refs = refs[4 : 4 + pieces]
    keep_ref, send_ref, wide_ref = refs[4 + pieces :]
    blocks = coefs_refs[0].shape[0]
    rows = 4 * inc
    for w in range(3):
        piece = window_refs[w][:rows, : blocks * block]
        turned = jnp.concatenate(
            [times_i(piece[: 2 * inc], inc), times_i(piece[2 * inc :], inc)], axis=0
        )
        for b in range(blocks):
            at = (w * blocks + b) * 2 * block
            wide_ref[:, at : at + block] = piece[:, b * block : (b + 1) * block]
            wide_ref[:, at + block : at + 2 * block] = turned[:, b * block : (b + 1) * block]
    for i in range(blocks):
        total = None
        for k in range(slots):
            start = pl.multiple_of(picks_ref[i, k] * (2 * block), 2 * block)
            field = wide_ref[:, pl.ds(start, 2 * block)]
            span = slice(k * 2 * block, (k + 1) * 2 * block)
            coefs = [ref[i, :, span] for ref in coefs_refs]
            coefs = coefs[0] if pieces == 1 else jnp.concatenate(coefs, axis=0)
            term = nt_dot(field, coefs)
            total = term if total is None else total + term
        width = total.shape[1]
        keep_ref[:, i * width : (i + 1) * width] = total[: 2 * inc]
        send_ref[:, i * width : (i + 1) * width] = total[2 * inc :].astype(BF16)


def far_kernel(count, inc, index_ref, near_ref, rank_ref, coupling_ref, target_ref, *refs):
    piece_refs = refs[:count]
    far_ref, gathered_ref = refs[count:]
    blocks, _, rank, columns = coupling_ref.shape
    block = target_ref.shape[3]
    size = blocks * rank
    me = index_ref[0]
    for k in range(count):
        at = lax.rem(me + k, count) * size
        at = pl.multiple_of(at, size)
        ref = piece_refs[k]
        lane = ref.shape[1] - gathered_ref.shape[1]
        gathered_ref[pl.ds(at, size), :] = ref[:size, lane:]
    block_id = lax.broadcasted_iota(jnp.int32, (rank, columns), 1) // rank
    within = lax.broadcasted_iota(jnp.int32, (rank, columns), 1) % rank
    row = lax.broadcasted_iota(jnp.int32, (rank, columns), 0)
    largest = jnp.maximum(within, row)
    masked = [[], []]
    for i in range(blocks):
        ranks = jnp.zeros((rank, columns), jnp.int32)
        for j in range(columns // rank):
            ranks = jnp.where(block_id == j, rank_ref[i, j], ranks)
        keep = largest < ranks
        for k in range(near_ref.shape[1]):
            keep = keep & (block_id != near_ref[i, k])
        for part in range(2):
            value = coupling_ref[i, part].astype(F32)
            masked[part].append(jnp.where(keep, value, 0.0).astype(BF16))
    masked = jnp.concatenate(masked[0] + masked[1], axis=0)
    both = jnp.dot(masked, gathered_ref[...], preferred_element_type=F32)[:, : 2 * inc]
    mixed = (both[:size] + times_i_lanes(both[size:], inc)).astype(BF16).astype(F32)
    mixed = jnp.concatenate([mixed, times_i_lanes(mixed, inc)], axis=0).astype(BF16)
    row_block = lax.broadcasted_iota(jnp.int32, (size, block), 0) // rank
    basis = [
        jnp.concatenate([target_ref[i, part] for i in range(blocks)], axis=0).astype(F32)
        for part in range(2)
    ]
    spread = [
        jnp.concatenate(
            [jnp.where(row_block == i, basis[part], 0.0) for part in range(2)], axis=0
        ).astype(BF16)
        for i in range(blocks)
    ]
    for i in range(blocks):
        far_ref[:, i * block : (i + 1) * block] = tn_dot(mixed, spread[i])


def final_kernel(count, rows, index_ref, field_ref, keep_ref, got_ref, far_ref, out_ref):
    _, inc, panels = field_ref.shape
    block = count * rows
    half = block // 2
    lane = lax.broadcasted_iota(jnp.int32, (2 * inc, block), 1)
    me = index_ref[1]
    for i in range(panels // block):
        span = slice(i * block, (i + 1) * block)
        part = slice(i * half, (i + 1) * half)
        near = jnp.concatenate([keep_ref[:, part], got_ref[:, part].astype(F32)], axis=1)
        bit = 1
        while bit < count:
            shift = bit * rows
            upper = (lane // shift) % 2 == 1
            swapped = jnp.where(
                upper, pltpu.roll(near, shift, 1), pltpu.roll(near, block - shift, 1)
            )
            near = jnp.where((me // bit) % 2 == 1, swapped, near)
            bit *= 2
        field = jnp.concatenate([field_ref[0][:, span], field_ref[1][:, span]], axis=0)
        result = (field.astype(F32) * 0.5 + near + far_ref[:, span]).astype(BF16)
        out_ref[0, :, span] = result[:inc]
        out_ref[1, :, span] = result[inc:]


def local(surface_field, near_block, near_index, source_basis, coupling, target_basis, far_rank):
    blocks, rows, slots, _, block = near_block.shape
    _, inc, panels = surface_field.shape
    rank = source_basis.shape[2]
    panel_count = lax.axis_size("panel")
    inc_count = lax.axis_size("inc")
    half = inc_count // 2
    panel_at = lax.axis_index("panel")
    inc_at = lax.axis_index("inc")

    def across(x, bit):
        return lax.ppermute(x, "inc", [(i, i ^ bit) for i in range(inc_count)])

    def onward(x, step):
        return lax.ppermute(
            x, "panel", [(i, (i - step) % panel_count) for i in range(panel_count)]
        )

    local_ids = jnp.arange(blocks, dtype=jnp.int32)[:, None]
    offsets = (near_index - (panel_at * blocks + local_ids) + blocks) % (panel_count * blocks)
    picks = jnp.minimum(offsets + local_ids, 3 * blocks - 1)
    index = jnp.stack([panel_at, inc_at]).astype(jnp.int32)

    other = across(surface_field, half)
    coefs = {0: near_block.reshape(blocks, rows, slots * 2 * block)}
    bit = half // 2
    while bit:
        for at in sorted(coefs):
            coefs[at | bit] = across(coefs[at], bit)
        bit //= 2
    coefs = [coefs[at] for at in range(half)]
    if rows % 16:
        coefs = [jnp.concatenate(coefs, axis=1)]

    height = max(4 * inc, blocks * rank)
    pad = -(-2 * inc // LANES) * LANES
    payload, packed = pl.pallas_call(
        pack_kernel,
        out_shape=(
            jax.ShapeDtypeStruct((height, panels + pad), BF16),
            jax.ShapeDtypeStruct((blocks * rank, pad), BF16),
        ),
        in_specs=[VMEM] * 3,
        out_specs=(VMEM, VMEM),
        compiler_params=PARAMS,
        name="pack",
    )(surface_field, other, source_basis)
    above = onward(payload, 1)
    below = onward(payload, panel_count - 1)
    rest = [onward(packed, k) for k in range(2, panel_count - 1)]

    width = blocks * half * rows
    keep, send = pl.pallas_call(
        functools.partial(near_kernel, len(coefs), inc, block, slots),
        out_shape=(
            jax.ShapeDtypeStruct((2 * inc, width), F32),
            jax.ShapeDtypeStruct((2 * inc, width), BF16),
        ),
        in_specs=[SMEM] + [VMEM] * (3 + len(coefs)),
        out_specs=(VMEM, VMEM),
        scratch_shapes=[pltpu.VMEM((4 * inc, 3 * blocks * 2 * block), BF16)],
        compiler_params=PARAMS,
        name="near",
    )(picks, below, payload, above, *coefs)
    got = across(send, half)

    far = pl.pallas_call(
        functools.partial(far_kernel, panel_count, inc),
        out_shape=jax.ShapeDtypeStruct((2 * inc, panels), F32),
        in_specs=[SMEM] * 3 + [VMEM] * (2 + panel_count),
        out_specs=VMEM,
        scratch_shapes=[pltpu.VMEM((panel_count * blocks * rank, pad), BF16)],
        compiler_params=PARAMS,
        name="far",
    )(index, near_index, far_rank, coupling, target_basis, packed, above, *rest, below)

    return pl.pallas_call(
        functools.partial(final_kernel, inc_count, rows),
        out_shape=jax.ShapeDtypeStruct((2, inc, panels), BF16),
        in_specs=[SMEM] + [VMEM] * 4,
        out_specs=VMEM,
        compiler_params=PARAMS,
        name="final",
    )(index, surface_field, keep, got, far)


def solution(mesh):
    return jax.shard_map(
        local,
        mesh=mesh,
        in_specs=(
            P(None, "inc", "panel"),
            P("panel", "inc", None, None, None),
            P("panel", None),
            P("panel", None, None, None),
            P("panel", None, None, None),
            P("panel", None, None, None),
            P("panel", None),
        ),
        out_specs=P(None, "inc", "panel"),
        check_vma=False,
    )
```

time: 62.1 us -> 26.7 us (0.43)
  blocking collectives: 29.6 us -> 0 us
  local copies, waits for them, and re-layouts: 11.4 us -> 1.76 us
  starting transfers between devices: 7.66 us -> 12.7 us
  matrix products: 4.79 us -> 0 us
  Pallas kernels: 0 us -> 3.95 us
  waiting for transfers between devices: 5.84 us -> 7.94 us
  other arithmetic: 1.98 us -> 0.16 us
    all_gather x2 -> x0, blocking collectives: 29.6 us -> none  [the longest x1 15.9 us: local(): everyone = lax.all_gather(surface_field, 'inc', axis=1, tiled=True)]
    ppermute x2 -> x8, starting transfers between devices: 2.98 us -> 12.7 us  [the longest x5 7.97 us: across(): return lax.ppermute(x, 'inc', [(i, i ^ bit) for i in range(inc_count)])]
    ppermute x2 -> x8, waiting for transfers between devices: 0.01 us -> 7.94 us  [the longest x5 4.99 us: across(): return lax.ppermute(x, 'inc', [(i, i ^ bit) for i in range(inc_count)])]
    all_to_all x1 -> x0, waiting for transfers between devices: 5.84 us -> none  [local(): lax.all_to_all(near_rows, 'inc', split_axis=1, concat_axis=3, tiled=True)]
    gather x8 -> x0, local copies, waits for them, and re-layouts: 4.89 us -> none  [near_product(): source = jnp.take(window, window_blocks[:, near_slot], axis=2)]
    dot_general x22 -> x0, matrix products: 4.79 us -> none  [the longest x8 2.05 us: near_product(): jnp.einsum('brs,pmbs->pmbr', coefficients[:, :, near_slot, 0], source, pr...]
    all_to_all x1 -> x0, starting transfers between devices: 4.68 us -> none  [local(): lax.all_to_all(near_rows, 'inc', split_axis=1, concat_axis=3, tiled=True)]
    pallas_call x0 -> x4, Pallas kernels: none -> 3.95 us  [the longest x1 1.49 us: local(): pl.pallas_call(functools.partial(final_kernel, inc_count, rows), out_shap...]
  transfers between devices with their start and end apart: 3 -> 8, of which waited for: 1 -> 4; matrix products, arithmetic and copies ran while one was open for 4% -> 1% of each run, Pallas kernels for 0% -> 9%
where the time goes in v1:
time: 26.7 us; the launch traced here: 26.6 us
  starting transfers between devices  12.7 us (48%)
  waiting for transfers between devices  7.94 us (30%)
  Pallas kernels  3.95 us (15%)
  local copies, waits for them, and re-layouts  1.76 us (7%)
    ppermute x5, starting transfers between devices, across(): return lax.ppermute(x, 'inc', [(i, i ^ bit) for i in range(inc_count)])  7.97 us
    ppermute x5, waiting for transfers between devices, across(): return lax.ppermute(x, 'inc', [(i, i ^ bit) for i in range(inc_count)])  4.99 us
    ppermute x3, starting transfers between devices, onward(): lax.ppermute(x, 'panel', [(i, (i - step) % panel_count) for i in range(pa...  4.73 us
    ppermute x3, waiting for transfers between devices, onward(): lax.ppermute(x, 'panel', [(i, (i - step) % panel_count) for i in range(pa...  2.95 us
    pallas_call x1, Pallas kernels, local(): pl.pallas_call(functools.partial(final_kernel, inc_count, rows), out_shap...  1.49 us
    pallas_call x1, Pallas kernels, local(): pl.pallas_call(functools.partial(far_kernel, panel_count, inc), out_shape...  1.15 us
    reshape x1, local copies, waits for them, and re-layouts, local(): coefs = {0: near_block.reshape(blocks, rows, slots * 2 * block)}  1.14 us
    pallas_call x1, Pallas kernels, local(): pl.pallas_call(functools.partial(near_kernel, len(coefs), inc, block, slo...  1.1 us
  transfers between devices with their start and end apart: 8, of which 4 were waited for; matrix products, arithmetic and copies ran while one was open for 1% of the time, Pallas kernels for 9%

profile of v1, /device:TPU:0, one launch (start us, length us, event | category | flops | bytes accessed | tf_op | source)
XLA Modules:
  0.0 26.6 jit_solution(13302540838686621330)
XLA Ops:
  0.0 0.0 copy-start
  0.0 0.0 copy-start.2
  0.0 1.1 %reshape.8.refs_4_ = bf16[4,16,2048]{2,1,0:T(8,128)(2,1)S(1)} reshape(bf16[4,16,8,2,128]{4,3,2,1,0:T(2,128)(2,1)} %param.8) | data formatting | bytes 524288 | tf_op jit(solution)/shard_map/reshape | solution.py:189
  1.1 3.1 %collective-permute-start.4 = (bf16[4,16,2048]{2,1,0:T(8,128)(2,1)S(1)}, bf16[4,16,2048]{2,1,0:T(8,128)(2,1)S(1)}, u32[]{:S(2)}, u32[]{:S(2)}) collective-permute-start(bf16[4,16,2048]{2,1,0:T(8,128)(2,1)S(1)} %reshape.8.refs_4_), channel_id=1, source_target_pairs={{0,2},{1,3},{2,0},{3,1},{4,6},{5,7},{6,4},{7,5},{8,10},{9,11},{10,... | collective-permute-start | bytes 786440 | tf_op jit(solution)/shard_map/ppermute | solution.py:176
  4.2 0.0 collective-permute-start.3
  4.2 0.0 copy-done
  4.2 2.6 %collective-permute-start = (bf16[2,16,512]{2,1,0:T(8,128)(2,1)S(1)}, bf16[2,16,512]{2,1,0:T(8,128)(2,1)S(1)}, u32[]{:S(2)}, u32[]{:S(2)}) collective-permute-start(bf16[2,16,512]{2,1,0:T(8,128)(2,1)S(1)} %copy-done), channel_id=1, source_target_pairs={{0,4},{1,5},{2,6},{3,7},{4,0},{5,1},{6,2},{7,3},{8,12},{9,13},{10,... | collective-permute-start | bytes 98312 | tf_op jit(solution)/shard_map/ppermute | solution.py:176
  6.8 4.4 %collective-permute-done.4.refs_6_ = bf16[4,16,2048]{2,1,0:T(8,128)(2,1)S(1)} collective-permute-done((bf16[4,16,2048]{2,1,0:T(8,128)(2,1)S(1)}, bf16[4,16,2048]{2,1,0:T(8,128)(2,1)S(1)}, u32[]{:S(2)}, u32[]{:S(2)}) %collective-permute-start.4) | collective-permute-done | bytes 262176 | tf_op jit(solution)/shard_map/ppermute | solution.py:176
  11.2 0.0 collective-permute-start.5
  11.2 0.0 collective-permute-done.other_ref
  11.3 0.0 copy-done.2
  11.3 0.0 copy-start.4
  11.3 0.2 pack.1
  11.5 1.7 %collective-permute-start.1 = (bf16[64,640]{1,0:T(8,128)(2,1)S(1)}, bf16[64,640]{1,0:T(8,128)(2,1)S(1)}, u32[]{:S(2)}, u32[]{:S(2)}) collective-permute-start(bf16[64,640]{1,0:T(8,128)(2,1)S(1)} %get-tuple-element.9.refs_2_), channel_id=1, source_target_pairs={{0,8},{8,16},{16,24},{24,0},{1,9},{9,17},{17,25},{25,1},{2,10},{10... | collective-permute-start | bytes 245768 | tf_op jit(solution)/shard_map/ppermute | solution.py:179
  13.2 1.3 %collective-permute-start.2 = (bf16[64,640]{1,0:T(8,128)(2,1)S(1)}, bf16[64,640]{1,0:T(8,128)(2,1)S(1)}, u32[]{:S(2)}, u32[]{:S(2)}) collective-permute-start(bf16[64,640]{1,0:T(8,128)(2,1)S(1)} %get-tuple-element.9.refs_2_), channel_id=1, source_target_pairs={{0,24},{8,0},{16,8},{24,16},{1,25},{9,1},{17,9},{25,17},{2,26},{10... | collective-permute-start | bytes 245768 | tf_op jit(solution)/shard_map/ppermute | solution.py:179
  14.5 0.0 copy-done.4
  14.5 0.1 fusion.2.refs_0_
  14.6 0.0 copy-start.1
  14.6 0.0 copy-start.3
  14.6 1.7 %collective-permute-start.7 = (bf16[64,128]{1,0:T(8,128)(2,1)S(1)}, bf16[64,128]{1,0:T(8,128)(2,1)S(1)}, u32[]{:S(2)}, u32[]{:S(2)}) collective-permute-start(bf16[64,128]{1,0:T(8,128)(2,1)S(1)} %get-tuple-element.12.refs_0_), channel_id=1, source_target_pairs={{0,16},{8,24},{16,0},{24,8},{1,17},{9,25},{17,1},{25,9},{2,18},{10... | collective-permute-start | bytes 49160 | tf_op jit(solution)/shard_map/ppermute | solution.py:179
  16.3 1.3 %collective-permute-done.1.refs_1_.refs_3_ = bf16[64,640]{1,0:T(8,128)(2,1)S(1)} collective-permute-done((bf16[64,640]{1,0:T(8,128)(2,1)S(1)}, bf16[64,640]{1,0:T(8,128)(2,1)S(1)}, u32[]{:S(2)}, u32[]{:S(2)}) %collective-permute-start.1) | collective-permute-done | bytes 81952 | tf_op jit(solution)/shard_map/ppermute | solution.py:179
  17.6 1.7 %collective-permute-done.2.refs_3_.refs_1_ = bf16[64,640]{1,0:T(8,128)(2,1)S(1)} collective-permute-done((bf16[64,640]{1,0:T(8,128)(2,1)S(1)}, bf16[64,640]{1,0:T(8,128)(2,1)S(1)}, u32[]{:S(2)}, u32[]{:S(2)}) %collective-permute-start.2) | collective-permute-done | bytes 81952 | tf_op jit(solution)/shard_map/ppermute | solution.py:179
  19.3 0.0 collective-permute-done.3.refs_5_
  19.3 0.0 collective-permute-done.5.refs_7_
  19.3 1.1 %near.1 = (f32[32,256]{1,0:T(8,128)S(1)}, bf16[32,256]{1,0:T(8,128)(2,1)S(1)}) custom-call(s32[4,8]{1,0:T(4,128)S(1)} %fusion.2.refs_0_, bf16[64,640]{1,0:T(8,128)(2,1)S(1)} %collective-permute-done.1.refs_1_.refs_3_, bf16[64,640]{1,0:T(8,128)(2,1)S(1)} %get-tuple-element.9.refs_2_, bf16[64,640]{1,0:T(8,128)(2,1)S(1)} %collective-permute-done.2.refs_3_.refs_1_, ...), custom_call_target="tpu_custom_call" | custom-call | tf_op jit(solution)/shard_map/near/pallas_call | solution.py:217
  20.4 2.3 %collective-permute-start.6 = (bf16[32,256]{1,0:T(8,128)(2,1)S(1)}, bf16[32,256]{1,0:T(8,128)(2,1)S(1)}, u32[]{:S(2)}, u32[]{:S(2)}) collective-permute-start(bf16[32,256]{1,0:T(8,128)(2,1)S(1)} %get-tuple-element.11), channel_id=1, source_target_pairs={{0,4},{1,5},{2,6},{3,7},{4,0},{5,1},{6,2},{7,3},{8,12},{9,13},{10,... | collective-permute-start | bytes 49160 | tf_op jit(solution)/shard_map/ppermute | solution.py:176
  22.7 0.0 copy-start.5
  22.7 0.1 pad_add_fusion.index_ref
  22.7 0.0 collective-permute-done.7.refs_2_
  22.7 0.0 copy-done.1
  22.7 0.0 copy-done.3
  22.8 0.6 %copy-done.5 = s32[4,16]{1,0:T(4,128)S(1)} copy-done((s32[4,16]{1,0:T(4,128)S(1)}, s32[4,16]{1,0:T(4,128)}, u32[]{:S(2)}) %copy-start.5) | copy-done | bytes 280
  23.3 1.1 %far.1.far_ref = f32[32,512]{1,0:T(8,128)S(1)} custom-call(s32[2]{0:T(128)S(1)} %pad_add_fusion.index_ref, s32[4,8]{1,0:T(4,128)S(1)} %copy-done.4, s32[4,16]{1,0:T(4,128)S(1)} %copy-done.5, bf16[4,2,16,256]{3,2,1,0:T(8,128)(2,1)S(1)} %copy-done.1, bf16[4,2,16,128]{3,2,1,0:T(8,128)(2,1)S(1)} %copy-done.3, bf16[64,128]{1,0:T(8,128)(2,1)S(1)} %get-tuple-element.12.refs_0_, ...), custom_call_target="tpu_custom_call" | custom-call | tf_op jit(solution)/shard_map/far/pallas_call | solution.py:231
  24.5 0.6 %collective-permute-done.6.got_ref = bf16[32,256]{1,0:T(8,128)(2,1)S(1)} collective-permute-done((bf16[32,256]{1,0:T(8,128)(2,1)S(1)}, bf16[32,256]{1,0:T(8,128)(2,1)S(1)}, u32[]{:S(2)}, u32[]{:S(2)}) %collective-permute-start.6) | collective-permute-done | bytes 16416 | tf_op jit(solution)/shard_map/ppermute | solution.py:176
  25.1 1.5 %final.1 = bf16[2,16,512]{2,1,0:T(8,128)(2,1)} custom-call(s32[2]{0:T(128)S(1)} %pad_add_fusion.index_ref, bf16[2,16,512]{2,1,0:T(8,128)(2,1)S(1)} %copy-done, f32[32,256]{1,0:T(8,128)S(1)} %get-tuple-element.10.keep_ref, bf16[32,256]{1,0:T(8,128)(2,1)S(1)} %collective-permute-done.6.got_ref, f32[32,512]{1,0:T(8,128)S(1)} %far.1.far_ref), custom_call_target="tpu_custom_call" | custom-call | tf_op jit(solution)/shard_map/final/pallas_call | solution.py:241
  (1 shorter events, 0.0 us)
Async XLA Ops:
  0.0 4.2 %copy-start = (bf16[2,16,512]{2,1,0:T(8,128)(2,1)S(1)}, bf16[2,16,512]{2,1,0:T(8,128)(2,1)}, u32[]{:S(2)}) copy-start(bf16[2,16,512]{2,1,0:T(8,128)(2,1)} %field_ref.1) | copy-start | bytes 98308
  0.0 11.3 %copy-start.2 = (bf16[4,2,16,128]{3,2,1,0:T(8,128)(2,1)S(1)}, bf16[4,2,16,128]{3,2,1,0:T(8,128)(2,1)}, u32[]{:S(2)}) copy-start(bf16[4,2,16,128]{3,2,1,0:T(8,128)(2,1)} %basis_ref.1) | copy-start | bytes 98308
  1.1 10.1 %collective-permute-start.4 = (bf16[4,16,2048]{2,1,0:T(8,128)(2,1)S(1)}, bf16[4,16,2048]{2,1,0:T(8,128)(2,1)S(1)}, u32[]{:S(2)}, u32[]{:S(2)}) collective-permute-start(bf16[4,16,2048]{2,1,0:T(8,128)(2,1)S(1)} %reshape.8.refs_4_), channel_id=1, source_target_pairs={{0,2},{1,3},{2,0},{3,1},{4,6},{5,7},{6,4},{7,5},{8,10},{9,11},{10,... | collective-permute-start | bytes 786440 | tf_op jit(solution)/shard_map/ppermute | solution.py:176
  4.2 15.0 %collective-permute-start.3 = (bf16[4,16,2048]{2,1,0:T(8,128)(2,1)S(1)}, bf16[4,16,2048]{2,1,0:T(8,128)(2,1)S(1)}, u32[]{:S(2)}, u32[]{:S(2)}) collective-permute-start(bf16[4,16,2048]{2,1,0:T(8,128)(2,1)S(1)} %reshape.8.refs_4_), channel_id=1, source_target_pairs={{0,1},{1,0},{2,3},{3,2},{4,5},{5,4},{6,7},{7,6},{8,9},{9,8},{10,11... | collective-permute-start | bytes 786440 | tf_op jit(solution)/shard_map/ppermute | solution.py:176
  4.2 7.0 %collective-permute-start = (bf16[2,16,512]{2,1,0:T(8,128)(2,1)S(1)}, bf16[2,16,512]{2,1,0:T(8,128)(2,1)S(1)}, u32[]{:S(2)}, u32[]{:S(2)}) collective-permute-start(bf16[2,16,512]{2,1,0:T(8,128)(2,1)S(1)} %copy-done), channel_id=1, source_target_pairs={{0,4},{1,5},{2,6},{3,7},{4,0},{5,1},{6,2},{7,3},{8,12},{9,13},{10,... | collective-permute-start | bytes 98312 | tf_op jit(solution)/shard_map/ppermute | solution.py:176
  11.2 8.0 %collective-permute-start.5 = (bf16[4,16,2048]{2,1,0:T(8,128)(2,1)S(1)}, bf16[4,16,2048]{2,1,0:T(8,128)(2,1)S(1)}, u32[]{:S(2)}, u32[]{:S(2)}) collective-permute-start(bf16[4,16,2048]{2,1,0:T(8,128)(2,1)S(1)} %collective-permute-done.4.refs_6_), channel_id=1, source_target_pairs={{0,1},{1,0},{2,3},{3,2},{4,5},{5,4},{6,7},{7,6},{8,9},{9,8},{10,11... | collective-permute-start | bytes 786440 | tf_op jit(solution)/shard_map/ppermute | solution.py:176
  11.3 3.2 %copy-start.4 = (s32[4,8]{1,0:T(4,128)S(1)}, s32[4,8]{1,0:T(4,128)}, u32[]{:S(2)}) copy-start(s32[4,8]{1,0:T(4,128)} %near_ref.1) | copy-start | bytes 388
  11.5 6.1 %collective-permute-start.1 = (bf16[64,640]{1,0:T(8,128)(2,1)S(1)}, bf16[64,640]{1,0:T(8,128)(2,1)S(1)}, u32[]{:S(2)}, u32[]{:S(2)}) collective-permute-start(bf16[64,640]{1,0:T(8,128)(2,1)S(1)} %get-tuple-element.9.refs_2_), channel_id=1, source_target_pairs={{0,8},{8,16},{16,24},{24,0},{1,9},{9,17},{17,25},{25,1},{2,10},{10... | collective-permute-start | bytes 245768 | tf_op jit(solution)/shard_map/ppermute | solution.py:179
  13.2 6.1 %collective-permute-start.2 = (bf16[64,640]{1,0:T(8,128)(2,1)S(1)}, bf16[64,640]{1,0:T(8,128)(2,1)S(1)}, u32[]{:S(2)}, u32[]{:S(2)}) collective-permute-start(bf16[64,640]{1,0:T(8,128)(2,1)S(1)} %get-tuple-element.9.refs_2_), channel_id=1, source_target_pairs={{0,24},{8,0},{16,8},{24,16},{1,25},{9,1},{17,9},{25,17},{2,26},{10... | collective-permute-start | bytes 245768 | tf_op jit(solution)/shard_map/ppermute | solution.py:179
  14.6 8.2 %copy-start.1 = (bf16[4,2,16,256]{3,2,1,0:T(8,128)(2,1)S(1)}, bf16[4,2,16,256]{3,2,1,0:T(8,128)(2,1)}, u32[]{:S(2)}) copy-start(bf16[4,2,16,256]{3,2,1,0:T(8,128)(2,1)} %coupling_ref.1) | copy-start | bytes 196612
  14.6 8.2 %copy-start.3 = (bf16[4,2,16,128]{3,2,1,0:T(8,128)(2,1)S(1)}, bf16[4,2,16,128]{3,2,1,0:T(8,128)(2,1)}, u32[]{:S(2)}) copy-start(bf16[4,2,16,128]{3,2,1,0:T(8,128)(2,1)} %target_ref.1) | copy-start | bytes 98308
  14.6 8.2 %collective-permute-start.7 = (bf16[64,128]{1,0:T(8,128)(2,1)S(1)}, bf16[64,128]{1,0:T(8,128)(2,1)S(1)}, u32[]{:S(2)}, u32[]{:S(2)}) collective-permute-start(bf16[64,128]{1,0:T(8,128)(2,1)S(1)} %get-tuple-element.12.refs_0_), channel_id=1, source_target_pairs={{0,16},{8,24},{16,0},{24,8},{1,17},{9,25},{17,1},{25,9},{2,18},{10... | collective-permute-start | bytes 49160 | tf_op jit(solution)/shard_map/ppermute | solution.py:179
  20.4 4.7 %collective-permute-start.6 = (bf16[32,256]{1,0:T(8,128)(2,1)S(1)}, bf16[32,256]{1,0:T(8,128)(2,1)S(1)}, u32[]{:S(2)}, u32[]{:S(2)}) collective-permute-start(bf16[32,256]{1,0:T(8,128)(2,1)S(1)} %get-tuple-element.11), channel_id=1, source_target_pairs={{0,4},{1,5},{2,6},{3,7},{4,0},{5,1},{6,2},{7,3},{8,12},{9,13},{10,... | collective-permute-start | bytes 49160 | tf_op jit(solution)/shard_map/ppermute | solution.py:176
  22.7 0.7 %copy-start.5 = (s32[4,16]{1,0:T(4,128)S(1)}, s32[4,16]{1,0:T(4,128)}, u32[]{:S(2)}) copy-start(s32[4,16]{1,0:T(4,128)} %rank_ref.1) | copy-start | bytes 772

commit v2 on v1

v2 whole, which is shorter than its diff:
```python
import functools

import jax
import jax.numpy as jnp
from jax import lax
from jax.experimental import pallas as pl
from jax.experimental.pallas import tpu as pltpu
from jax.sharding import PartitionSpec as P

F32 = jnp.float32
BF16 = jnp.bfloat16
VMEM = pl.BlockSpec(memory_space=pltpu.VMEM)
SMEM = pl.BlockSpec(memory_space=pltpu.SMEM)
ANY = pl.BlockSpec(memory_space=pl.ANY)


TURN = 3.0
TURN2 = 3.0


def params():
    return pltpu.CompilerParams(vmem_limit_bytes=8 * 1024 * 1024)


def cost(us):
    return pl.CostEstimate(flops=int(us * 1e9), bytes_accessed=0, transcendentals=0)


def in_hbm(x):
    return pltpu.with_memory_space_constraint(x, pltpu.HBM)


def nt_dot(left, right):
    return lax.dot_general(left, right, (((1,), (1,)), ((), ())), preferred_element_type=F32)


def tn_dot(left, right):
    return lax.dot_general(left, right, (((0,), (0,)), ((), ())), preferred_element_type=F32)


def times_i(pair_rows, width):
    return jnp.concatenate([-pair_rows[width:], pair_rows[:width]], axis=0)


def times_i_lanes(pair_lanes, width):
    return jnp.concatenate([-pair_lanes[:, width:], pair_lanes[:, :width]], axis=1)


def compress_kernel(field_hbm, basis_hbm, packed_ref, field_ref, basis_ref, sems):
    copies = [
        pltpu.make_async_copy(field_hbm, field_ref, sems.at[0]),
        pltpu.make_async_copy(basis_hbm, basis_ref, sems.at[1]),
    ]
    for copy in copies:
        copy.start()
    for copy in copies:
        copy.wait()
    _, inc, _ = field_ref.shape
    blocks, _, rank, block = basis_ref.shape
    pieces = []
    for j in range(blocks):
        basis = jnp.concatenate([basis_ref[j, 0], basis_ref[j, 1]], axis=0)
        field = jnp.concatenate(
            [field_ref[part][:, j * block : (j + 1) * block] for part in range(2)], axis=0
        )
        both = nt_dot(basis, field)
        pieces.append(both[:rank] + times_i_lanes(both[rank:], inc))
    packed_ref[...] = jnp.concatenate(pieces, axis=1).astype(BF16)


def pack_kernel(own_ref, other_ref, packed_ref, payload_ref, again_ref):
    _, inc, panels = own_ref.shape
    block = payload_ref.shape[1]
    for b in range(panels // block):
        for side, ref in enumerate((own_ref, other_ref)):
            for part in range(2):
                at = ((b * 2 + side) * 2 + part) * inc
                payload_ref[at : at + inc, :] = ref[part][:, b * block : (b + 1) * block]
    payload_ref[4 * inc * (panels // block) :, :] = packed_ref[...]
    again_ref[...] = packed_ref[...]


def fill_wide(wide_ref, window_refs, inc, blocks, block):
    for w, refs in enumerate(window_refs):
        for b in range(blocks):
            span = slice(b * 4 * inc, (b + 1) * 4 * inc)
            piece = refs[0][span, :]
            if len(refs) == 2:
                odd = lax.rem(lax.axis_index("panel"), 2) == 1
                piece = jnp.where(odd, refs[1][span, :], piece)
            turned = jnp.concatenate(
                [times_i(piece[: 2 * inc], inc), times_i(piece[2 * inc :], inc)], axis=0
            )
            at = (w * blocks + b) * 2 * block
            wide_ref[:, at : at + block] = piece
            wide_ref[:, at + block : at + 2 * block] = turned


def pick_matrix(near_ref, i, rows, slots, blocks, panel_count):
    total = blocks * panel_count
    shape = ((2 * blocks + 1) * 2 * rows, rows * slots * 2)
    out = lax.broadcasted_iota(jnp.int32, shape, 0)
    col = lax.broadcasted_iota(jnp.int32, (1, shape[1]), 1)
    slot = (col // 2) % slots
    distance = jnp.zeros((1, shape[1]), jnp.int32)
    for k in range(slots):
        distance = jnp.where(slot == k, near_ref[i : i + 1, k : k + 1], distance)
    distance = distance - (lax.axis_index("panel") * blocks + i) + blocks
    distance = jnp.where(distance < 0, distance + total, distance)
    distance = jnp.where(distance >= total, distance - total, distance)
    source = (distance * 2 + col % 2) * rows + col // (2 * slots)
    return jnp.where(out == source, 1.0, 0.0).astype(BF16)


def turn(pick, piece_ref, i):
    lines = pick.shape[1]
    piece = piece_ref[i * lines : (i + 1) * lines, :]
    return jnp.dot(pick, piece, preferred_element_type=F32).astype(BF16)


def turn_first_kernel(sizes, near_ref, *refs):
    rows, slots, block, blocks, panel_count, swaps = sizes
    own_ref, mate_ref = refs[:2]
    pick_ref, own_out, mate_out = refs[-3:]
    for i in range(blocks):
        pick = pick_matrix(near_ref, i, rows, slots, blocks, panel_count)
        pick_ref[i] = pick
        own_out[i] = turn(pick, own_ref, i)
        mate_out[i] = turn(pick, mate_ref, i)


def turn_one_kernel(blocks, pick_ref, piece_ref, *refs):
    for i in range(blocks):
        refs[-1][i] = turn(pick_ref[i], piece_ref, i)


def near_kernel(
    sizes, inc, pick_ref, last_ref, below_ref, own_ref, above_ref, *refs
):
    rows, slots, block, blocks, panel_count, swaps = sizes
    keep_ref, send_ref, wide_ref, last_turned = refs[-4:]
    turned = list(refs[:-4]) + [last_turned]
    for i in range(blocks):
        last_turned[i] = turn(pick_ref[i], last_ref, i)
    low, high = ((below_ref, above_ref), (above_ref, below_ref)) if swaps else ((below_ref,), (above_ref,))
    fill_wide(wide_ref, (low, (own_ref,), high), inc, blocks, block)
    for pair in range(blocks // 2):
        sums = []
        for i in (2 * pair, 2 * pair + 1):
            total = None
            for step in range(2 * blocks + 1):
                coefs = []
                for ref in turned:
                    at = step * 2 * rows
                    coefs.append(
                        jnp.concatenate(
                            [ref[i, at : at + rows, :], ref[i, at + rows : at + 2 * rows, :]],
                            axis=1,
                        )
                    )
                start = (i + step) * 2 * block
                term = nt_dot(
                    wide_ref[:, start : start + 2 * block], jnp.concatenate(coefs, axis=0)
                )
                total = term if total is None else total + term
            sums.append(total)
        both = jnp.concatenate(sums, axis=1)
        span = slice(pair * block, (pair + 1) * block)
        keep_ref[:, span] = both[: 2 * inc]
        send_ref[:, span] = both[2 * inc :].astype(BF16)


def near_rows_kernel(sizes, inc, near_ref, coefs_ref, below_ref, own_ref, above_ref, *refs):
    rows, slots, block, blocks, panel_count, swaps = sizes
    keep_ref, send_ref, wide_ref = refs
    low, high = ((below_ref, above_ref), (above_ref, below_ref)) if swaps else ((below_ref,), (above_ref,))
    fill_wide(wide_ref, (low, (own_ref,), high), inc, blocks, block)
    total_blocks = blocks * panel_count
    me = lax.axis_index("panel")
    half = coefs_ref.shape[1]
    for i in range(blocks):
        total = None
        for k in range(slots):
            at = near_ref[i, k] - (me * blocks + i) + blocks
            at = jnp.where(at < 0, at + total_blocks, at)
            at = jnp.where(at >= total_blocks, at - total_blocks, at)
            start = pl.multiple_of(jnp.minimum(at + i, 3 * blocks - 1) * (2 * block), 2 * block)
            coefs = coefs_ref[i, :, k * 2 * block : (k + 1) * 2 * block]
            term = nt_dot(wide_ref[:, pl.ds(start, 2 * block)], coefs)
            total = term if total is None else total + term
        span = slice(i * half, (i + 1) * half)
        keep_ref[:, span] = total[: 2 * inc]
        send_ref[:, span] = total[2 * inc :].astype(BF16)


def in_order(rows_of, bits, rows):
    lanes = rows_of.shape[1]
    lane = lax.broadcasted_iota(jnp.int32, rows_of.shape, 1)
    me = lax.axis_index("inc")
    bit = 1
    while bit < bits:
        shift = bit * rows
        upper = (lane // shift) % 2 == 1
        swapped = jnp.where(
            upper, pltpu.roll(rows_of, shift, 1), pltpu.roll(rows_of, lanes - shift, 1)
        )
        rows_of = jnp.where((me // bit) % 2 == 1, swapped, rows_of)
        bit *= 2
    return rows_of


def base_kernel(
    order, inc, bits, rows, near_ref, rank_ref, field_ref, keep_ref, coupling_ref, target_ref, *refs
):
    count = len(order)
    piece_refs = refs[:count]
    base_ref, place_ref, gathered_ref = refs[count:]
    blocks, _, rank, columns = coupling_ref.shape
    block = target_ref.shape[3]
    size = blocks * rank
    me = lax.axis_index("panel")
    for ref, (step, swap) in zip(piece_refs, order):
        at = lax.bitwise_xor(me, swap) if swap else lax.rem(me + step, count)
        piece = ref[ref.shape[0] - rank :, :]
        for j in range(blocks):
            row = pl.multiple_of(at * size + j * rank, rank)
            gathered_ref[pl.ds(row, rank), :] = piece[:, j * 2 * inc : (j + 1) * 2 * inc]
    block_id = lax.broadcasted_iota(jnp.int32, (rank, columns), 1) // rank
    within = lax.broadcasted_iota(jnp.int32, (rank, columns), 1) % rank
    row = lax.broadcasted_iota(jnp.int32, (rank, columns), 0)
    largest = jnp.maximum(within, row)
    masked = [[], []]
    for i in range(blocks):
        ranks = jnp.zeros((rank, columns), jnp.int32)
        for j in range(columns // rank):
            ranks = jnp.where(block_id == j, rank_ref[i, j], ranks)
        keep = largest < ranks
        for k in range(near_ref.shape[1]):
            keep = keep & (block_id != near_ref[i, k])
        for part in range(2):
            value = coupling_ref[i, part].astype(F32)
            masked[part].append(jnp.where(keep, value, 0.0).astype(BF16))
    masked = jnp.concatenate(masked[0] + masked[1], axis=0)
    both = jnp.dot(masked, gathered_ref[...], preferred_element_type=F32)
    mixed = (both[:size] + times_i_lanes(both[size:], inc)).astype(BF16).astype(F32)
    mixed = jnp.concatenate([mixed, times_i_lanes(mixed, inc)], axis=0).astype(BF16)
    row_block = lax.broadcasted_iota(jnp.int32, (size, block), 0) // rank
    basis = [
        jnp.concatenate([target_ref[i, part] for i in range(blocks)], axis=0).astype(F32)
        for part in range(2)
    ]
    half = block // 2
    high = lax.axis_index("inc") // (lax.axis_size("inc") // 2) == 1
    empty = jnp.zeros((2 * inc, half), F32)
    sent = lax.broadcasted_iota(jnp.int32, (block, 2 * block), 0)
    lane = lax.broadcasted_iota(jnp.int32, (block, 2 * block), 1)
    me_inc, groups = lax.axis_index("inc"), half // rows
    group = (sent // rows) % groups
    if bits > 1:
        group = lax.bitwise_xor(group, lax.bitwise_xor(me_inc, groups))
    else:
        group = group + lax.bitwise_xor(me_inc // groups, 1) * groups
    target = (sent // half) * block + group * rows + sent % rows
    place_ref[...] = jnp.where(lane == target, 1.0, 0.0).astype(BF16)
    for pair in range(blocks // 2):
        own = keep_ref[:, pair * block : (pair + 1) * block]
        if bits > 1:
            own = in_order(own, bits, rows)
        for i in (2 * pair, 2 * pair + 1):
            spread = jnp.concatenate(
                [jnp.where(row_block == i, basis[part], 0.0) for part in range(2)], axis=0
            ).astype(BF16)
            far = tn_dot(mixed, spread)
            span = slice(i * block, (i + 1) * block)
            kept = own[:, (i - 2 * pair) * half : (i - 2 * pair + 1) * half]
            near = jnp.where(
                high, jnp.concatenate([empty, kept], axis=1), jnp.concatenate([kept, empty], axis=1)
            )
            field = jnp.concatenate([field_ref[0][:, span], field_ref[1][:, span]], axis=0)
            base_ref[:, span] = field.astype(F32) * 0.5 + near + far


def final_kernel(base_ref, got_ref, place_ref, out_ref):
    _, inc, panels = out_ref.shape
    block, width = place_ref.shape
    for pair in range(panels // width):
        near = jnp.dot(
            got_ref[:, pair * block : (pair + 1) * block],
            place_ref[...],
            preferred_element_type=F32,
        )
        span = slice(pair * width, (pair + 1) * width)
        result = (base_ref[:, span] + near).astype(BF16)
        out_ref[0, :, span] = result[:inc]
        out_ref[1, :, span] = result[inc:]


def call(kernel, name, out_shape, ins, out_specs, scratch=(), us=1.0, **more):
    return pl.pallas_call(
        kernel,
        out_shape=out_shape,
        in_specs=ins,
        out_specs=out_specs,
        scratch_shapes=list(scratch),
        compiler_params=params(),
        cost_estimate=cost(us),
        name=name,
        **more,
    )


def local(surface_field, near_block, near_index, source_basis, coupling, target_basis, far_rank):
    blocks, rows, slots, _, block = near_block.shape
    _, inc, panels = surface_field.shape
    rank = source_basis.shape[2]
    panel_count = lax.axis_size("panel")
    inc_count = lax.axis_size("inc")
    half = inc_count // 2
    swaps = panel_count == 4
    lines = rows * slots * 2

    def across(x, bit):
        return lax.ppermute(x, "inc", [(i, i ^ bit) for i in range(inc_count)])

    def onward(x, step, swap=0):
        if swap:
            return lax.ppermute(x, "panel", [(i, i ^ swap) for i in range(panel_count)])
        return lax.ppermute(
            x, "panel", [(i, (i - step) % panel_count) for i in range(panel_count)]
        )

    if swaps:
        order = [(0, 0), (0, 1), (0, 3), (0, 2)]
    else:
        order = [(0, 0), (1, 0), (panel_count - 1, 0)]
        order += [(k, 0) for k in range(2, panel_count - 1)]

    other = across(surface_field, half)
    raw = near_block.reshape(blocks * lines, block)
    paired = half == 4 and rows % 16 == 0
    if paired:
        beyond = across(raw, 2)
        mate = across(raw, 1)

    packed, field = call(
        compress_kernel,
        "compress",
        (
            jax.ShapeDtypeStruct((rank, blocks * 2 * inc), BF16),
            jax.ShapeDtypeStruct(surface_field.shape, BF16),
        ),
        [ANY] * 2,
        (VMEM, VMEM),
        [
            pltpu.VMEM(source_basis.shape, BF16),
            pltpu.SemaphoreType.DMA((2,)),
        ],
        us=0.2,
    )(in_hbm(surface_field), in_hbm(source_basis))
    payload, again = call(
        pack_kernel,
        "pack",
        (
            jax.ShapeDtypeStruct((blocks * 4 * inc + rank, block), BF16),
            jax.ShapeDtypeStruct(packed.shape, BF16),
        ),
        [VMEM] * 3,
        (VMEM, VMEM),
        us=100.0,
    )(field, other, packed)
    first = onward(payload, *order[1])
    second = onward(payload, *order[2])
    rest = [onward(again, *which) for which in order[3:]]

    sizes = (rows, slots, block, blocks, panel_count, swaps)
    width = blocks * half * rows
    near_shape = (
        jax.ShapeDtypeStruct((2 * inc, width), F32),
        jax.ShapeDtypeStruct((2 * inc, width), BF16),
    )
    wide = pltpu.VMEM((4 * inc, 3 * blocks * 2 * block), BF16)
    if paired:
        picked = (2 * blocks + 1) * 2 * rows
        shape = jax.ShapeDtypeStruct((blocks, picked, block), BF16)
        pick, own_turned, mate_turned = call(
            functools.partial(turn_first_kernel, sizes),
            "turn_first",
            (jax.ShapeDtypeStruct((blocks, picked, lines), BF16), shape, shape),
            [VMEM] * 3,
            (VMEM,) * 3,
            us=TURN,
        )(near_index, raw, mate)
        last = across(beyond, 1)
        beyond_turned = call(
            functools.partial(turn_one_kernel, blocks),
            "turn_beyond",
            shape,
            [VMEM] * 2,
            VMEM,
            us=TURN2,
        )(pick, beyond)
        keep, send = call(
            functools.partial(near_kernel, sizes, inc),
            "near",
            near_shape,
            [VMEM] * 8,
            (VMEM, VMEM),
            [wide, pltpu.VMEM(shape.shape, BF16)],
        )(pick, last, second, payload, first, own_turned, mate_turned, beyond_turned)
    else:
        coefs = {0: near_block.reshape(blocks, rows, slots * 2 * block)}
        bit = half // 2
        while bit:
            for at in sorted(coefs):
                coefs[at | bit] = across(coefs[at], bit)
            bit //= 2
        me = lax.axis_index("inc") % half
        stacked = jnp.stack([coefs[at] for at in range(half)], axis=1)
        stacked = jnp.take(stacked, jnp.arange(half) ^ me, axis=1)
        stacked = stacked.reshape(blocks, half * rows, slots * 2 * block)
        keep, send = call(
            functools.partial(near_rows_kernel, sizes, inc),
            "near_rows",
            near_shape,
            [SMEM] + [VMEM] * 4,
            (VMEM, VMEM),
            [wide],
        )(near_index, stacked, second, payload, first)
    bits = half if paired else 1
    got = across(send, half)

    base, place = call(
        functools.partial(base_kernel, order, inc, bits, rows),
        "base",
        (
            jax.ShapeDtypeStruct((2 * inc, panels), F32),
            jax.ShapeDtypeStruct((block, 2 * block), BF16),
        ),
        [SMEM] * 2 + [VMEM] * (4 + panel_count),
        (VMEM, VMEM),
        [pltpu.VMEM((panel_count * blocks * rank, 2 * inc), BF16)],
    )(near_index, far_rank, field, keep, coupling, target_basis, packed, first, second, *rest)

    return call(
        final_kernel,
        "final",
        jax.ShapeDtypeStruct((2, inc, panels), BF16),
        [VMEM] * 3,
        VMEM,
    )(base, got, place)


def solution(mesh):
    return jax.shard_map(
        local,
        mesh=mesh,
        in_specs=(
            P(None, "inc", "panel"),
            P("panel", "inc", None, None, None),
            P("panel", None),
            P("panel", None, None, None),
            P("panel", None, None, None),
            P("panel", None, None, None),
            P("panel", None),
        ),
        out_specs=P(None, "inc", "panel"),
        check_vma=False,
    )
```

time: 26.7 us -> 20.4 us (0.76)
  waiting for transfers between devices: 7.94 us -> 4.02 us
  local copies, waits for them, and re-layouts: 1.76 us -> 0.03 us
  starting transfers between devices: 12.7 us -> 11.4 us
  Pallas kernels: 3.95 us -> 4.71 us
    ppermute x3, waiting for transfers between devices: 2.95 us -> 0.85 us  [onward(): return lax.ppermute(x, 'panel', [(i, i ^ swap) for i in range(panel_count)])]
    ppermute x5, waiting for transfers between devices: 4.99 us -> 3.17 us  [across(): return lax.ppermute(x, 'inc', [(i, i ^ bit) for i in range(inc_count)])]
    ppermute x3, starting transfers between devices: 4.73 us -> 3.55 us  [onward(): return lax.ppermute(x, 'panel', [(i, i ^ swap) for i in range(panel_count)])]
    reshape x1 -> x0, local copies, waits for them, and re-layouts: 1.14 us -> none  [local(): coefs = {0: near_block.reshape(blocks, rows, slots * 2 * block)}]
    pallas_call x4 -> x7, Pallas kernels: 3.95 us -> 4.71 us  [the longest x1 1.22 us: local(): call(functools.partial(base_kernel, order, inc, bits, rows), 'base', (jax...]
    unnamed x12 -> x10, local copies, waits for them, and re-layouts: 0.62 us -> 0.03 us
  transfers between devices with their start and end apart: 8 -> 8, of which waited for: 4 -> 3; matrix products, arithmetic and copies ran while one was open for 1% -> 0% of each run, Pallas kernels for 9% -> 20%
where the time goes in v2:
time: 20.4 us; the launch traced here: 20.3 us
  starting transfers between devices  11.4 us (56%)
  Pallas kernels  4.71 us (23%)
  waiting for transfers between devices  4.02 us (20%)
    ppermute x5, starting transfers between devices, across(): return lax.ppermute(x, 'inc', [(i, i ^ bit) for i in range(inc_count)])  7.84 us
    ppermute x3, starting transfers between devices, onward(): return lax.ppermute(x, 'panel', [(i, i ^ swap) for i in range(panel_count)])  3.55 us
    ppermute x5, waiting for transfers between devices, across(): return lax.ppermute(x, 'inc', [(i, i ^ bit) for i in range(inc_count)])  3.17 us
    pallas_call x1, Pallas kernels, local(): call(functools.partial(base_kernel, order, inc, bits, rows), 'base', (jax...  1.22 us
    pallas_call x1, Pallas kernels, local(): call(compress_kernel, 'compress', (jax.ShapeDtypeStruct((rank, blocks * 2...  1.07 us
    ppermute x3, waiting for transfers between devices, onward(): return lax.ppermute(x, 'panel', [(i, i ^ swap) for i in range(panel_count)])  0.85 us
    pallas_call x1, Pallas kernels, local(): call(final_kernel, 'final', jax.ShapeDtypeStruct((2, inc, panels), BF16),...  0.75 us
    pallas_call x1, Pallas kernels, local(): call(functools.partial(near_kernel, sizes, inc), 'near', near_shape, [VME...  0.7 us
  transfers between devices with their start and end apart: 8, of which 3 were waited for; matrix products, arithmetic and copies ran while one was open for 0% of the time, Pallas kernels for 20%

profile of v2, /device:TPU:0, one launch (start us, length us, event | category | flops | bytes accessed | tf_op | source)
XLA Modules:
  0.0 20.3 jit_solution(11628668956418688581)
XLA Ops:
  0.0 4.0 %collective-permute-start.3 = (bf16[2,16,512]{2,1,0:T(8,128)(2,1)}, bf16[2,16,512]{2,1,0:T(8,128)(2,1)S(1)}, u32[]{:S(2)}, u32[]{:S(2)}) collective-permute-start(bf16[2,16,512]{2,1,0:T(8,128)(2,1)} %field_hbm.1), channel_id=1, source_target_pairs={{0,4},{1,5},{2,6},{3,7},{4,0},{5,1},{6,2},{7,3},{8,12},{9,13},{10,... | collective-permute-start | bytes 98312 | tf_op jit(solution)/shard_map/ppermute | solution.py:323
  4.0 1.6 %collective-permute-start.1 = (bf16[1024,128]{1,0:T(8,128)(2,1)}, bf16[1024,128]{1,0:T(8,128)(2,1)S(1)}, u32[]{:S(2)}, u32[]{:S(2)}) collective-permute-start(bf16[1024,128]{1,0:T(8,128)(2,1)} %bitcast.1), channel_id=1, source_target_pairs={{0,2},{1,3},{2,0},{3,1},{4,6},{5,7},{6,4},{7,5},{8,10},{9,11},{10,... | collective-permute-start | bytes 786440 | tf_op jit(solution)/shard_map/ppermute | solution.py:323
  5.6 0.0 collective-permute-start
  5.6 1.1 %compress.1 = (bf16[16,128]{1,0:T(8,128)(2,1)S(1)}, bf16[2,16,512]{2,1,0:T(8,128)(2,1)S(1)}) custom-call(bf16[2,16,512]{2,1,0:T(8,128)(2,1)} %field_hbm.1, bf16[4,2,16,128]{3,2,1,0:T(8,128)(2,1)} %basis_hbm.1), custom_call_target="tpu_custom_call" | custom-call | flops 200000000 | tf_op jit(solution)/shard_map/compress/pallas_call | solution.py:345
  6.7 0.0 collective-permute-done.3.other_ref
  6.7 0.0 copy-start
  6.7 0.0 copy-start.3
  6.7 1.6 %collective-permute-start.5 = (bf16[272,128]{1,0:T(8,128)(2,1)S(1)}, bf16[272,128]{1,0:T(8,128)(2,1)S(1)}, u32[]{:S(2)}, u32[]{:S(2)}) collective-permute-start(bf16[272,128]{1,0:T(8,128)(2,1)S(1)} %get-tuple-element.19.own_ref), channel_id=1, source_target_pairs={{0,8},{8,0},{16,24},{24,16},{1,9},{9,1},{17,25},{25,17},{2,10},{10... | collective-permute-start | bytes 208904 | tf_op jit(solution)/shard_map/ppermute | solution.py:327
  8.3 1.5 %collective-permute-start.4 = (bf16[272,128]{1,0:T(8,128)(2,1)S(1)}, bf16[272,128]{1,0:T(8,128)(2,1)S(1)}, u32[]{:S(2)}, u32[]{:S(2)}) collective-permute-start(bf16[272,128]{1,0:T(8,128)(2,1)S(1)} %get-tuple-element.19.own_ref), channel_id=1, source_target_pairs={{0,24},{8,16},{16,8},{24,0},{1,25},{9,17},{17,9},{25,1},{2,26},{10... | collective-permute-start | bytes 208904 | tf_op jit(solution)/shard_map/ppermute | solution.py:327
  9.8 0.5 %collective-permute-start.6 = (bf16[16,128]{1,0:T(8,128)(2,1)S(1)}, bf16[16,128]{1,0:T(8,128)(2,1)S(1)}, u32[]{:S(2)}, u32[]{:S(2)}) collective-permute-start(bf16[16,128]{1,0:T(8,128)(2,1)S(1)} %get-tuple-element.23), channel_id=1, source_target_pairs={{0,16},{8,24},{16,0},{24,8},{1,17},{9,25},{17,1},{25,9},{2,18},{10... | collective-permute-start | bytes 12296 | tf_op jit(solution)/shard_map/ppermute | solution.py:327
  10.3 1.7 %collective-permute-done.1.piece_ref = bf16[1024,128]{1,0:T(8,128)(2,1)S(1)} collective-permute-done((bf16[1024,128]{1,0:T(8,128)(2,1)}, bf16[1024,128]{1,0:T(8,128)(2,1)S(1)}, u32[]{:S(2)}, u32[]{:S(2)}) %collective-permute-start.1) | collective-permute-done | bytes 262176 | tf_op jit(solution)/shard_map/ppermute | solution.py:323
  12.1 0.0 collective-permute-start.2
  12.1 0.0 collective-permute-done.refs_1_
  12.1 0.0 copy-done
  12.1 0.0 copy-done.3
  12.1 0.6 %turn_first.1 = (bf16[4,288,256]{2,1,0:T(8,128)(2,1)S(1)}, bf16[4,288,128]{2,1,0:T(8,128)(2,1)S(1)}, bf16[4,288,128]{2,1,0:T(8,128)(2,1)S(1)}) custom-call(s32[4,8]{1,0:T(4,128)S(1)} %copy-done.3, bf16[1024,128]{1,0:T(8,128)(2,1)S(1)} %bitcast.3, bf16[1024,128]{1,0:T(8,128)(2,1)S(1)} %collective-permute-done.refs_1_), custom_call_target="tpu_custom_call" | custom-call | flops 3000000000 | tf_op jit(solution)/shard_map/turn_first/pallas_call | solution.py:385
  12.7 0.3 %turn_beyond.1.refs_2_ = bf16[4,288,128]{2,1,0:T(8,128)(2,1)S(1)} custom-call(bf16[4,288,256]{2,1,0:T(8,128)(2,1)S(1)} %get-tuple-element.17.pick_ref, bf16[1024,128]{1,0:T(8,128)(2,1)S(1)} %collective-permute-done.1.piece_ref), custom_call_target="tpu_custom_call" | custom-call | flops 3000000000 | tf_op jit(solution)/shard_map/turn_beyond/pallas_call | solution.py:394
  13.0 0.0 collective-permute-done.5.above_ref.refs_1_
  13.1 0.8 %collective-permute-done.4.below_ref.refs_2_ = bf16[272,128]{1,0:T(8,128)(2,1)S(1)} collective-permute-done((bf16[272,128]{1,0:T(8,128)(2,1)S(1)}, bf16[272,128]{1,0:T(8,128)(2,1)S(1)}, u32[]{:S(2)}, u32[]{:S(2)}) %collective-permute-start.4) | collective-permute-done | bytes 69664 | tf_op jit(solution)/shard_map/ppermute | solution.py:327
  13.9 0.0 collective-permute-done.2.last_ref
  13.9 0.0 copy-start.1
  13.9 0.0 copy-start.2
  13.9 0.7 %near.1 = (f32[32,256]{1,0:T(8,128)S(1)}, bf16[32,256]{1,0:T(8,128)(2,1)S(1)}) custom-call(bf16[4,288,256]{2,1,0:T(8,128)(2,1)S(1)} %get-tuple-element.17.pick_ref, bf16[1024,128]{1,0:T(8,128)(2,1)S(1)} %collective-permute-done.2.last_ref, bf16[272,128]{1,0:T(8,128)(2,1)S(1)} %collective-permute-done.4.below_ref.refs_2_, ...), custom_call_target="tpu_custom_call" | custom-call | flops 1000000000 | tf_op jit(solution)/shard_map/near/pallas_call | solution.py:402
  14.6 0.0 copy-start.4
  14.6 2.2 %collective-permute-start.7 = (bf16[32,256]{1,0:T(8,128)(2,1)S(1)}, bf16[32,256]{1,0:T(8,128)(2,1)S(1)}, u32[]{:S(2)}, u32[]{:S(2)}) collective-permute-start(bf16[32,256]{1,0:T(8,128)(2,1)S(1)} %get-tuple-element.25), channel_id=1, source_target_pairs={{0,4},{1,5},{2,6},{3,7},{4,0},{5,1},{6,2},{7,3},{8,12},{9,13},{10,... | collective-permute-start | bytes 49160 | tf_op jit(solution)/shard_map/ppermute | solution.py:323
  16.9 0.0 collective-permute-done.6.refs_3_
  16.9 0.0 copy-done.1
  16.9 0.0 copy-done.2
  16.9 0.0 copy-done.4
  16.9 1.2 %base.1 = (f32[32,512]{1,0:T(8,128)S(1)}, bf16[128,256]{1,0:T(8,128)(2,1)S(1)}) custom-call(s32[4,8]{1,0:T(4,128)S(1)} %copy-done.3, s32[4,16]{1,0:T(4,128)S(1)} %copy-done.4, bf16[2,16,512]{2,1,0:T(8,128)(2,1)S(1)} %get-tuple-element.16.own_ref.field_ref, f32[32,256]{1,0:T(8,128)S(1)} %get-tuple-element.22.keep_ref, bf16[4,2,16,256]{3,2,1,0:T(8,128)(2,1)S(1)} %copy-done.1, ...), custom_call_target="tpu_custom_call" | custom-call | flops 1000000000 | tf_op jit(solution)/shard_map/base/pallas_call | solution.py:432
  18.1 1.4 %collective-permute-done.7.got_ref = bf16[32,256]{1,0:T(8,128)(2,1)S(1)} collective-permute-done((bf16[32,256]{1,0:T(8,128)(2,1)S(1)}, bf16[32,256]{1,0:T(8,128)(2,1)S(1)}, u32[]{:S(2)}, u32[]{:S(2)}) %collective-permute-start.7) | collective-permute-done | bytes 16416 | tf_op jit(solution)/shard_map/ppermute | solution.py:323
  19.5 0.8 %final.1 = bf16[2,16,512]{2,1,0:T(8,128)(2,1)} custom-call(f32[32,512]{1,0:T(8,128)S(1)} %get-tuple-element.24.base_ref, bf16[32,256]{1,0:T(8,128)(2,1)S(1)} %collective-permute-done.7.got_ref, bf16[128,256]{1,0:T(8,128)(2,1)S(1)} %get-tuple-element.26.place_ref), custom_call_target="tpu_custom_call" | custom-call | flops 1000000000 | tf_op jit(solution)/shard_map/final/pallas_call | solution.py:444
  (1 shorter events, 0.0 us)
Async XLA Ops:
  0.0 6.7 %collective-permute-start.3 = (bf16[2,16,512]{2,1,0:T(8,128)(2,1)}, bf16[2,16,512]{2,1,0:T(8,128)(2,1)S(1)}, u32[]{:S(2)}, u32[]{:S(2)}) collective-permute-start(bf16[2,16,512]{2,1,0:T(8,128)(2,1)} %field_hbm.1), channel_id=1, source_target_pairs={{0,4},{1,5},{2,6},{3,7},{4,0},{5,1},{6,2},{7,3},{8,12},{9,13},{10,... | collective-permute-start | bytes 98312 | tf_op jit(solution)/shard_map/ppermute | solution.py:323
  4.0 8.0 %collective-permute-start.1 = (bf16[1024,128]{1,0:T(8,128)(2,1)}, bf16[1024,128]{1,0:T(8,128)(2,1)S(1)}, u32[]{:S(2)}, u32[]{:S(2)}) collective-permute-start(bf16[1024,128]{1,0:T(8,128)(2,1)} %bitcast.1), channel_id=1, source_target_pairs={{0,2},{1,3},{2,0},{3,1},{4,6},{5,7},{6,4},{7,5},{8,10},{9,11},{10,... | collective-permute-start | bytes 786440 | tf_op jit(solution)/shard_map/ppermute | solution.py:323
  5.6 6.4 %collective-permute-start = (bf16[1024,128]{1,0:T(8,128)(2,1)}, bf16[1024,128]{1,0:T(8,128)(2,1)S(1)}, u32[]{:S(2)}, u32[]{:S(2)}) collective-permute-start(bf16[1024,128]{1,0:T(8,128)(2,1)} %bitcast.2), channel_id=1, source_target_pairs={{0,1},{1,0},{2,3},{3,2},{4,5},{5,4},{6,7},{7,6},{8,9},{9,8},{10,11... | collective-permute-start | bytes 786440 | tf_op jit(solution)/shard_map/ppermute | solution.py:323
  6.7 5.4 %copy-start = (bf16[4,16,8,2,128]{4,3,2,1,0:T(2,128)(2,1)S(1)}, bf16[4,16,8,2,128]{4,3,2,1,0:T(2,128)(2,1)}, u32[]{:S(2)}) copy-start(bf16[4,16,8,2,128]{4,3,2,1,0:T(2,128)(2,1)} %param.8) | copy-start | bytes 786436
  6.7 5.3 %copy-start.3 = (s32[4,8]{1,0:T(4,128)S(1)}, s32[4,8]{1,0:T(4,128)}, u32[]{:S(2)}) copy-start(s32[4,8]{1,0:T(4,128)} %near_ref.3) | copy-start | bytes 388
  6.7 6.3 %collective-permute-start.5 = (bf16[272,128]{1,0:T(8,128)(2,1)S(1)}, bf16[272,128]{1,0:T(8,128)(2,1)S(1)}, u32[]{:S(2)}, u32[]{:S(2)}) collective-permute-start(bf16[272,128]{1,0:T(8,128)(2,1)S(1)} %get-tuple-element.19.own_ref), channel_id=1, source_target_pairs={{0,8},{8,0},{16,24},{24,16},{1,9},{9,1},{17,25},{25,17},{2,10},{10... | collective-permute-start | bytes 208904 | tf_op jit(solution)/shard_map/ppermute | solution.py:327
  8.3 5.6 %collective-permute-start.4 = (bf16[272,128]{1,0:T(8,128)(2,1)S(1)}, bf16[272,128]{1,0:T(8,128)(2,1)S(1)}, u32[]{:S(2)}, u32[]{:S(2)}) collective-permute-start(bf16[272,128]{1,0:T(8,128)(2,1)S(1)} %get-tuple-element.19.own_ref), channel_id=1, source_target_pairs={{0,24},{8,16},{16,8},{24,0},{1,25},{9,17},{17,9},{25,1},{2,26},{10... | collective-permute-start | bytes 208904 | tf_op jit(solution)/shard_map/ppermute | solution.py:327
  9.8 7.0 %collective-permute-start.6 = (bf16[16,128]{1,0:T(8,128)(2,1)S(1)}, bf16[16,128]{1,0:T(8,128)(2,1)S(1)}, u32[]{:S(2)}, u32[]{:S(2)}) collective-permute-start(bf16[16,128]{1,0:T(8,128)(2,1)S(1)} %get-tuple-element.23), channel_id=1, source_target_pairs={{0,16},{8,24},{16,0},{24,8},{1,17},{9,25},{17,1},{25,9},{2,18},{10... | collective-permute-start | bytes 12296 | tf_op jit(solution)/shard_map/ppermute | solution.py:327
  12.1 1.8 %collective-permute-start.2 = (bf16[1024,128]{1,0:T(8,128)(2,1)S(1)}, bf16[1024,128]{1,0:T(8,128)(2,1)S(1)}, u32[]{:S(2)}, u32[]{:S(2)}) collective-permute-start(bf16[1024,128]{1,0:T(8,128)(2,1)S(1)} %collective-permute-done.1.piece_ref), channel_id=1, source_target_pairs={{0,1},{1,0},{2,3},{3,2},{4,5},{5,4},{6,7},{7,6},{8,9},{9,8},{10,11... | collective-permute-start | bytes 786440 | tf_op jit(solution)/shard_map/ppermute | solution.py:323
  13.9 3.0 %copy-start.1 = (bf16[4,2,16,256]{3,2,1,0:T(8,128)(2,1)S(1)}, bf16[4,2,16,256]{3,2,1,0:T(8,128)(2,1)}, u32[]{:S(2)}) copy-start(bf16[4,2,16,256]{3,2,1,0:T(8,128)(2,1)} %coupling_ref.1) | copy-start | bytes 196612
  13.9 3.0 %copy-start.2 = (bf16[4,2,16,128]{3,2,1,0:T(8,128)(2,1)S(1)}, bf16[4,2,16,128]{3,2,1,0:T(8,128)(2,1)}, u32[]{:S(2)}) copy-start(bf16[4,2,16,128]{3,2,1,0:T(8,128)(2,1)} %target_ref.1) | copy-start | bytes 98308
  14.6 2.2 %copy-start.4 = (s32[4,16]{1,0:T(4,128)S(1)}, s32[4,16]{1,0:T(4,128)}, u32[]{:S(2)}) copy-start(s32[4,16]{1,0:T(4,128)} %rank_ref.1) | copy-start | bytes 772
  14.6 4.9 %collective-permute-start.7 = (bf16[32,256]{1,0:T(8,128)(2,1)S(1)}, bf16[32,256]{1,0:T(8,128)(2,1)S(1)}, u32[]{:S(2)}, u32[]{:S(2)}) collective-permute-start(bf16[32,256]{1,0:T(8,128)(2,1)S(1)} %get-tuple-element.25), channel_id=1, source_target_pairs={{0,4},{1,5},{2,6},{3,7},{4,0},{5,1},{6,2},{7,3},{8,12},{9,13},{10,... | collective-permute-start | bytes 49160 | tf_op jit(solution)/shard_map/ppermute | solution.py:323

commit v3 on v2

--- a/solution.py
+++ b/solution.py
@@ -80,20 +80,19 @@
     again_ref[...] = packed_ref[...]
 
 
-def fill_wide(wide_ref, window_refs, inc, blocks, block):
+def fill_wide(wide_ref, window_refs, inc, blocks, block, sides):
     for w, refs in enumerate(window_refs):
         for b in range(blocks):
-            span = slice(b * 4 * inc, (b + 1) * 4 * inc)
-            piece = refs[0][span, :]
-            if len(refs) == 2:
-                odd = lax.rem(lax.axis_index("panel"), 2) == 1
-                piece = jnp.where(odd, refs[1][span, :], piece)
-            turned = jnp.concatenate(
-                [times_i(piece[: 2 * inc], inc), times_i(piece[2 * inc :], inc)], axis=0
-            )
             at = (w * blocks + b) * 2 * block
-            wide_ref[:, at : at + block] = piece
-            wide_ref[:, at + block : at + 2 * block] = turned
+            for n, side in enumerate(sides):
+                start = (b * 2 + side) * 2 * inc
+                piece = refs[0][start : start + 2 * inc, :]
+                if len(refs) == 2:
+                    odd = lax.rem(lax.axis_index("panel") + lax.axis_index("inc"), 2) == 1
+                    piece = jnp.where(odd, refs[1][start : start + 2 * inc, :], piece)
+                rows = slice(n * 2 * inc, (n + 1) * 2 * inc)
+                wide_ref[rows, at : at + block] = piece
+                wide_ref[rows, at + block : at + 2 * block] = times_i(piece, inc)
 
 
 def pick_matrix(near_ref, i, rows, slots, blocks, panel_count):
@@ -138,12 +137,23 @@
     sizes, inc, pick_ref, last_ref, below_ref, own_ref, above_ref, *refs
 ):
     rows, slots, block, blocks, panel_count, swaps = sizes
-    keep_ref, send_ref, wide_ref, last_turned = refs[-4:]
-    turned = list(refs[:-4]) + [last_turned]
+    send_ref, last_turned, wide_ref = refs[-3:]
+    turned = list(refs[:-3]) + [last_turned]
     for i in range(blocks):
         last_turned[i] = turn(pick_ref[i], last_ref, i)
+    near_sums(sizes, inc, 1, turned, (below_ref, own_ref, above_ref), wide_ref, send_ref)
+
+
+def near_keep_kernel(sizes, inc, below_ref, own_ref, above_ref, *refs):
+    keep_ref, wide_ref = refs[-2:]
+    near_sums(sizes, inc, 0, refs[:-2], (below_ref, own_ref, above_ref), wide_ref, keep_ref)
+
+
+def near_sums(sizes, inc, side, turned, windows, wide_ref, out_ref):
+    rows, slots, block, blocks, panel_count, swaps = sizes
+    below_ref, own_ref, above_ref = windows
     low, high = ((below_ref, above_ref), (above_ref, below_ref)) if swaps else ((below_ref,), (above_ref,))
-    fill_wide(wide_ref, (low, (own_ref,), high), inc, blocks, block)
+    fill_wide(wide_ref, (low, (own_ref,), high), inc, blocks, block, (side,))
     for pair in range(blocks // 2):
         sums = []
         for i in (2 * pair, 2 * pair + 1):
@@ -164,17 +174,15 @@
                 )
                 total = term if total is None else total + term
             sums.append(total)
-        both = jnp.concatenate(sums, axis=1)
         span = slice(pair * block, (pair + 1) * block)
-        keep_ref[:, span] = both[: 2 * inc]
-        send_ref[:, span] = both[2 * inc :].astype(BF16)
+        out_ref[:, span] = jnp.concatenate(sums, axis=1).astype(out_ref.dtype)
 
 
 def near_rows_kernel(sizes, inc, near_ref, coefs_ref, below_ref, own_ref, above_ref, *refs):
     rows, slots, block, blocks, panel_count, swaps = sizes
     keep_ref, send_ref, wide_ref = refs
     low, high = ((below_ref, above_ref), (above_ref, below_ref)) if swaps else ((below_ref,), (above_ref,))
-    fill_wide(wide_ref, (low, (own_ref,), high), inc, blocks, block)
+    fill_wide(wide_ref, (low, (own_ref,), high), inc, blocks, block, (0, 1))
     total_blocks = blocks * panel_count
     me = lax.axis_index("panel")
     half = coefs_ref.shape[1]
@@ -219,8 +227,10 @@
     block = target_ref.shape[3]
     size = blocks * rank
     me = lax.axis_index("panel")
-    for ref, (step, swap) in zip(piece_refs, order):
-        at = lax.bitwise_xor(me, swap) if swap else lax.rem(me + step, count)
+    core = lax.rem(lax.axis_index("inc"), 2)
+    for ref, (step, even, odd) in zip(piece_refs, order):
+        swap = jnp.where(core == 1, odd, even)
+        at = lax.bitwise_xor(me, swap) if even else lax.rem(me + step, count)
         piece = ref[ref.shape[0] - rank :, :]
         for j in range(blocks):
             row = pl.multiple_of(at * size + j * rank, rank)
@@ -257,7 +267,7 @@
     me_inc, groups = lax.axis_index("inc"), half // rows
     group = (sent // rows) % groups
     if bits > 1:
-        group = lax.bitwise_xor(group, lax.bitwise_xor(me_inc, groups))
+        group = lax.bitwise_xor(group, lax.bitwise_xor(me_inc, groups | 1))
     else:
         group = group + lax.bitwise_xor(me_inc // groups, 1) * groups
     target = (sent // half) * block + group * rows + sent % rows
@@ -322,20 +332,26 @@
     def across(x, bit):
         return lax.ppermute(x, "inc", [(i, i ^ bit) for i in range(inc_count)])
 
-    def onward(x, step, swap=0):
-        if swap:
-            return lax.ppermute(x, "panel", [(i, i ^ swap) for i in range(panel_count)])
+    def onward(x, step, even=0, odd=0):
+        if even:
+            pairs = [
+                (p * inc_count + i, (p ^ (odd if i % 2 else even)) * inc_count + i)
+                for p in range(panel_count)
+                for i in range(inc_count)
+            ]
+            return lax.ppermute(x, ("panel", "inc"), pairs)
         return lax.ppermute(
             x, "panel", [(i, (i - step) % panel_count) for i in range(panel_count)]
         )
 
     if swaps:
-        order = [(0, 0), (0, 1), (0, 3), (0, 2)]
+        order = [(0, 0, 0), (0, 1, 3), (0, 3, 1), (0, 2, 2)]
     else:
-        order = [(0, 0), (1, 0), (panel_count - 1, 0)]
-        order += [(k, 0) for k in range(2, panel_count - 1)]
-
-    other = across(surface_field, half)
+        order = [(0, 0, 0), (1, 0, 0), (panel_count - 1, 0, 0)]
+        order += [(k, 0, 0) for k in range(2, panel_count - 1)]
+
+    partner = half | 1
+    other = across(surface_field, partner)
     raw = near_block.reshape(blocks * lines, block)
     paired = half == 4 and rows % 16 == 0
     if paired:
@@ -399,14 +415,25 @@
             VMEM,
             us=TURN2,
         )(pick, beyond)
-        keep, send = call(
+        wide = pltpu.VMEM((2 * inc, 3 * blocks * 2 * block), BF16)
+        windows = (second, payload, first)
+        turned = (own_turned, mate_turned, beyond_turned)
+        send, last_turned = call(
             functools.partial(near_kernel, sizes, inc),
-            "near",
-            near_shape,
+            "near_send",
+            (near_shape[1], shape),
             [VMEM] * 8,
             (VMEM, VMEM),
-            [wide, pltpu.VMEM(shape.shape, BF16)],
-        )(pick, last, second, payload, first, own_turned, mate_turned, beyond_turned)
+            [wide],
+        )(pick, last, *windows, *turned)
+        keep = call(
+            functools.partial(near_keep_kernel, sizes, inc),
+            "near_keep",
+            near_shape[0],
+            [VMEM] * 7,
+            VMEM,
+            [wide],
+        )(*windows, *turned, last_turned)
     else:
         coefs = {0: near_block.reshape(blocks, rows, slots * 2 * block)}
         bit = half // 2
@@ -427,7 +454,7 @@
             [wide],
         )(near_index, stacked, second, payload, first)
     bits = half if paired else 1
-    got = across(send, half)
+    got = across(send, partner)
 
     base, place = call(
         functools.partial(base_kernel, order, inc, bits, rows),

time: 20.4 us -> 19.9 us (0.975)
  starting transfers between devices: 11.4 us -> 9.68 us
  Pallas kernels: 4.71 us -> 5.1 us
  waiting for transfers between devices: 4.02 us -> 4.37 us
  local copies, waits for them, and re-layouts: 0.03 us -> 0.37 us
    ppermute x5, starting transfers between devices: 7.84 us -> 6.12 us  [across(): return lax.ppermute(x, 'inc', [(i, i ^ bit) for i in range(inc_count)])]
    ppermute x5, waiting for transfers between devices: 3.17 us -> 4.36 us  [across(): return lax.ppermute(x, 'inc', [(i, i ^ bit) for i in range(inc_count)])]
    ppermute x3, waiting for transfers between devices: 0.85 us -> 0.01 us  [onward(): return lax.ppermute(x, ('panel', 'inc'), pairs)]
    pallas_call x1 -> x2, Pallas kernels: 0.7 us -> 1.1 us  [the longest x1 0.64 us: local(): call(functools.partial(near_kernel, sizes, inc), 'near_send', (near_shape...]
    unnamed x10, local copies, waits for them, and re-layouts: 0.03 us -> 0.37 us
  transfers between devices with their start and end apart: 8 -> 8, of which waited for: 3 -> 3; matrix products, arithmetic and copies ran while one was open for 0% -> 0% of each run, Pallas kernels for 20% -> 22%
where the time goes in v3:
time: 19.9 us; the launch traced here: 19.6 us
  starting transfers between devices  9.68 us (49%)
  Pallas kernels  5.1 us (26%)
  waiting for transfers between devices  4.37 us (22%)
  local copies, waits for them, and re-layouts  0.37 us (2%)
    ppermute x5, starting transfers between devices, across(): return lax.ppermute(x, 'inc', [(i, i ^ bit) for i in range(inc_count)])  6.12 us
    ppermute x5, waiting for transfers between devices, across(): return lax.ppermute(x, 'inc', [(i, i ^ bit) for i in range(inc_count)])  4.36 us
    ppermute x3, starting transfers between devices, onward(): return lax.ppermute(x, ('panel', 'inc'), pairs)  3.55 us
    pallas_call x1, Pallas kernels, local(): call(functools.partial(base_kernel, order, inc, bits, rows), 'base', (jax...  1.22 us
    pallas_call x1, Pallas kernels, local(): call(compress_kernel, 'compress', (jax.ShapeDtypeStruct((rank, blocks * 2...  1.07 us
    pallas_call x1, Pallas kernels, local(): call(final_kernel, 'final', jax.ShapeDtypeStruct((2, inc, panels), BF16),...  0.75 us
    pallas_call x1, Pallas kernels, local(): call(functools.partial(near_kernel, sizes, inc), 'near_send', (near_shape...  0.64 us
    pallas_call x1, Pallas kernels, local(): call(functools.partial(turn_first_kernel, sizes), 'turn_first', (jax.Shap...  0.63 us
  transfers between devices with their start and end apart: 8, of which 3 were waited for; matrix products, arithmetic and copies ran while one was open for 0% of the time, Pallas kernels for 22%

profile of v3, /device:TPU:0, one launch (start us, length us, event | category | flops | bytes accessed | tf_op | source)
XLA Modules:
  0.0 19.6 jit_solution(6906082466516239323)
XLA Ops:
  0.0 3.5 %collective-permute-start = (bf16[2,16,512]{2,1,0:T(8,128)(2,1)}, bf16[2,16,512]{2,1,0:T(8,128)(2,1)S(1)}, u32[]{:S(2)}, u32[]{:S(2)}) collective-permute-start(bf16[2,16,512]{2,1,0:T(8,128)(2,1)} %field_hbm.1), channel_id=1, source_target_pairs={{0,5},{1,4},{2,7},{3,6},{4,1},{5,0},{6,3},{7,2},{8,13},{9,12},{10,... | collective-permute-start | bytes 98312 | tf_op jit(solution)/shard_map/ppermute | solution.py:333
  3.5 1.6 %collective-permute-start.4 = (bf16[1024,128]{1,0:T(8,128)(2,1)}, bf16[1024,128]{1,0:T(8,128)(2,1)S(1)}, u32[]{:S(2)}, u32[]{:S(2)}) collective-permute-start(bf16[1024,128]{1,0:T(8,128)(2,1)} %bitcast.1), channel_id=1, source_target_pairs={{0,2},{1,3},{2,0},{3,1},{4,6},{5,7},{6,4},{7,5},{8,10},{9,11},{10,... | collective-permute-start | bytes 786440 | tf_op jit(solution)/shard_map/ppermute | solution.py:333
  5.1 0.4 %collective-permute-start.3 = (bf16[1024,128]{1,0:T(8,128)(2,1)}, bf16[1024,128]{1,0:T(8,128)(2,1)S(1)}, u32[]{:S(2)}, u32[]{:S(2)}) collective-permute-start(bf16[1024,128]{1,0:T(8,128)(2,1)} %bitcast.2), channel_id=1, source_target_pairs={{0,1},{1,0},{2,3},{3,2},{4,5},{5,4},{6,7},{7,6},{8,9},{9,8},{10,11... | collective-permute-start | bytes 786440 | tf_op jit(solution)/shard_map/ppermute | solution.py:333
  5.5 1.1 %compress.1 = (bf16[16,128]{1,0:T(8,128)(2,1)S(1)}, bf16[2,16,512]{2,1,0:T(8,128)(2,1)S(1)}) custom-call(bf16[2,16,512]{2,1,0:T(8,128)(2,1)} %field_hbm.1, bf16[4,2,16,128]{3,2,1,0:T(8,128)(2,1)} %basis_hbm.1), custom_call_target="tpu_custom_call" | custom-call | flops 200000000 | tf_op jit(solution)/shard_map/compress/pallas_call | solution.py:361
  6.5 0.0 collective-permute-done.other_ref
  6.5 0.0 copy-start
  6.6 0.0 copy-start.3
  6.6 1.6 %collective-permute-start.2 = (bf16[272,128]{1,0:T(8,128)(2,1)S(1)}, bf16[272,128]{1,0:T(8,128)(2,1)S(1)}, u32[]{:S(2)}, u32[]{:S(2)}) collective-permute-start(bf16[272,128]{1,0:T(8,128)(2,1)S(1)} %get-tuple-element.18.own_ref), channel_id=1, source_target_pairs={{0,8},{1,25},{2,10},{3,27},{4,12},{5,29},{6,14},{7,31},{8,0},{9,17... | collective-permute-start | bytes 208904 | tf_op jit(solution)/shard_map/ppermute | solution.py:342
  8.1 1.5 %collective-permute-start.1 = (bf16[272,128]{1,0:T(8,128)(2,1)S(1)}, bf16[272,128]{1,0:T(8,128)(2,1)S(1)}, u32[]{:S(2)}, u32[]{:S(2)}) collective-permute-start(bf16[272,128]{1,0:T(8,128)(2,1)S(1)} %get-tuple-element.18.own_ref), channel_id=1, source_target_pairs={{0,24},{1,9},{2,26},{3,11},{4,28},{5,13},{6,30},{7,15},{8,16},{9,1... | collective-permute-start | bytes 208904 | tf_op jit(solution)/shard_map/ppermute | solution.py:342
  9.6 0.5 %collective-permute-start.6 = (bf16[16,128]{1,0:T(8,128)(2,1)S(1)}, bf16[16,128]{1,0:T(8,128)(2,1)S(1)}, u32[]{:S(2)}, u32[]{:S(2)}) collective-permute-start(bf16[16,128]{1,0:T(8,128)(2,1)S(1)} %get-tuple-element.23), channel_id=1, source_target_pairs={{0,16},{1,17},{2,18},{3,19},{4,20},{5,21},{6,22},{7,23},{8,24},{9,... | collective-permute-start | bytes 12296 | tf_op jit(solution)/shard_map/ppermute | solution.py:342
  10.1 2.4 %collective-permute-done.4.piece_ref = bf16[1024,128]{1,0:T(8,128)(2,1)S(1)} collective-permute-done((bf16[1024,128]{1,0:T(8,128)(2,1)}, bf16[1024,128]{1,0:T(8,128)(2,1)S(1)}, u32[]{:S(2)}, u32[]{:S(2)}) %collective-permute-start.4) | collective-permute-done | bytes 262176 | tf_op jit(solution)/shard_map/ppermute | solution.py:333
  12.6 0.0 collective-permute-start.5
  12.6 0.0 collective-permute-done.3.refs_1_
  12.6 0.0 copy-done
  12.6 0.0 copy-done.3
  12.6 0.6 %turn_first.1 = (bf16[4,288,256]{2,1,0:T(8,128)(2,1)S(1)}, bf16[4,288,128]{2,1,0:T(8,128)(2,1)S(1)}, bf16[4,288,128]{2,1,0:T(8,128)(2,1)S(1)}) custom-call(s32[4,8]{1,0:T(4,128)S(1)} %copy-done.3, bf16[1024,128]{1,0:T(8,128)(2,1)S(1)} %bitcast.3, bf16[1024,128]{1,0:T(8,128)(2,1)S(1)} %collective-permute-done.3.refs_1_), custom_call_target="tpu_custom_call" | custom-call | flops 3000000000 | tf_op jit(solution)/shard_map/turn_first/pallas_call | solution.py:401
  13.2 0.3 %turn_beyond.1.refs_2_ = bf16[4,288,128]{2,1,0:T(8,128)(2,1)S(1)} custom-call(bf16[4,288,256]{2,1,0:T(8,128)(2,1)S(1)} %get-tuple-element.21.pick_ref, bf16[1024,128]{1,0:T(8,128)(2,1)S(1)} %collective-permute-done.4.piece_ref), custom_call_target="tpu_custom_call" | custom-call | flops 3000000000 | tf_op jit(solution)/shard_map/turn_beyond/pallas_call | solution.py:410
  13.6 0.0 collective-permute-done.2.above_ref.refs_1_
  13.6 0.0 collective-permute-done.1.below_ref.refs_2_
  13.6 0.5 %collective-permute-done.5.last_ref = bf16[1024,128]{1,0:T(8,128)(2,1)S(1)} collective-permute-done((bf16[1024,128]{1,0:T(8,128)(2,1)S(1)}, bf16[1024,128]{1,0:T(8,128)(2,1)S(1)}, u32[]{:S(2)}, u32[]{:S(2)}) %collective-permute-start.5) | collective-permute-done | bytes 262176 | tf_op jit(solution)/shard_map/ppermute | solution.py:333
  14.1 0.6 %near_send.1 = (bf16[32,256]{1,0:T(8,128)(2,1)S(1)}, bf16[4,288,128]{2,1,0:T(8,128)(2,1)S(1)}) custom-call(bf16[4,288,256]{2,1,0:T(8,128)(2,1)S(1)} %get-tuple-element.21.pick_ref, bf16[1024,128]{1,0:T(8,128)(2,1)S(1)} %collective-permute-done.5.last_ref, bf16[272,128]{1,0:T(8,128)(2,1)S(1)} %collective-permute-done.1.below_ref.refs_2_, ...), custom_call_target="tpu_custom_call" | custom-call | flops 1000000000 | tf_op jit(solution)/shard_map/near_send/pallas_call | solution.py:421
  14.8 0.7 %collective-permute-start.7 = (bf16[32,256]{1,0:T(8,128)(2,1)S(1)}, bf16[32,256]{1,0:T(8,128)(2,1)S(1)}, u32[]{:S(2)}, u32[]{:S(2)}) collective-permute-start(bf16[32,256]{1,0:T(8,128)(2,1)S(1)} %get-tuple-element.25), channel_id=1, source_target_pairs={{0,5},{1,4},{2,7},{3,6},{4,1},{5,0},{6,3},{7,2},{8,13},{9,12},{10,... | collective-permute-start | bytes 49160 | tf_op jit(solution)/shard_map/ppermute | solution.py:333
  15.4 0.0 copy-start.1
  15.4 0.0 copy-start.2
  15.4 0.0 copy-start.4
  15.4 0.5 %near_keep.1.keep_ref = f32[32,256]{1,0:T(8,128)S(1)} custom-call(bf16[272,128]{1,0:T(8,128)(2,1)S(1)} %collective-permute-done.1.below_ref.refs_2_, bf16[272,128]{1,0:T(8,128)(2,1)S(1)} %get-tuple-element.18.own_ref, bf16[272,128]{1,0:T(8,128)(2,1)S(1)} %collective-permute-done.2.above_ref.refs_1_, bf16[4,288,128]{2,1,0:T(8,128)(2,1)S(1)} %get-tuple-element.19.refs_0_, ...), custom_call_target="tpu_custom_call" | custom-call | flops 1000000000 | tf_op jit(solution)/shard_map/near_keep/pallas_call | solution.py:429
  15.9 0.0 collective-permute-done.6.refs_3_
  15.9 0.4 %copy-done.1 = bf16[4,2,16,256]{3,2,1,0:T(8,128)(2,1)S(1)} copy-done((bf16[4,2,16,256]{3,2,1,0:T(8,128)(2,1)S(1)}, bf16[4,2,16,256]{3,2,1,0:T(8,128)(2,1)}, u32[]{:S(2)}) %copy-start.1) | copy-done | bytes 65560
  16.3 0.0 copy-done.2
  16.3 0.0 copy-done.4
  16.3 1.2 %base.1 = (f32[32,512]{1,0:T(8,128)S(1)}, bf16[128,256]{1,0:T(8,128)(2,1)S(1)}) custom-call(s32[4,8]{1,0:T(4,128)S(1)} %copy-done.3, s32[4,16]{1,0:T(4,128)S(1)} %copy-done.4, bf16[2,16,512]{2,1,0:T(8,128)(2,1)S(1)} %get-tuple-element.16.own_ref.field_ref, f32[32,256]{1,0:T(8,128)S(1)} %near_keep.1.keep_ref, bf16[4,2,16,256]{3,2,1,0:T(8,128)(2,1)S(1)} %copy-done.1, ...), custom_call_target="tpu_custom_call" | custom-call | flops 1000000000 | tf_op jit(solution)/shard_map/base/pallas_call | solution.py:459
  17.5 1.4 %collective-permute-done.7.got_ref = bf16[32,256]{1,0:T(8,128)(2,1)S(1)} collective-permute-done((bf16[32,256]{1,0:T(8,128)(2,1)S(1)}, bf16[32,256]{1,0:T(8,128)(2,1)S(1)}, u32[]{:S(2)}, u32[]{:S(2)}) %collective-permute-start.7) | collective-permute-done | bytes 16416 | tf_op jit(solution)/shard_map/ppermute | solution.py:333
  18.9 0.8 %final.1 = bf16[2,16,512]{2,1,0:T(8,128)(2,1)} custom-call(f32[32,512]{1,0:T(8,128)S(1)} %get-tuple-element.24.base_ref, bf16[32,256]{1,0:T(8,128)(2,1)S(1)} %collective-permute-done.7.got_ref, bf16[128,256]{1,0:T(8,128)(2,1)S(1)} %get-tuple-element.26.place_ref), custom_call_target="tpu_custom_call" | custom-call | flops 1000000000 | tf_op jit(solution)/shard_map/final/pallas_call | solution.py:471
  (1 shorter events, 0.0 us)
Async XLA Ops:
  0.0 6.5 %collective-permute-start = (bf16[2,16,512]{2,1,0:T(8,128)(2,1)}, bf16[2,16,512]{2,1,0:T(8,128)(2,1)S(1)}, u32[]{:S(2)}, u32[]{:S(2)}) collective-permute-start(bf16[2,16,512]{2,1,0:T(8,128)(2,1)} %field_hbm.1), channel_id=1, source_target_pairs={{0,5},{1,4},{2,7},{3,6},{4,1},{5,0},{6,3},{7,2},{8,13},{9,12},{10,... | collective-permute-start | bytes 98312 | tf_op jit(solution)/shard_map/ppermute | solution.py:333
  3.5 9.1 %collective-permute-start.4 = (bf16[1024,128]{1,0:T(8,128)(2,1)}, bf16[1024,128]{1,0:T(8,128)(2,1)S(1)}, u32[]{:S(2)}, u32[]{:S(2)}) collective-permute-start(bf16[1024,128]{1,0:T(8,128)(2,1)} %bitcast.1), channel_id=1, source_target_pairs={{0,2},{1,3},{2,0},{3,1},{4,6},{5,7},{6,4},{7,5},{8,10},{9,11},{10,... | collective-permute-start | bytes 786440 | tf_op jit(solution)/shard_map/ppermute | solution.py:333
  5.1 7.5 %collective-permute-start.3 = (bf16[1024,128]{1,0:T(8,128)(2,1)}, bf16[1024,128]{1,0:T(8,128)(2,1)S(1)}, u32[]{:S(2)}, u32[]{:S(2)}) collective-permute-start(bf16[1024,128]{1,0:T(8,128)(2,1)} %bitcast.2), channel_id=1, source_target_pairs={{0,1},{1,0},{2,3},{3,2},{4,5},{5,4},{6,7},{7,6},{8,9},{9,8},{10,11... | collective-permute-start | bytes 786440 | tf_op jit(solution)/shard_map/ppermute | solution.py:333
  6.5 6.0 %copy-start = (bf16[4,16,8,2,128]{4,3,2,1,0:T(2,128)(2,1)S(1)}, bf16[4,16,8,2,128]{4,3,2,1,0:T(2,128)(2,1)}, u32[]{:S(2)}) copy-start(bf16[4,16,8,2,128]{4,3,2,1,0:T(2,128)(2,1)} %param.8) | copy-start | bytes 786436
  6.6 6.0 %copy-start.3 = (s32[4,8]{1,0:T(4,128)S(1)}, s32[4,8]{1,0:T(4,128)}, u32[]{:S(2)}) copy-start(s32[4,8]{1,0:T(4,128)} %near_ref.3) | copy-start | bytes 388
  6.6 7.0 %collective-permute-start.2 = (bf16[272,128]{1,0:T(8,128)(2,1)S(1)}, bf16[272,128]{1,0:T(8,128)(2,1)S(1)}, u32[]{:S(2)}, u32[]{:S(2)}) collective-permute-start(bf16[272,128]{1,0:T(8,128)(2,1)S(1)} %get-tuple-element.18.own_ref), channel_id=1, source_target_pairs={{0,8},{1,25},{2,10},{3,27},{4,12},{5,29},{6,14},{7,31},{8,0},{9,17... | collective-permute-start | bytes 208904 | tf_op jit(solution)/shard_map/ppermute | solution.py:342
  8.1 5.4 %collective-permute-start.1 = (bf16[272,128]{1,0:T(8,128)(2,1)S(1)}, bf16[272,128]{1,0:T(8,128)(2,1)S(1)}, u32[]{:S(2)}, u32[]{:S(2)}) collective-permute-start(bf16[272,128]{1,0:T(8,128)(2,1)S(1)} %get-tuple-element.18.own_ref), channel_id=1, source_target_pairs={{0,24},{1,9},{2,26},{3,11},{4,28},{5,13},{6,30},{7,15},{8,16},{9,1... | collective-permute-start | bytes 208904 | tf_op jit(solution)/shard_map/ppermute | solution.py:342
  9.6 6.3 %collective-permute-start.6 = (bf16[16,128]{1,0:T(8,128)(2,1)S(1)}, bf16[16,128]{1,0:T(8,128)(2,1)S(1)}, u32[]{:S(2)}, u32[]{:S(2)}) collective-permute-start(bf16[16,128]{1,0:T(8,128)(2,1)S(1)} %get-tuple-element.23), channel_id=1, source_target_pairs={{0,16},{1,17},{2,18},{3,19},{4,20},{5,21},{6,22},{7,23},{8,24},{9,... | collective-permute-start | bytes 12296 | tf_op jit(solution)/shard_map/ppermute | solution.py:342
  12.6 1.5 %collective-permute-start.5 = (bf16[1024,128]{1,0:T(8,128)(2,1)S(1)}, bf16[1024,128]{1,0:T(8,128)(2,1)S(1)}, u32[]{:S(2)}, u32[]{:S(2)}) collective-permute-start(bf16[1024,128]{1,0:T(8,128)(2,1)S(1)} %collective-permute-done.4.piece_ref), channel_id=1, source_target_pairs={{0,1},{1,0},{2,3},{3,2},{4,5},{5,4},{6,7},{7,6},{8,9},{9,8},{10,11... | collective-permute-start | bytes 786440 | tf_op jit(solution)/shard_map/ppermute | solution.py:333
  14.8 4.1 %collective-permute-start.7 = (bf16[32,256]{1,0:T(8,128)(2,1)S(1)}, bf16[32,256]{1,0:T(8,128)(2,1)S(1)}, u32[]{:S(2)}, u32[]{:S(2)}) collective-permute-start(bf16[32,256]{1,0:T(8,128)(2,1)S(1)} %get-tuple-element.25), channel_id=1, source_target_pairs={{0,5},{1,4},{2,7},{3,6},{4,1},{5,0},{6,3},{7,2},{8,13},{9,12},{10,... | collective-permute-start | bytes 49160 | tf_op jit(solution)/shard_map/ppermute | solution.py:333
  15.4 0.8 %copy-start.1 = (bf16[4,2,16,256]{3,2,1,0:T(8,128)(2,1)S(1)}, bf16[4,2,16,256]{3,2,1,0:T(8,128)(2,1)}, u32[]{:S(2)}) copy-start(bf16[4,2,16,256]{3,2,1,0:T(8,128)(2,1)} %coupling_ref.1) | copy-start | bytes 196612
  15.4 0.8 %copy-start.2 = (bf16[4,2,16,128]{3,2,1,0:T(8,128)(2,1)S(1)}, bf16[4,2,16,128]{3,2,1,0:T(8,128)(2,1)}, u32[]{:S(2)}) copy-start(bf16[4,2,16,128]{3,2,1,0:T(8,128)(2,1)} %target_ref.1) | copy-start | bytes 98308
  15.4 0.8 %copy-start.4 = (s32[4,16]{1,0:T(4,128)S(1)}, s32[4,16]{1,0:T(4,128)}, u32[]{:S(2)}) copy-start(s32[4,16]{1,0:T(4,128)} %rank_ref.1) | copy-start | bytes 772

commit v4 on v3

--- a/solution.py
+++ b/solution.py
@@ -16,6 +16,7 @@
 
 TURN = 3.0
 TURN2 = 3.0
+EARLY = 1.0
 
 
 def params():
@@ -133,49 +134,66 @@
         refs[-1][i] = turn(pick_ref[i], piece_ref, i)
 
 
-def near_kernel(
-    sizes, inc, pick_ref, last_ref, below_ref, own_ref, above_ref, *refs
-):
+def near_early_kernel(sizes, inc, below_ref, own_ref, above_ref, *refs):
+    blocks, block = sizes[3], sizes[2]
+    part_ref, wide_ref = refs[-2:]
+    fill_windows(sizes, inc, 1, (below_ref, own_ref, above_ref), wide_ref)
+    sums = near_sums(sizes, refs[:-2], wide_ref)
+    width = part_ref.shape[1] // blocks
+    for i in range(blocks):
+        part_ref[:, i * width : i * width + sums[i].shape[1]] = sums[i]
+
+
+def near_last_kernel(sizes, pick_ref, last_ref, wide_ref, part_ref, send_ref, last_turned):
     rows, slots, block, blocks, panel_count, swaps = sizes
-    send_ref, last_turned, wide_ref = refs[-3:]
-    turned = list(refs[:-3]) + [last_turned]
     for i in range(blocks):
         last_turned[i] = turn(pick_ref[i], last_ref, i)
-    near_sums(sizes, inc, 1, turned, (below_ref, own_ref, above_ref), wide_ref, send_ref)
+    sums = near_sums(sizes, [last_turned], wide_ref)
+    width = part_ref.shape[1] // blocks
+    for pair in range(blocks // 2):
+        both = []
+        for i in (2 * pair, 2 * pair + 1):
+            both += [part_ref[:, i * width : (i + 1) * width - rows], sums[i]]
+        span = slice(pair * block, (pair + 1) * block)
+        send_ref[:, span] = jnp.concatenate(both, axis=1).astype(BF16)
 
 
 def near_keep_kernel(sizes, inc, below_ref, own_ref, above_ref, *refs):
+    block, blocks = sizes[2], sizes[3]
     keep_ref, wide_ref = refs[-2:]
-    near_sums(sizes, inc, 0, refs[:-2], (below_ref, own_ref, above_ref), wide_ref, keep_ref)
-
-
-def near_sums(sizes, inc, side, turned, windows, wide_ref, out_ref):
+    fill_windows(sizes, inc, 0, (below_ref, own_ref, above_ref), wide_ref)
+    sums = near_sums(sizes, refs[:-2], wide_ref)
+    for pair in range(blocks // 2):
+        span = slice(pair * block, (pair + 1) * block)
+        keep_ref[:, span] = jnp.concatenate(sums[2 * pair : 2 * pair + 2], axis=1)
+
+
+def fill_windows(sizes, inc, side, windows, wide_ref):
     rows, slots, block, blocks, panel_count, swaps = sizes
     below_ref, own_ref, above_ref = windows
     low, high = ((below_ref, above_ref), (above_ref, below_ref)) if swaps else ((below_ref,), (above_ref,))
     fill_wide(wide_ref, (low, (own_ref,), high), inc, blocks, block, (side,))
-    for pair in range(blocks // 2):
-        sums = []
-        for i in (2 * pair, 2 * pair + 1):
-            total = None
-            for step in range(2 * blocks + 1):
-                coefs = []
-                for ref in turned:
-                    at = step * 2 * rows
-                    coefs.append(
-                        jnp.concatenate(
-                            [ref[i, at : at + rows, :], ref[i, at + rows : at + 2 * rows, :]],
-                            axis=1,
-                        )
-                    )
-                start = (i + step) * 2 * block
-                term = nt_dot(
-                    wide_ref[:, start : start + 2 * block], jnp.concatenate(coefs, axis=0)
+
+
+def near_sums(sizes, turned, wide_ref):
+    rows, slots, block, blocks, panel_count, swaps = sizes
+    sums = []
+    for i in range(blocks):
+        total = None
+        for step in range(2 * blocks + 1):
+            at = step * 2 * rows
+            coefs = [
+                jnp.concatenate(
+                    [ref[i, at : at + rows, :], ref[i, at + rows : at + 2 * rows, :]], axis=1
                 )
-                total = term if total is None else total + term
-            sums.append(total)
-        span = slice(pair * block, (pair + 1) * block)
-        out_ref[:, span] = jnp.concatenate(sums, axis=1).astype(out_ref.dtype)
+                for ref in turned
+            ]
+            coefs = coefs[0] if len(coefs) == 1 else jnp.concatenate(coefs, axis=0)
+            start = (i + step) * 2 * block
+            term = nt_dot(wide_ref[:, start : start + 2 * block], coefs)
+            total = term if total is None else total + term
+        sums.append(total)
+    return sums
 
 
 def near_rows_kernel(sizes, inc, near_ref, coefs_ref, below_ref, own_ref, above_ref, *refs):
@@ -418,14 +436,21 @@
         wide = pltpu.VMEM((2 * inc, 3 * blocks * 2 * block), BF16)
         windows = (second, payload, first)
         turned = (own_turned, mate_turned, beyond_turned)
+        part, filled = call(
+            functools.partial(near_early_kernel, sizes, inc),
+            "near_early",
+            (near_shape[0], jax.ShapeDtypeStruct(wide.shape, BF16)),
+            [VMEM] * 6,
+            (VMEM, VMEM),
+            us=EARLY,
+        )(*windows, *turned)
         send, last_turned = call(
-            functools.partial(near_kernel, sizes, inc),
-            "near_send",
+            functools.partial(near_last_kernel, sizes),
+            "near_last",
             (near_shape[1], shape),
-            [VMEM] * 8,
+            [VMEM] * 4,
             (VMEM, VMEM),
-            [wide],
-        )(pick, last, *windows, *turned)
+        )(pick, last, filled, part)
         keep = call(
             functools.partial(near_keep_kernel, sizes, inc),
             "near_keep",

time: 19.9 us -> 19.8 us (level)
  waiting for transfers between devices: 4.37 us -> 3.62 us
  Pallas kernels: 5.1 us -> 5.47 us
  starting transfers between devices: 9.68 us -> 9.95 us
    ppermute x5, waiting for transfers between devices: 4.36 us -> 3.61 us  [across(): return lax.ppermute(x, 'inc', [(i, i ^ bit) for i in range(inc_count)])]
    pallas_call x1 -> x2, Pallas kernels: 0.64 us -> 1.01 us  [the longest x1 0.57 us: local(): call(functools.partial(near_last_kernel, sizes), 'near_last', (near_shape...]
    ppermute x5, starting transfers between devices: 6.12 us -> 6.4 us  [across(): return lax.ppermute(x, 'inc', [(i, i ^ bit) for i in range(inc_count)])]
  transfers between devices with their start and end apart: 8 -> 8, of which waited for: 3 -> 3; matrix products, arithmetic and copies ran while one was open for 0% -> 0% of each run, Pallas kernels for 22% -> 24%
where the time goes in v4:
time: 19.8 us; the launch traced here: 19.5 us
  starting transfers between devices  9.95 us (50%)
  Pallas kernels  5.47 us (28%)
  waiting for transfers between devices  3.62 us (18%)
  local copies, waits for them, and re-layouts  0.38 us (2%)
    ppermute x5, starting transfers between devices, across(): return lax.ppermute(x, 'inc', [(i, i ^ bit) for i in range(inc_count)])  6.4 us
    ppermute x5, waiting for transfers between devices, across(): return lax.ppermute(x, 'inc', [(i, i ^ bit) for i in range(inc_count)])  3.61 us
    ppermute x3, starting transfers between devices, onward(): return lax.ppermute(x, ('panel', 'inc'), pairs)  3.55 us
    pallas_call x1, Pallas kernels, local(): call(functools.partial(base_kernel, order, inc, bits, rows), 'base', (jax...  1.22 us
    pallas_call x1, Pallas kernels, local(): call(compress_kernel, 'compress', (jax.ShapeDtypeStruct((rank, blocks * 2...  1.07 us
    pallas_call x1, Pallas kernels, local(): call(final_kernel, 'final', jax.ShapeDtypeStruct((2, inc, panels), BF16),...  0.75 us
    pallas_call x1, Pallas kernels, local(): call(functools.partial(turn_first_kernel, sizes), 'turn_first', (jax.Shap...  0.63 us
    pallas_call x1, Pallas kernels, local(): call(functools.partial(near_last_kernel, sizes), 'near_last', (near_shape...  0.57 us
  transfers between devices with their start and end apart: 8, of which 3 were waited for; matrix products, arithmetic and copies ran while one was open for 0% of the time, Pallas kernels for 24%

profile of v4, /device:TPU:0, one launch (start us, length us, event | category | flops | bytes accessed | tf_op | source)
XLA Modules:
  0.0 19.5 jit_solution(11843846781984793263)
XLA Ops:
  0.0 3.5 %collective-permute-start = (bf16[2,16,512]{2,1,0:T(8,128)(2,1)}, bf16[2,16,512]{2,1,0:T(8,128)(2,1)S(1)}, u32[]{:S(2)}, u32[]{:S(2)}) collective-permute-start(bf16[2,16,512]{2,1,0:T(8,128)(2,1)} %field_hbm.1), channel_id=1, source_target_pairs={{0,5},{1,4},{2,7},{3,6},{4,1},{5,0},{6,3},{7,2},{8,13},{9,12},{10,... | collective-permute-start | bytes 98312 | tf_op jit(solution)/shard_map/ppermute | solution.py:351
  3.5 1.6 %collective-permute-start.4 = (bf16[1024,128]{1,0:T(8,128)(2,1)}, bf16[1024,128]{1,0:T(8,128)(2,1)S(1)}, u32[]{:S(2)}, u32[]{:S(2)}) collective-permute-start(bf16[1024,128]{1,0:T(8,128)(2,1)} %bitcast.1), channel_id=1, source_target_pairs={{0,2},{1,3},{2,0},{3,1},{4,6},{5,7},{6,4},{7,5},{8,10},{9,11},{10,... | collective-permute-start | bytes 786440 | tf_op jit(solution)/shard_map/ppermute | solution.py:351
  5.1 0.4 %collective-permute-start.3 = (bf16[1024,128]{1,0:T(8,128)(2,1)}, bf16[1024,128]{1,0:T(8,128)(2,1)S(1)}, u32[]{:S(2)}, u32[]{:S(2)}) collective-permute-start(bf16[1024,128]{1,0:T(8,128)(2,1)} %bitcast.2), channel_id=1, source_target_pairs={{0,1},{1,0},{2,3},{3,2},{4,5},{5,4},{6,7},{7,6},{8,9},{9,8},{10,11... | collective-permute-start | bytes 786440 | tf_op jit(solution)/shard_map/ppermute | solution.py:351
  5.5 1.1 %compress.1 = (bf16[16,128]{1,0:T(8,128)(2,1)S(1)}, bf16[2,16,512]{2,1,0:T(8,128)(2,1)S(1)}) custom-call(bf16[2,16,512]{2,1,0:T(8,128)(2,1)} %field_hbm.1, bf16[4,2,16,128]{3,2,1,0:T(8,128)(2,1)} %basis_hbm.1), custom_call_target="tpu_custom_call" | custom-call | flops 200000000 | tf_op jit(solution)/shard_map/compress/pallas_call | solution.py:379
  6.5 0.0 collective-permute-done.other_ref
  6.5 0.0 copy-start
  6.6 0.0 copy-start.3
  6.6 1.6 %collective-permute-start.2 = (bf16[272,128]{1,0:T(8,128)(2,1)S(1)}, bf16[272,128]{1,0:T(8,128)(2,1)S(1)}, u32[]{:S(2)}, u32[]{:S(2)}) collective-permute-start(bf16[272,128]{1,0:T(8,128)(2,1)S(1)} %get-tuple-element.20.own_ref), channel_id=1, source_target_pairs={{0,8},{1,25},{2,10},{3,27},{4,12},{5,29},{6,14},{7,31},{8,0},{9,17... | collective-permute-start | bytes 208904 | tf_op jit(solution)/shard_map/ppermute | solution.py:360
  8.1 1.5 %collective-permute-start.1 = (bf16[272,128]{1,0:T(8,128)(2,1)S(1)}, bf16[272,128]{1,0:T(8,128)(2,1)S(1)}, u32[]{:S(2)}, u32[]{:S(2)}) collective-permute-start(bf16[272,128]{1,0:T(8,128)(2,1)S(1)} %get-tuple-element.20.own_ref), channel_id=1, source_target_pairs={{0,24},{1,9},{2,26},{3,11},{4,28},{5,13},{6,30},{7,15},{8,16},{9,1... | collective-permute-start | bytes 208904 | tf_op jit(solution)/shard_map/ppermute | solution.py:360
  9.6 0.5 %collective-permute-start.6 = (bf16[16,128]{1,0:T(8,128)(2,1)S(1)}, bf16[16,128]{1,0:T(8,128)(2,1)S(1)}, u32[]{:S(2)}, u32[]{:S(2)}) collective-permute-start(bf16[16,128]{1,0:T(8,128)(2,1)S(1)} %get-tuple-element.27), channel_id=1, source_target_pairs={{0,16},{1,17},{2,18},{3,19},{4,20},{5,21},{6,22},{7,23},{8,24},{9,... | collective-permute-start | bytes 12296 | tf_op jit(solution)/shard_map/ppermute | solution.py:360
  10.1 2.4 %collective-permute-done.4.piece_ref = bf16[1024,128]{1,0:T(8,128)(2,1)S(1)} collective-permute-done((bf16[1024,128]{1,0:T(8,128)(2,1)}, bf16[1024,128]{1,0:T(8,128)(2,1)S(1)}, u32[]{:S(2)}, u32[]{:S(2)}) %collective-permute-start.4) | collective-permute-done | bytes 262176 | tf_op jit(solution)/shard_map/ppermute | solution.py:351
  12.6 0.0 collective-permute-start.5
  12.6 0.0 collective-permute-done.3.refs_1_
  12.6 0.0 copy-done
  12.6 0.0 copy-done.3
  12.6 0.6 %turn_first.1 = (bf16[4,288,256]{2,1,0:T(8,128)(2,1)S(1)}, bf16[4,288,128]{2,1,0:T(8,128)(2,1)S(1)}, bf16[4,288,128]{2,1,0:T(8,128)(2,1)S(1)}) custom-call(s32[4,8]{1,0:T(4,128)S(1)} %copy-done.3, bf16[1024,128]{1,0:T(8,128)(2,1)S(1)} %bitcast.3, bf16[1024,128]{1,0:T(8,128)(2,1)S(1)} %collective-permute-done.3.refs_1_), custom_call_target="tpu_custom_call" | custom-call | flops 3000000000 | tf_op jit(solution)/shard_map/turn_first/pallas_call | solution.py:419
  13.2 0.3 %turn_beyond.1.refs_2_ = bf16[4,288,128]{2,1,0:T(8,128)(2,1)S(1)} custom-call(bf16[4,288,256]{2,1,0:T(8,128)(2,1)S(1)} %get-tuple-element.23.pick_ref, bf16[1024,128]{1,0:T(8,128)(2,1)S(1)} %collective-permute-done.4.piece_ref), custom_call_target="tpu_custom_call" | custom-call | flops 3000000000 | tf_op jit(solution)/shard_map/turn_beyond/pallas_call | solution.py:428
  13.6 0.0 collective-permute-done.2.above_ref.refs_1_
  13.6 0.0 collective-permute-done.1.below_ref.refs_2_
  13.6 0.4 %near_early.1 = (f32[32,256]{1,0:T(8,128)S(1)}, bf16[32,3072]{1,0:T(8,128)(2,1)S(1)}) custom-call(bf16[272,128]{1,0:T(8,128)(2,1)S(1)} %collective-permute-done.1.below_ref.refs_2_, bf16[272,128]{1,0:T(8,128)(2,1)S(1)} %get-tuple-element.20.own_ref, bf16[272,128]{1,0:T(8,128)(2,1)S(1)} %collective-permute-done.2.above_ref.refs_1_, ...), custom_call_target="tpu_custom_call" | custom-call | flops 1000000000 | tf_op jit(solution)/shard_map/near_early/pallas_call | solution.py:439
  14.0 0.1 collective-permute-done.5.last_ref
  14.1 0.6 %near_last.1 = (bf16[32,256]{1,0:T(8,128)(2,1)S(1)}, bf16[4,288,128]{2,1,0:T(8,128)(2,1)S(1)}) custom-call(bf16[4,288,256]{2,1,0:T(8,128)(2,1)S(1)} %get-tuple-element.23.pick_ref, bf16[1024,128]{1,0:T(8,128)(2,1)S(1)} %collective-permute-done.5.last_ref, bf16[32,3072]{1,0:T(8,128)(2,1)S(1)} %get-tuple-element.24.wide_ref, ...), custom_call_target="tpu_custom_call" | custom-call | flops 1000000000 | tf_op jit(solution)/shard_map/near_last/pallas_call | solution.py:447
  14.7 0.9 %collective-permute-start.7 = (bf16[32,256]{1,0:T(8,128)(2,1)S(1)}, bf16[32,256]{1,0:T(8,128)(2,1)S(1)}, u32[]{:S(2)}, u32[]{:S(2)}) collective-permute-start(bf16[32,256]{1,0:T(8,128)(2,1)S(1)} %get-tuple-element.29), channel_id=1, source_target_pairs={{0,5},{1,4},{2,7},{3,6},{4,1},{5,0},{6,3},{7,2},{8,13},{9,12},{10,... | collective-permute-start | bytes 49160 | tf_op jit(solution)/shard_map/ppermute | solution.py:351
  15.6 0.0 copy-start.1
  15.6 0.0 copy-start.2
  15.6 0.0 copy-start.4
  15.6 0.5 %near_keep.1.keep_ref = f32[32,256]{1,0:T(8,128)S(1)} custom-call(bf16[272,128]{1,0:T(8,128)(2,1)S(1)} %collective-permute-done.1.below_ref.refs_2_, bf16[272,128]{1,0:T(8,128)(2,1)S(1)} %get-tuple-element.20.own_ref, bf16[272,128]{1,0:T(8,128)(2,1)S(1)} %collective-permute-done.2.above_ref.refs_1_, bf16[4,288,128]{2,1,0:T(8,128)(2,1)S(1)} %get-tuple-element.21.refs_0_, ...), custom_call_target="tpu_custom_call" | custom-call | flops 1000000000 | tf_op jit(solution)/shard_map/near_keep/pallas_call | solution.py:454
  16.1 0.0 collective-permute-done.6.refs_3_
  16.1 0.4 %copy-done.1 = bf16[4,2,16,256]{3,2,1,0:T(8,128)(2,1)S(1)} copy-done((bf16[4,2,16,256]{3,2,1,0:T(8,128)(2,1)S(1)}, bf16[4,2,16,256]{3,2,1,0:T(8,128)(2,1)}, u32[]{:S(2)}) %copy-start.1) | copy-done | bytes 65560
  16.5 0.0 copy-done.2
  16.5 0.0 copy-done.4
  16.5 1.2 %base.1 = (f32[32,512]{1,0:T(8,128)S(1)}, bf16[128,256]{1,0:T(8,128)(2,1)S(1)}) custom-call(s32[4,8]{1,0:T(4,128)S(1)} %copy-done.3, s32[4,16]{1,0:T(4,128)S(1)} %copy-done.4, bf16[2,16,512]{2,1,0:T(8,128)(2,1)S(1)} %get-tuple-element.18.own_ref.field_ref, f32[32,256]{1,0:T(8,128)S(1)} %near_keep.1.keep_ref, bf16[4,2,16,256]{3,2,1,0:T(8,128)(2,1)S(1)} %copy-done.1, ...), custom_call_target="tpu_custom_call" | custom-call | flops 1000000000 | tf_op jit(solution)/shard_map/base/pallas_call | solution.py:484
  17.7 1.1 %collective-permute-done.7.got_ref = bf16[32,256]{1,0:T(8,128)(2,1)S(1)} collective-permute-done((bf16[32,256]{1,0:T(8,128)(2,1)S(1)}, bf16[32,256]{1,0:T(8,128)(2,1)S(1)}, u32[]{:S(2)}, u32[]{:S(2)}) %collective-permute-start.7) | collective-permute-done | bytes 16416 | tf_op jit(solution)/shard_map/ppermute | solution.py:351
  18.8 0.8 %final.1 = bf16[2,16,512]{2,1,0:T(8,128)(2,1)} custom-call(f32[32,512]{1,0:T(8,128)S(1)} %get-tuple-element.28.base_ref, bf16[32,256]{1,0:T(8,128)(2,1)S(1)} %collective-permute-done.7.got_ref, bf16[128,256]{1,0:T(8,128)(2,1)S(1)} %get-tuple-element.30.place_ref), custom_call_target="tpu_custom_call" | custom-call | flops 1000000000 | tf_op jit(solution)/shard_map/final/pallas_call | solution.py:496
  (1 shorter events, 0.0 us)
Async XLA Ops:
  0.0 6.5 %collective-permute-start = (bf16[2,16,512]{2,1,0:T(8,128)(2,1)}, bf16[2,16,512]{2,1,0:T(8,128)(2,1)S(1)}, u32[]{:S(2)}, u32[]{:S(2)}) collective-permute-start(bf16[2,16,512]{2,1,0:T(8,128)(2,1)} %field_hbm.1), channel_id=1, source_target_pairs={{0,5},{1,4},{2,7},{3,6},{4,1},{5,0},{6,3},{7,2},{8,13},{9,12},{10,... | collective-permute-start | bytes 98312 | tf_op jit(solution)/shard_map/ppermute | solution.py:351
  3.5 9.1 %collective-permute-start.4 = (bf16[1024,128]{1,0:T(8,128)(2,1)}, bf16[1024,128]{1,0:T(8,128)(2,1)S(1)}, u32[]{:S(2)}, u32[]{:S(2)}) collective-permute-start(bf16[1024,128]{1,0:T(8,128)(2,1)} %bitcast.1), channel_id=1, source_target_pairs={{0,2},{1,3},{2,0},{3,1},{4,6},{5,7},{6,4},{7,5},{8,10},{9,11},{10,... | collective-permute-start | bytes 786440 | tf_op jit(solution)/shard_map/ppermute | solution.py:351
  5.1 7.5 %collective-permute-start.3 = (bf16[1024,128]{1,0:T(8,128)(2,1)}, bf16[1024,128]{1,0:T(8,128)(2,1)S(1)}, u32[]{:S(2)}, u32[]{:S(2)}) collective-permute-start(bf16[1024,128]{1,0:T(8,128)(2,1)} %bitcast.2), channel_id=1, source_target_pairs={{0,1},{1,0},{2,3},{3,2},{4,5},{5,4},{6,7},{7,6},{8,9},{9,8},{10,11... | collective-permute-start | bytes 786440 | tf_op jit(solution)/shard_map/ppermute | solution.py:351
  6.5 6.0 %copy-start = (bf16[4,16,8,2,128]{4,3,2,1,0:T(2,128)(2,1)S(1)}, bf16[4,16,8,2,128]{4,3,2,1,0:T(2,128)(2,1)}, u32[]{:S(2)}) copy-start(bf16[4,16,8,2,128]{4,3,2,1,0:T(2,128)(2,1)} %param.8) | copy-start | bytes 786436
  6.6 6.0 %copy-start.3 = (s32[4,8]{1,0:T(4,128)S(1)}, s32[4,8]{1,0:T(4,128)}, u32[]{:S(2)}) copy-start(s32[4,8]{1,0:T(4,128)} %near_ref.3) | copy-start | bytes 388
  6.6 7.0 %collective-permute-start.2 = (bf16[272,128]{1,0:T(8,128)(2,1)S(1)}, bf16[272,128]{1,0:T(8,128)(2,1)S(1)}, u32[]{:S(2)}, u32[]{:S(2)}) collective-permute-start(bf16[272,128]{1,0:T(8,128)(2,1)S(1)} %get-tuple-element.20.own_ref), channel_id=1, source_target_pairs={{0,8},{1,25},{2,10},{3,27},{4,12},{5,29},{6,14},{7,31},{8,0},{9,17... | collective-permute-start | bytes 208904 | tf_op jit(solution)/shard_map/ppermute | solution.py:360
  8.1 5.4 %collective-permute-start.1 = (bf16[272,128]{1,0:T(8,128)(2,1)S(1)}, bf16[272,128]{1,0:T(8,128)(2,1)S(1)}, u32[]{:S(2)}, u32[]{:S(2)}) collective-permute-start(bf16[272,128]{1,0:T(8,128)(2,1)S(1)} %get-tuple-element.20.own_ref), channel_id=1, source_target_pairs={{0,24},{1,9},{2,26},{3,11},{4,28},{5,13},{6,30},{7,15},{8,16},{9,1... | collective-permute-start | bytes 208904 | tf_op jit(solution)/shard_map/ppermute | solution.py:360
  9.6 6.5 %collective-permute-start.6 = (bf16[16,128]{1,0:T(8,128)(2,1)S(1)}, bf16[16,128]{1,0:T(8,128)(2,1)S(1)}, u32[]{:S(2)}, u32[]{:S(2)}) collective-permute-start(bf16[16,128]{1,0:T(8,128)(2,1)S(1)} %get-tuple-element.27), channel_id=1, source_target_pairs={{0,16},{1,17},{2,18},{3,19},{4,20},{5,21},{6,22},{7,23},{8,24},{9,... | collective-permute-start | bytes 12296 | tf_op jit(solution)/shard_map/ppermute | solution.py:360
  12.6 1.5 %collective-permute-start.5 = (bf16[1024,128]{1,0:T(8,128)(2,1)S(1)}, bf16[1024,128]{1,0:T(8,128)(2,1)S(1)}, u32[]{:S(2)}, u32[]{:S(2)}) collective-permute-start(bf16[1024,128]{1,0:T(8,128)(2,1)S(1)} %collective-permute-done.4.piece_ref), channel_id=1, source_target_pairs={{0,1},{1,0},{2,3},{3,2},{4,5},{5,4},{6,7},{7,6},{8,9},{9,8},{10,11... | collective-permute-start | bytes 786440 | tf_op jit(solution)/shard_map/ppermute | solution.py:351
  14.7 4.1 %collective-permute-start.7 = (bf16[32,256]{1,0:T(8,128)(2,1)S(1)}, bf16[32,256]{1,0:T(8,128)(2,1)S(1)}, u32[]{:S(2)}, u32[]{:S(2)}) collective-permute-start(bf16[32,256]{1,0:T(8,128)(2,1)S(1)} %get-tuple-element.29), channel_id=1, source_target_pairs={{0,5},{1,4},{2,7},{3,6},{4,1},{5,0},{6,3},{7,2},{8,13},{9,12},{10,... | collective-permute-start | bytes 49160 | tf_op jit(solution)/shard_map/ppermute | solution.py:351
  15.6 0.8 %copy-start.1 = (bf16[4,2,16,256]{3,2,1,0:T(8,128)(2,1)S(1)}, bf16[4,2,16,256]{3,2,1,0:T(8,128)(2,1)}, u32[]{:S(2)}) copy-start(bf16[4,2,16,256]{3,2,1,0:T(8,128)(2,1)} %coupling_ref.1) | copy-start | bytes 196612
  15.6 0.8 %copy-start.2 = (bf16[4,2,16,128]{3,2,1,0:T(8,128)(2,1)S(1)}, bf16[4,2,16,128]{3,2,1,0:T(8,128)(2,1)}, u32[]{:S(2)}) copy-start(bf16[4,2,16,128]{3,2,1,0:T(8,128)(2,1)} %target_ref.1) | copy-start | bytes 98308
  15.6 0.8 %copy-start.4 = (s32[4,16]{1,0:T(4,128)S(1)}, s32[4,16]{1,0:T(4,128)}, u32[]{:S(2)}) copy-start(s32[4,16]{1,0:T(4,128)} %rank_ref.1) | copy-start | bytes 772

commit v5 on v4

--- a/solution.py
+++ b/solution.py
@@ -29,6 +29,14 @@
 
 def in_hbm(x):
     return pltpu.with_memory_space_constraint(x, pltpu.HBM)
+
+
+def token_kernel(in_ref, out_ref):
+    out_ref[...] = jnp.zeros(out_ref.shape, F32)
+
+
+def stage_kernel(in_ref, token_ref, out_ref):
+    out_ref[...] = in_ref[...]
 
 
 def nt_dot(left, right):
@@ -373,6 +381,22 @@
     raw = near_block.reshape(blocks * lines, block)
     paired = half == 4 and rows % 16 == 0
     if paired:
+        token = call(
+            token_kernel,
+            "token",
+            jax.ShapeDtypeStruct((8, 128), F32),
+            [ANY],
+            VMEM,
+            us=0.1,
+        )(in_hbm(surface_field))
+        raw = call(
+            stage_kernel,
+            "stage",
+            jax.ShapeDtypeStruct(raw.shape, BF16),
+            [VMEM, ANY],
+            VMEM,
+            us=50.0,
+        )(raw, token)
         beyond = across(raw, 2)
         mate = across(raw, 1)
 

time: 19.8 us -> 19.6 us (0.990)
  waiting for transfers between devices: 3.62 us -> 3.33 us
    ppermute x5, waiting for transfers between devices: 3.61 us -> 3.27 us  [across(): return lax.ppermute(x, 'inc', [(i, i ^ bit) for i in range(inc_count)])]
where the time goes in v5:
time: 19.6 us; the launch traced here: 19.4 us
  starting transfers between devices  10.1 us (52%)
  Pallas kernels  5.49 us (28%)
  waiting for transfers between devices  3.33 us (17%)
  local copies, waits for them, and re-layouts  0.38 us (2%)
    ppermute x5, starting transfers between devices, across(): return lax.ppermute(x, 'inc', [(i, i ^ bit) for i in range(inc_count)])  6.57 us
    ppermute x3, starting transfers between devices, onward(): return lax.ppermute(x, ('panel', 'inc'), pairs)  3.55 us
    ppermute x5, waiting for transfers between devices, across(): return lax.ppermute(x, 'inc', [(i, i ^ bit) for i in range(inc_count)])  3.27 us
    pallas_call x1, Pallas kernels, local(): call(functools.partial(base_kernel, order, inc, bits, rows), 'base', (jax...  1.22 us
    pallas_call x1, Pallas kernels, local(): call(compress_kernel, 'compress', (jax.ShapeDtypeStruct((rank, blocks * 2...  1.07 us
    pallas_call x1, Pallas kernels, local(): call(final_kernel, 'final', jax.ShapeDtypeStruct((2, inc, panels), BF16),...  0.75 us
    pallas_call x1, Pallas kernels, local(): call(functools.partial(turn_first_kernel, sizes), 'turn_first', (jax.Shap...  0.63 us
    pallas_call x1, Pallas kernels, local(): call(functools.partial(near_last_kernel, sizes), 'near_last', (near_shape...  0.56 us
  transfers between devices with their start and end apart: 8, of which 3 were waited for; matrix products, arithmetic and copies ran while one was open for 0% of the time, Pallas kernels for 24%

profile of v5, /device:TPU:0, one launch (start us, length us, event | category | flops | bytes accessed | tf_op | source)
XLA Modules:
  0.0 19.4 jit_solution(4935418415351386371)
XLA Ops:
  0.0 0.0 copy-start
  0.0 3.5 %collective-permute-start = (bf16[2,16,512]{2,1,0:T(8,128)(2,1)}, bf16[2,16,512]{2,1,0:T(8,128)(2,1)S(1)}, u32[]{:S(2)}, u32[]{:S(2)}) collective-permute-start(bf16[2,16,512]{2,1,0:T(8,128)(2,1)} %in_ref.1), channel_id=1, source_target_pairs={{0,5},{1,4},{2,7},{3,6},{4,1},{5,0},{6,3},{7,2},{8,13},{9,12},{10,... | collective-permute-start | bytes 98312 | tf_op jit(solution)/shard_map/ppermute | solution.py:359
  3.5 0.0 copy-done
  3.5 1.6 %collective-permute-start.4 = (bf16[1024,128]{1,0:T(8,128)(2,1)S(1)}, bf16[1024,128]{1,0:T(8,128)(2,1)S(1)}, u32[]{:S(2)}, u32[]{:S(2)}) collective-permute-start(bf16[1024,128]{1,0:T(8,128)(2,1)S(1)} %stage.1.refs_0_), channel_id=1, source_target_pairs={{0,2},{1,3},{2,0},{3,1},{4,6},{5,7},{6,4},{7,5},{8,10},{9,11},{10,... | collective-permute-start | bytes 786440 | tf_op jit(solution)/shard_map/ppermute | solution.py:359
  5.1 0.4 %collective-permute-start.3 = (bf16[1024,128]{1,0:T(8,128)(2,1)S(1)}, bf16[1024,128]{1,0:T(8,128)(2,1)S(1)}, u32[]{:S(2)}, u32[]{:S(2)}) collective-permute-start(bf16[1024,128]{1,0:T(8,128)(2,1)S(1)} %stage.1.refs_0_), channel_id=1, source_target_pairs={{0,1},{1,0},{2,3},{3,2},{4,5},{5,4},{6,7},{7,6},{8,9},{9,8},{10,11... | collective-permute-start | bytes 786440 | tf_op jit(solution)/shard_map/ppermute | solution.py:359
  5.5 1.1 %compress.1 = (bf16[16,128]{1,0:T(8,128)(2,1)S(1)}, bf16[2,16,512]{2,1,0:T(8,128)(2,1)S(1)}) custom-call(bf16[2,16,512]{2,1,0:T(8,128)(2,1)} %in_ref.1, bf16[4,2,16,128]{3,2,1,0:T(8,128)(2,1)} %basis_hbm.1), custom_call_target="tpu_custom_call" | custom-call | flops 200000000 | tf_op jit(solution)/shard_map/compress/pallas_call | solution.py:403
  6.6 0.0 collective-permute-done.other_ref
  6.7 0.0 copy-start.3
  6.7 1.6 %collective-permute-start.2 = (bf16[272,128]{1,0:T(8,128)(2,1)S(1)}, bf16[272,128]{1,0:T(8,128)(2,1)S(1)}, u32[]{:S(2)}, u32[]{:S(2)}) collective-permute-start(bf16[272,128]{1,0:T(8,128)(2,1)S(1)} %get-tuple-element.20.own_ref), channel_id=1, source_target_pairs={{0,8},{1,25},{2,10},{3,27},{4,12},{5,29},{6,14},{7,31},{8,0},{9,17... | collective-permute-start | bytes 208904 | tf_op jit(solution)/shard_map/ppermute | solution.py:368
  8.2 1.5 %collective-permute-start.1 = (bf16[272,128]{1,0:T(8,128)(2,1)S(1)}, bf16[272,128]{1,0:T(8,128)(2,1)S(1)}, u32[]{:S(2)}, u32[]{:S(2)}) collective-permute-start(bf16[272,128]{1,0:T(8,128)(2,1)S(1)} %get-tuple-element.20.own_ref), channel_id=1, source_target_pairs={{0,24},{1,9},{2,26},{3,11},{4,28},{5,13},{6,30},{7,15},{8,16},{9,1... | collective-permute-start | bytes 208904 | tf_op jit(solution)/shard_map/ppermute | solution.py:368
  9.7 0.5 %collective-permute-start.6 = (bf16[16,128]{1,0:T(8,128)(2,1)S(1)}, bf16[16,128]{1,0:T(8,128)(2,1)S(1)}, u32[]{:S(2)}, u32[]{:S(2)}) collective-permute-start(bf16[16,128]{1,0:T(8,128)(2,1)S(1)} %get-tuple-element.27), channel_id=1, source_target_pairs={{0,16},{1,17},{2,18},{3,19},{4,20},{5,21},{6,22},{7,23},{8,24},{9,... | collective-permute-start | bytes 12296 | tf_op jit(solution)/shard_map/ppermute | solution.py:368
  10.2 2.2 %collective-permute-done.4.piece_ref = bf16[1024,128]{1,0:T(8,128)(2,1)S(1)} collective-permute-done((bf16[1024,128]{1,0:T(8,128)(2,1)S(1)}, bf16[1024,128]{1,0:T(8,128)(2,1)S(1)}, u32[]{:S(2)}, u32[]{:S(2)}) %collective-permute-start.4) | collective-permute-done | bytes 262176 | tf_op jit(solution)/shard_map/ppermute | solution.py:359
  12.5 0.0 collective-permute-start.5
  12.5 0.0 collective-permute-done.3.refs_1_
  12.5 0.0 copy-done.3
  12.5 0.6 %turn_first.1 = (bf16[4,288,256]{2,1,0:T(8,128)(2,1)S(1)}, bf16[4,288,128]{2,1,0:T(8,128)(2,1)S(1)}, bf16[4,288,128]{2,1,0:T(8,128)(2,1)S(1)}) custom-call(s32[4,8]{1,0:T(4,128)S(1)} %copy-done.3, bf16[1024,128]{1,0:T(8,128)(2,1)S(1)} %stage.1.refs_0_, bf16[1024,128]{1,0:T(8,128)(2,1)S(1)} %collective-permute-done.3.refs_1_), custom_call_target="tpu_custom_call" | custom-call | flops 3000000000 | tf_op jit(solution)/shard_map/turn_first/pallas_call | solution.py:443
  13.1 0.3 %turn_beyond.1.refs_2_ = bf16[4,288,128]{2,1,0:T(8,128)(2,1)S(1)} custom-call(bf16[4,288,256]{2,1,0:T(8,128)(2,1)S(1)} %get-tuple-element.23.pick_ref, bf16[1024,128]{1,0:T(8,128)(2,1)S(1)} %collective-permute-done.4.piece_ref), custom_call_target="tpu_custom_call" | custom-call | flops 3000000000 | tf_op jit(solution)/shard_map/turn_beyond/pallas_call | solution.py:452
  13.4 0.0 collective-permute-done.2.above_ref.refs_1_
  13.4 0.1 collective-permute-done.1.below_ref.refs_2_
  13.5 0.4 %near_early.1 = (f32[32,256]{1,0:T(8,128)S(1)}, bf16[32,3072]{1,0:T(8,128)(2,1)S(1)}) custom-call(bf16[272,128]{1,0:T(8,128)(2,1)S(1)} %collective-permute-done.1.below_ref.refs_2_, bf16[272,128]{1,0:T(8,128)(2,1)S(1)} %get-tuple-element.20.own_ref, bf16[272,128]{1,0:T(8,128)(2,1)S(1)} %collective-permute-done.2.above_ref.refs_1_, ...), custom_call_target="tpu_custom_call" | custom-call | flops 1000000000 | tf_op jit(solution)/shard_map/near_early/pallas_call | solution.py:463
  14.0 0.0 collective-permute-done.5.last_ref
  14.0 0.6 %near_last.1 = (bf16[32,256]{1,0:T(8,128)(2,1)S(1)}, bf16[4,288,128]{2,1,0:T(8,128)(2,1)S(1)}) custom-call(bf16[4,288,256]{2,1,0:T(8,128)(2,1)S(1)} %get-tuple-element.23.pick_ref, bf16[1024,128]{1,0:T(8,128)(2,1)S(1)} %collective-permute-done.5.last_ref, bf16[32,3072]{1,0:T(8,128)(2,1)S(1)} %get-tuple-element.24.wide_ref, ...), custom_call_target="tpu_custom_call" | custom-call | flops 1000000000 | tf_op jit(solution)/shard_map/near_last/pallas_call | solution.py:471
  14.6 1.1 %collective-permute-start.7 = (bf16[32,256]{1,0:T(8,128)(2,1)S(1)}, bf16[32,256]{1,0:T(8,128)(2,1)S(1)}, u32[]{:S(2)}, u32[]{:S(2)}) collective-permute-start(bf16[32,256]{1,0:T(8,128)(2,1)S(1)} %get-tuple-element.29), channel_id=1, source_target_pairs={{0,5},{1,4},{2,7},{3,6},{4,1},{5,0},{6,3},{7,2},{8,13},{9,12},{10,... | collective-permute-start | bytes 49160 | tf_op jit(solution)/shard_map/ppermute | solution.py:359
  15.6 0.0 copy-start.1
  15.6 0.0 copy-start.2
  15.6 0.0 copy-start.4
  15.6 0.5 %near_keep.1.keep_ref = f32[32,256]{1,0:T(8,128)S(1)} custom-call(bf16[272,128]{1,0:T(8,128)(2,1)S(1)} %collective-permute-done.1.below_ref.refs_2_, bf16[272,128]{1,0:T(8,128)(2,1)S(1)} %get-tuple-element.20.own_ref, bf16[272,128]{1,0:T(8,128)(2,1)S(1)} %collective-permute-done.2.above_ref.refs_1_, bf16[4,288,128]{2,1,0:T(8,128)(2,1)S(1)} %get-tuple-element.21.refs_0_, ...), custom_call_target="tpu_custom_call" | custom-call | flops 1000000000 | tf_op jit(solution)/shard_map/near_keep/pallas_call | solution.py:478
  16.1 0.0 collective-permute-done.6.refs_3_
  16.1 0.4 %copy-done.1 = bf16[4,2,16,256]{3,2,1,0:T(8,128)(2,1)S(1)} copy-done((bf16[4,2,16,256]{3,2,1,0:T(8,128)(2,1)S(1)}, bf16[4,2,16,256]{3,2,1,0:T(8,128)(2,1)}, u32[]{:S(2)}) %copy-start.1) | copy-done | bytes 65560
  16.5 0.0 copy-done.2
  16.5 0.0 copy-done.4
  16.5 1.2 %base.1 = (f32[32,512]{1,0:T(8,128)S(1)}, bf16[128,256]{1,0:T(8,128)(2,1)S(1)}) custom-call(s32[4,8]{1,0:T(4,128)S(1)} %copy-done.3, s32[4,16]{1,0:T(4,128)S(1)} %copy-done.4, bf16[2,16,512]{2,1,0:T(8,128)(2,1)S(1)} %get-tuple-element.18.own_ref.field_ref, f32[32,256]{1,0:T(8,128)S(1)} %near_keep.1.keep_ref, bf16[4,2,16,256]{3,2,1,0:T(8,128)(2,1)S(1)} %copy-done.1, ...), custom_call_target="tpu_custom_call" | custom-call | flops 1000000000 | tf_op jit(solution)/shard_map/base/pallas_call | solution.py:508
  17.7 1.0 %collective-permute-done.7.got_ref = bf16[32,256]{1,0:T(8,128)(2,1)S(1)} collective-permute-done((bf16[32,256]{1,0:T(8,128)(2,1)S(1)}, bf16[32,256]{1,0:T(8,128)(2,1)S(1)}, u32[]{:S(2)}, u32[]{:S(2)}) %collective-permute-start.7) | collective-permute-done | bytes 16416 | tf_op jit(solution)/shard_map/ppermute | solution.py:359
  18.7 0.8 %final.1 = bf16[2,16,512]{2,1,0:T(8,128)(2,1)} custom-call(f32[32,512]{1,0:T(8,128)S(1)} %get-tuple-element.28.base_ref, bf16[32,256]{1,0:T(8,128)(2,1)S(1)} %collective-permute-done.7.got_ref, bf16[128,256]{1,0:T(8,128)(2,1)S(1)} %get-tuple-element.30.place_ref), custom_call_target="tpu_custom_call" | custom-call | flops 1000000000 | tf_op jit(solution)/shard_map/final/pallas_call | solution.py:520
  (3 shorter events, 0.0 us)
Async XLA Ops:
  0.0 3.5 %copy-start = (bf16[4,16,8,2,128]{4,3,2,1,0:T(2,128)(2,1)S(1)}, bf16[4,16,8,2,128]{4,3,2,1,0:T(2,128)(2,1)}, u32[]{:S(2)}) copy-start(bf16[4,16,8,2,128]{4,3,2,1,0:T(2,128)(2,1)} %param.8) | copy-start | bytes 786436
  0.0 6.6 %collective-permute-start = (bf16[2,16,512]{2,1,0:T(8,128)(2,1)}, bf16[2,16,512]{2,1,0:T(8,128)(2,1)S(1)}, u32[]{:S(2)}, u32[]{:S(2)}) collective-permute-start(bf16[2,16,512]{2,1,0:T(8,128)(2,1)} %in_ref.1), channel_id=1, source_target_pairs={{0,5},{1,4},{2,7},{3,6},{4,1},{5,0},{6,3},{7,2},{8,13},{9,12},{10,... | collective-permute-start | bytes 98312 | tf_op jit(solution)/shard_map/ppermute | solution.py:359
  3.5 9.0 %collective-permute-start.4 = (bf16[1024,128]{1,0:T(8,128)(2,1)S(1)}, bf16[1024,128]{1,0:T(8,128)(2,1)S(1)}, u32[]{:S(2)}, u32[]{:S(2)}) collective-permute-start(bf16[1024,128]{1,0:T(8,128)(2,1)S(1)} %stage.1.refs_0_), channel_id=1, source_target_pairs={{0,2},{1,3},{2,0},{3,1},{4,6},{5,7},{6,4},{7,5},{8,10},{9,11},{10,... | collective-permute-start | bytes 786440 | tf_op jit(solution)/shard_map/ppermute | solution.py:359
  5.1 7.3 %collective-permute-start.3 = (bf16[1024,128]{1,0:T(8,128)(2,1)S(1)}, bf16[1024,128]{1,0:T(8,128)(2,1)S(1)}, u32[]{:S(2)}, u32[]{:S(2)}) collective-permute-start(bf16[1024,128]{1,0:T(8,128)(2,1)S(1)} %stage.1.refs_0_), channel_id=1, source_target_pairs={{0,1},{1,0},{2,3},{3,2},{4,5},{5,4},{6,7},{7,6},{8,9},{9,8},{10,11... | collective-permute-start | bytes 786440 | tf_op jit(solution)/shard_map/ppermute | solution.py:359
  6.7 5.8 %copy-start.3 = (s32[4,8]{1,0:T(4,128)S(1)}, s32[4,8]{1,0:T(4,128)}, u32[]{:S(2)}) copy-start(s32[4,8]{1,0:T(4,128)} %near_ref.3) | copy-start | bytes 388
  6.7 6.8 %collective-permute-start.2 = (bf16[272,128]{1,0:T(8,128)(2,1)S(1)}, bf16[272,128]{1,0:T(8,128)(2,1)S(1)}, u32[]{:S(2)}, u32[]{:S(2)}) collective-permute-start(bf16[272,128]{1,0:T(8,128)(2,1)S(1)} %get-tuple-element.20.own_ref), channel_id=1, source_target_pairs={{0,8},{1,25},{2,10},{3,27},{4,12},{5,29},{6,14},{7,31},{8,0},{9,17... | collective-permute-start | bytes 208904 | tf_op jit(solution)/shard_map/ppermute | solution.py:368
  8.2 5.3 %collective-permute-start.1 = (bf16[272,128]{1,0:T(8,128)(2,1)S(1)}, bf16[272,128]{1,0:T(8,128)(2,1)S(1)}, u32[]{:S(2)}, u32[]{:S(2)}) collective-permute-start(bf16[272,128]{1,0:T(8,128)(2,1)S(1)} %get-tuple-element.20.own_ref), channel_id=1, source_target_pairs={{0,24},{1,9},{2,26},{3,11},{4,28},{5,13},{6,30},{7,15},{8,16},{9,1... | collective-permute-start | bytes 208904 | tf_op jit(solution)/shard_map/ppermute | solution.py:368
  9.7 6.4 %collective-permute-start.6 = (bf16[16,128]{1,0:T(8,128)(2,1)S(1)}, bf16[16,128]{1,0:T(8,128)(2,1)S(1)}, u32[]{:S(2)}, u32[]{:S(2)}) collective-permute-start(bf16[16,128]{1,0:T(8,128)(2,1)S(1)} %get-tuple-element.27), channel_id=1, source_target_pairs={{0,16},{1,17},{2,18},{3,19},{4,20},{5,21},{6,22},{7,23},{8,24},{9,... | collective-permute-start | bytes 12296 | tf_op jit(solution)/shard_map/ppermute | solution.py:368
  12.5 1.5 %collective-permute-start.5 = (bf16[1024,128]{1,0:T(8,128)(2,1)S(1)}, bf16[1024,128]{1,0:T(8,128)(2,1)S(1)}, u32[]{:S(2)}, u32[]{:S(2)}) collective-permute-start(bf16[1024,128]{1,0:T(8,128)(2,1)S(1)} %collective-permute-done.4.piece_ref), channel_id=1, source_target_pairs={{0,1},{1,0},{2,3},{3,2},{4,5},{5,4},{6,7},{7,6},{8,9},{9,8},{10,11... | collective-permute-start | bytes 786440 | tf_op jit(solution)/shard_map/ppermute | solution.py:359
  14.6 4.1 %collective-permute-start.7 = (bf16[32,256]{1,0:T(8,128)(2,1)S(1)}, bf16[32,256]{1,0:T(8,128)(2,1)S(1)}, u32[]{:S(2)}, u32[]{:S(2)}) collective-permute-start(bf16[32,256]{1,0:T(8,128)(2,1)S(1)} %get-tuple-element.29), channel_id=1, source_target_pairs={{0,5},{1,4},{2,7},{3,6},{4,1},{5,0},{6,3},{7,2},{8,13},{9,12},{10,... | collective-permute-start | bytes 49160 | tf_op jit(solution)/shard_map/ppermute | solution.py:359
  15.6 0.8 %copy-start.1 = (bf16[4,2,16,256]{3,2,1,0:T(8,128)(2,1)S(1)}, bf16[4,2,16,256]{3,2,1,0:T(8,128)(2,1)}, u32[]{:S(2)}) copy-start(bf16[4,2,16,256]{3,2,1,0:T(8,128)(2,1)} %coupling_ref.1) | copy-start | bytes 196612
  15.6 0.8 %copy-start.2 = (bf16[4,2,16,128]{3,2,1,0:T(8,128)(2,1)S(1)}, bf16[4,2,16,128]{3,2,1,0:T(8,128)(2,1)}, u32[]{:S(2)}) copy-start(bf16[4,2,16,128]{3,2,1,0:T(8,128)(2,1)} %target_ref.1) | copy-start | bytes 98308
  15.6 0.8 %copy-start.4 = (s32[4,16]{1,0:T(4,128)S(1)}, s32[4,16]{1,0:T(4,128)}, u32[]{:S(2)}) copy-start(s32[4,16]{1,0:T(4,128)} %rank_ref.1) | copy-start | bytes 772

commit v6 on v5

--- a/solution.py
+++ b/solution.py
@@ -143,27 +143,47 @@
 
 
 def near_early_kernel(sizes, inc, below_ref, own_ref, above_ref, *refs):
-    blocks, block = sizes[3], sizes[2]
+    block, blocks = sizes[2], sizes[3]
     part_ref, wide_ref = refs[-2:]
     fill_windows(sizes, inc, 1, (below_ref, own_ref, above_ref), wide_ref)
-    sums = near_sums(sizes, refs[:-2], wide_ref)
-    width = part_ref.shape[1] // blocks
-    for i in range(blocks):
-        part_ref[:, i * width : i * width + sums[i].shape[1]] = sums[i]
+    pieces = [[ref.at[i] for ref in refs[:-2]] for i in range(blocks)]
+    for pair in range(blocks // 2):
+        total = pair_sum(sizes, pair, pieces, wide_ref)
+        part_ref[:, pair * block : pair * block + total.shape[1]] = total
 
 
 def near_last_kernel(sizes, pick_ref, last_ref, wide_ref, part_ref, send_ref, last_turned):
     rows, slots, block, blocks, panel_count, swaps = sizes
+    values = [turn(pick_ref[i], last_ref, i) for i in range(blocks)]
     for i in range(blocks):
-        last_turned[i] = turn(pick_ref[i], last_ref, i)
-    sums = near_sums(sizes, [last_turned], wide_ref)
-    width = part_ref.shape[1] // blocks
+        last_turned[i] = values[i]
     for pair in range(blocks // 2):
-        both = []
+        total = pair_sum(sizes, pair, [[value] for value in values], wide_ref)
+        span = slice(pair * block, (pair + 1) * block - total.shape[1])
+        both = jnp.concatenate([part_ref[:, span], total], axis=1)
+        send_ref[:, pair * block : (pair + 1) * block] = both.astype(BF16)
+
+
+def pair_sum(sizes, pair, pieces, wide_ref):
+    rows, slots, block, blocks, panel_count, swaps = sizes
+    reach = 2 * blocks
+    total = None
+    for j in range(2 * pair, 2 * pair + 2 + reach):
+        coefs = []
         for i in (2 * pair, 2 * pair + 1):
-            both += [part_ref[:, i * width : (i + 1) * width - rows], sums[i]]
-        span = slice(pair * block, (pair + 1) * block)
-        send_ref[:, span] = jnp.concatenate(both, axis=1).astype(BF16)
+            arrays = pieces[i]
+            if not 0 <= j - i <= reach:
+                coefs.append(jnp.zeros((len(arrays) * rows, 2 * block), BF16))
+                continue
+            at = (j - i) * 2 * rows
+            coefs += [
+                jnp.concatenate([x[at : at + rows, :], x[at + rows : at + 2 * rows, :]], axis=1)
+                for x in arrays
+            ]
+        field = wide_ref[:, j * 2 * block : (j + 1) * 2 * block]
+        term = nt_dot(field, jnp.concatenate(coefs, axis=0))
+        total = term if total is None else total + term
+    return total
 
 
 def near_keep_kernel(sizes, inc, below_ref, own_ref, above_ref, *refs):
@@ -292,11 +312,15 @@
     lane = lax.broadcasted_iota(jnp.int32, (block, 2 * block), 1)
     me_inc, groups = lax.axis_index("inc"), half // rows
     group = (sent // rows) % groups
+    which = sent // half
     if bits > 1:
+        early = 2 * half - 2 * rows
+        group = jnp.where(sent < early, (sent // rows) % (groups - 1), groups - 1)
+        which = jnp.where(sent < early, sent // (half - rows), (sent - early) // rows)
         group = lax.bitwise_xor(group, lax.bitwise_xor(me_inc, groups | 1))
     else:
         group = group + lax.bitwise_xor(me_inc // groups, 1) * groups
-    target = (sent // half) * block + group * rows + sent % rows
+    target = which * block + group * rows + sent % rows
     place_ref[...] = jnp.where(lane == target, 1.0, 0.0).astype(BF16)
     for pair in range(blocks // 2):
         own = keep_ref[:, pair * block : (pair + 1) * block]

time: 19.6 us -> 19.6 us (level)
  transfers between devices with their start and end apart: 8 -> 8, of which waited for: 3 -> 4; matrix products, arithmetic and copies ran while one was open for 0% -> 0% of each run, Pallas kernels for 24% -> 24%
where the time goes in v6:
time: 19.6 us; the launch traced here: 19.4 us
  starting transfers between devices  10.1 us (52%)
  Pallas kernels  5.42 us (28%)
  waiting for transfers between devices  3.4 us (17%)
  local copies, waits for them, and re-layouts  0.38 us (2%)
    ppermute x5, starting transfers between devices, across(): return lax.ppermute(x, 'inc', [(i, i ^ bit) for i in range(inc_count)])  6.53 us
    ppermute x3, starting transfers between devices, onward(): return lax.ppermute(x, ('panel', 'inc'), pairs)  3.55 us
    ppermute x5, waiting for transfers between devices, across(): return lax.ppermute(x, 'inc', [(i, i ^ bit) for i in range(inc_count)])  3.34 us
    pallas_call x1, Pallas kernels, local(): call(functools.partial(base_kernel, order, inc, bits, rows), 'base', (jax...  1.22 us
    pallas_call x1, Pallas kernels, local(): call(compress_kernel, 'compress', (jax.ShapeDtypeStruct((rank, blocks * 2...  1.07 us
    pallas_call x1, Pallas kernels, local(): call(final_kernel, 'final', jax.ShapeDtypeStruct((2, inc, panels), BF16),...  0.75 us
    pallas_call x1, Pallas kernels, local(): call(functools.partial(turn_first_kernel, sizes), 'turn_first', (jax.Shap...  0.63 us
    pallas_call x1, Pallas kernels, local(): call(functools.partial(near_last_kernel, sizes), 'near_last', (near_shape...  0.54 us
  transfers between devices with their start and end apart: 8, of which 4 were waited for; matrix products, arithmetic and copies ran while one was open for 0% of the time, Pallas kernels for 24%

profile of v6, /device:TPU:0, one launch (start us, length us, event | category | flops | bytes accessed | tf_op | source)
XLA Modules:
  0.0 19.4 jit_solution(12415757372938181335)
XLA Ops:
  0.0 0.0 copy-start
  0.0 3.5 %collective-permute-start = (bf16[2,16,512]{2,1,0:T(8,128)(2,1)}, bf16[2,16,512]{2,1,0:T(8,128)(2,1)S(1)}, u32[]{:S(2)}, u32[]{:S(2)}) collective-permute-start(bf16[2,16,512]{2,1,0:T(8,128)(2,1)} %in_ref.1), channel_id=1, source_target_pairs={{0,5},{1,4},{2,7},{3,6},{4,1},{5,0},{6,3},{7,2},{8,13},{9,12},{10,... | collective-permute-start | bytes 98312 | tf_op jit(solution)/shard_map/ppermute | solution.py:383
  3.5 0.0 copy-done
  3.5 1.6 %collective-permute-start.4 = (bf16[1024,128]{1,0:T(8,128)(2,1)S(1)}, bf16[1024,128]{1,0:T(8,128)(2,1)S(1)}, u32[]{:S(2)}, u32[]{:S(2)}) collective-permute-start(bf16[1024,128]{1,0:T(8,128)(2,1)S(1)} %stage.1.refs_0_), channel_id=1, source_target_pairs={{0,2},{1,3},{2,0},{3,1},{4,6},{5,7},{6,4},{7,5},{8,10},{9,11},{10,... | collective-permute-start | bytes 786440 | tf_op jit(solution)/shard_map/ppermute | solution.py:383
  5.1 0.4 %collective-permute-start.3 = (bf16[1024,128]{1,0:T(8,128)(2,1)S(1)}, bf16[1024,128]{1,0:T(8,128)(2,1)S(1)}, u32[]{:S(2)}, u32[]{:S(2)}) collective-permute-start(bf16[1024,128]{1,0:T(8,128)(2,1)S(1)} %stage.1.refs_0_), channel_id=1, source_target_pairs={{0,1},{1,0},{2,3},{3,2},{4,5},{5,4},{6,7},{7,6},{8,9},{9,8},{10,11... | collective-permute-start | bytes 786440 | tf_op jit(solution)/shard_map/ppermute | solution.py:383
  5.5 1.1 %compress.1 = (bf16[16,128]{1,0:T(8,128)(2,1)S(1)}, bf16[2,16,512]{2,1,0:T(8,128)(2,1)S(1)}) custom-call(bf16[2,16,512]{2,1,0:T(8,128)(2,1)} %in_ref.1, bf16[4,2,16,128]{3,2,1,0:T(8,128)(2,1)} %basis_hbm.1), custom_call_target="tpu_custom_call" | custom-call | flops 200000000 | tf_op jit(solution)/shard_map/compress/pallas_call | solution.py:427
  6.6 0.0 collective-permute-done.other_ref
  6.7 0.0 copy-start.3
  6.7 1.6 %collective-permute-start.2 = (bf16[272,128]{1,0:T(8,128)(2,1)S(1)}, bf16[272,128]{1,0:T(8,128)(2,1)S(1)}, u32[]{:S(2)}, u32[]{:S(2)}) collective-permute-start(bf16[272,128]{1,0:T(8,128)(2,1)S(1)} %get-tuple-element.20.own_ref), channel_id=1, source_target_pairs={{0,8},{1,25},{2,10},{3,27},{4,12},{5,29},{6,14},{7,31},{8,0},{9,17... | collective-permute-start | bytes 208904 | tf_op jit(solution)/shard_map/ppermute | solution.py:392
  8.2 1.5 %collective-permute-start.1 = (bf16[272,128]{1,0:T(8,128)(2,1)S(1)}, bf16[272,128]{1,0:T(8,128)(2,1)S(1)}, u32[]{:S(2)}, u32[]{:S(2)}) collective-permute-start(bf16[272,128]{1,0:T(8,128)(2,1)S(1)} %get-tuple-element.20.own_ref), channel_id=1, source_target_pairs={{0,24},{1,9},{2,26},{3,11},{4,28},{5,13},{6,30},{7,15},{8,16},{9,1... | collective-permute-start | bytes 208904 | tf_op jit(solution)/shard_map/ppermute | solution.py:392
  9.7 0.5 %collective-permute-start.6 = (bf16[16,128]{1,0:T(8,128)(2,1)S(1)}, bf16[16,128]{1,0:T(8,128)(2,1)S(1)}, u32[]{:S(2)}, u32[]{:S(2)}) collective-permute-start(bf16[16,128]{1,0:T(8,128)(2,1)S(1)} %get-tuple-element.27), channel_id=1, source_target_pairs={{0,16},{1,17},{2,18},{3,19},{4,20},{5,21},{6,22},{7,23},{8,24},{9,... | collective-permute-start | bytes 12296 | tf_op jit(solution)/shard_map/ppermute | solution.py:392
  10.2 2.2 %collective-permute-done.4.piece_ref = bf16[1024,128]{1,0:T(8,128)(2,1)S(1)} collective-permute-done((bf16[1024,128]{1,0:T(8,128)(2,1)S(1)}, bf16[1024,128]{1,0:T(8,128)(2,1)S(1)}, u32[]{:S(2)}, u32[]{:S(2)}) %collective-permute-start.4) | collective-permute-done | bytes 262176 | tf_op jit(solution)/shard_map/ppermute | solution.py:383
  12.5 0.0 collective-permute-start.5
  12.5 0.0 collective-permute-done.3.refs_1_
  12.5 0.0 copy-done.3
  12.5 0.6 %turn_first.1 = (bf16[4,288,256]{2,1,0:T(8,128)(2,1)S(1)}, bf16[4,288,128]{2,1,0:T(8,128)(2,1)S(1)}, bf16[4,288,128]{2,1,0:T(8,128)(2,1)S(1)}) custom-call(s32[4,8]{1,0:T(4,128)S(1)} %copy-done.3, bf16[1024,128]{1,0:T(8,128)(2,1)S(1)} %stage.1.refs_0_, bf16[1024,128]{1,0:T(8,128)(2,1)S(1)} %collective-permute-done.3.refs_1_), custom_call_target="tpu_custom_call" | custom-call | flops 3000000000 | tf_op jit(solution)/shard_map/turn_first/pallas_call | solution.py:467
  13.1 0.3 %turn_beyond.1.refs_2_ = bf16[4,288,128]{2,1,0:T(8,128)(2,1)S(1)} custom-call(bf16[4,288,256]{2,1,0:T(8,128)(2,1)S(1)} %get-tuple-element.23.pick_ref, bf16[1024,128]{1,0:T(8,128)(2,1)S(1)} %collective-permute-done.4.piece_ref), custom_call_target="tpu_custom_call" | custom-call | flops 3000000000 | tf_op jit(solution)/shard_map/turn_beyond/pallas_call | solution.py:476
  13.4 0.0 collective-permute-done.2.above_ref.refs_1_
  13.4 0.1 collective-permute-done.1.below_ref.refs_2_
  13.5 0.4 %near_early.1 = (f32[32,256]{1,0:T(8,128)S(1)}, bf16[32,3072]{1,0:T(8,128)(2,1)S(1)}) custom-call(bf16[272,128]{1,0:T(8,128)(2,1)S(1)} %collective-permute-done.1.below_ref.refs_2_, bf16[272,128]{1,0:T(8,128)(2,1)S(1)} %get-tuple-element.20.own_ref, bf16[272,128]{1,0:T(8,128)(2,1)S(1)} %collective-permute-done.2.above_ref.refs_1_, ...), custom_call_target="tpu_custom_call" | custom-call | flops 1000000000 | tf_op jit(solution)/shard_map/near_early/pallas_call | solution.py:487
  13.9 0.1 collective-permute-done.5.last_ref
  14.0 0.5 %near_last.1 = (bf16[32,256]{1,0:T(8,128)(2,1)S(1)}, bf16[4,288,128]{2,1,0:T(8,128)(2,1)S(1)}) custom-call(bf16[4,288,256]{2,1,0:T(8,128)(2,1)S(1)} %get-tuple-element.23.pick_ref, bf16[1024,128]{1,0:T(8,128)(2,1)S(1)} %collective-permute-done.5.last_ref, bf16[32,3072]{1,0:T(8,128)(2,1)S(1)} %get-tuple-element.24.wide_ref, ...), custom_call_target="tpu_custom_call" | custom-call | flops 1000000000 | tf_op jit(solution)/shard_map/near_last/pallas_call | solution.py:495
  14.5 1.0 %collective-permute-start.7 = (bf16[32,256]{1,0:T(8,128)(2,1)S(1)}, bf16[32,256]{1,0:T(8,128)(2,1)S(1)}, u32[]{:S(2)}, u32[]{:S(2)}) collective-permute-start(bf16[32,256]{1,0:T(8,128)(2,1)S(1)} %get-tuple-element.29), channel_id=1, source_target_pairs={{0,5},{1,4},{2,7},{3,6},{4,1},{5,0},{6,3},{7,2},{8,13},{9,12},{10,... | collective-permute-start | bytes 49160 | tf_op jit(solution)/shard_map/ppermute | solution.py:383
  15.5 0.0 copy-start.1
  15.6 0.0 copy-start.2
  15.6 0.0 copy-start.4
  15.6 0.5 %near_keep.1.keep_ref = f32[32,256]{1,0:T(8,128)S(1)} custom-call(bf16[272,128]{1,0:T(8,128)(2,1)S(1)} %collective-permute-done.1.below_ref.refs_2_, bf16[272,128]{1,0:T(8,128)(2,1)S(1)} %get-tuple-element.20.own_ref, bf16[272,128]{1,0:T(8,128)(2,1)S(1)} %collective-permute-done.2.above_ref.refs_1_, bf16[4,288,128]{2,1,0:T(8,128)(2,1)S(1)} %get-tuple-element.21.refs_0_, ...), custom_call_target="tpu_custom_call" | custom-call | flops 1000000000 | tf_op jit(solution)/shard_map/near_keep/pallas_call | solution.py:502
  16.0 0.0 collective-permute-done.6.refs_3_
  16.0 0.4 %copy-done.1 = bf16[4,2,16,256]{3,2,1,0:T(8,128)(2,1)S(1)} copy-done((bf16[4,2,16,256]{3,2,1,0:T(8,128)(2,1)S(1)}, bf16[4,2,16,256]{3,2,1,0:T(8,128)(2,1)}, u32[]{:S(2)}) %copy-start.1) | copy-done | bytes 65560
  16.4 0.0 copy-done.2
  16.4 0.0 copy-done.4
  16.4 1.2 %base.1 = (f32[32,512]{1,0:T(8,128)S(1)}, bf16[128,256]{1,0:T(8,128)(2,1)S(1)}) custom-call(s32[4,8]{1,0:T(4,128)S(1)} %copy-done.3, s32[4,16]{1,0:T(4,128)S(1)} %copy-done.4, bf16[2,16,512]{2,1,0:T(8,128)(2,1)S(1)} %get-tuple-element.18.own_ref.field_ref, f32[32,256]{1,0:T(8,128)S(1)} %near_keep.1.keep_ref, bf16[4,2,16,256]{3,2,1,0:T(8,128)(2,1)S(1)} %copy-done.1, ...), custom_call_target="tpu_custom_call" | custom-call | flops 1000000000 | tf_op jit(solution)/shard_map/base/pallas_call | solution.py:532
  17.6 1.0 %collective-permute-done.7.got_ref = bf16[32,256]{1,0:T(8,128)(2,1)S(1)} collective-permute-done((bf16[32,256]{1,0:T(8,128)(2,1)S(1)}, bf16[32,256]{1,0:T(8,128)(2,1)S(1)}, u32[]{:S(2)}, u32[]{:S(2)}) %collective-permute-start.7) | collective-permute-done | bytes 16416 | tf_op jit(solution)/shard_map/ppermute | solution.py:383
  18.6 0.8 %final.1 = bf16[2,16,512]{2,1,0:T(8,128)(2,1)} custom-call(f32[32,512]{1,0:T(8,128)S(1)} %get-tuple-element.28.base_ref, bf16[32,256]{1,0:T(8,128)(2,1)S(1)} %collective-permute-done.7.got_ref, bf16[128,256]{1,0:T(8,128)(2,1)S(1)} %get-tuple-element.30.place_ref), custom_call_target="tpu_custom_call" | custom-call | flops 1000000000 | tf_op jit(solution)/shard_map/final/pallas_call | solution.py:544
  (3 shorter events, 0.0 us)
Async XLA Ops:
  0.0 3.5 %copy-start = (bf16[4,16,8,2,128]{4,3,2,1,0:T(2,128)(2,1)S(1)}, bf16[4,16,8,2,128]{4,3,2,1,0:T(2,128)(2,1)}, u32[]{:S(2)}) copy-start(bf16[4,16,8,2,128]{4,3,2,1,0:T(2,128)(2,1)} %param.8) | copy-start | bytes 786436
  0.0 6.6 %collective-permute-start = (bf16[2,16,512]{2,1,0:T(8,128)(2,1)}, bf16[2,16,512]{2,1,0:T(8,128)(2,1)S(1)}, u32[]{:S(2)}, u32[]{:S(2)}) collective-permute-start(bf16[2,16,512]{2,1,0:T(8,128)(2,1)} %in_ref.1), channel_id=1, source_target_pairs={{0,5},{1,4},{2,7},{3,6},{4,1},{5,0},{6,3},{7,2},{8,13},{9,12},{10,... | collective-permute-start | bytes 98312 | tf_op jit(solution)/shard_map/ppermute | solution.py:383
  3.5 9.0 %collective-permute-start.4 = (bf16[1024,128]{1,0:T(8,128)(2,1)S(1)}, bf16[1024,128]{1,0:T(8,128)(2,1)S(1)}, u32[]{:S(2)}, u32[]{:S(2)}) collective-permute-start(bf16[1024,128]{1,0:T(8,128)(2,1)S(1)} %stage.1.refs_0_), channel_id=1, source_target_pairs={{0,2},{1,3},{2,0},{3,1},{4,6},{5,7},{6,4},{7,5},{8,10},{9,11},{10,... | collective-permute-start | bytes 786440 | tf_op jit(solution)/shard_map/ppermute | solution.py:383
  5.1 7.3 %collective-permute-start.3 = (bf16[1024,128]{1,0:T(8,128)(2,1)S(1)}, bf16[1024,128]{1,0:T(8,128)(2,1)S(1)}, u32[]{:S(2)}, u32[]{:S(2)}) collective-permute-start(bf16[1024,128]{1,0:T(8,128)(2,1)S(1)} %stage.1.refs_0_), channel_id=1, source_target_pairs={{0,1},{1,0},{2,3},{3,2},{4,5},{5,4},{6,7},{7,6},{8,9},{9,8},{10,11... | collective-permute-start | bytes 786440 | tf_op jit(solution)/shard_map/ppermute | solution.py:383
  6.7 5.8 %copy-start.3 = (s32[4,8]{1,0:T(4,128)S(1)}, s32[4,8]{1,0:T(4,128)}, u32[]{:S(2)}) copy-start(s32[4,8]{1,0:T(4,128)} %near_ref.3) | copy-start | bytes 388
  6.7 6.8 %collective-permute-start.2 = (bf16[272,128]{1,0:T(8,128)(2,1)S(1)}, bf16[272,128]{1,0:T(8,128)(2,1)S(1)}, u32[]{:S(2)}, u32[]{:S(2)}) collective-permute-start(bf16[272,128]{1,0:T(8,128)(2,1)S(1)} %get-tuple-element.20.own_ref), channel_id=1, source_target_pairs={{0,8},{1,25},{2,10},{3,27},{4,12},{5,29},{6,14},{7,31},{8,0},{9,17... | collective-permute-start | bytes 208904 | tf_op jit(solution)/shard_map/ppermute | solution.py:392
  8.2 5.3 %collective-permute-start.1 = (bf16[272,128]{1,0:T(8,128)(2,1)S(1)}, bf16[272,128]{1,0:T(8,128)(2,1)S(1)}, u32[]{:S(2)}, u32[]{:S(2)}) collective-permute-start(bf16[272,128]{1,0:T(8,128)(2,1)S(1)} %get-tuple-element.20.own_ref), channel_id=1, source_target_pairs={{0,24},{1,9},{2,26},{3,11},{4,28},{5,13},{6,30},{7,15},{8,16},{9,1... | collective-permute-start | bytes 208904 | tf_op jit(solution)/shard_map/ppermute | solution.py:392
  9.7 6.3 %collective-permute-start.6 = (bf16[16,128]{1,0:T(8,128)(2,1)S(1)}, bf16[16,128]{1,0:T(8,128)(2,1)S(1)}, u32[]{:S(2)}, u32[]{:S(2)}) collective-permute-start(bf16[16,128]{1,0:T(8,128)(2,1)S(1)} %get-tuple-element.27), channel_id=1, source_target_pairs={{0,16},{1,17},{2,18},{3,19},{4,20},{5,21},{6,22},{7,23},{8,24},{9,... | collective-permute-start | bytes 12296 | tf_op jit(solution)/shard_map/ppermute | solution.py:392
  12.5 1.5 %collective-permute-start.5 = (bf16[1024,128]{1,0:T(8,128)(2,1)S(1)}, bf16[1024,128]{1,0:T(8,128)(2,1)S(1)}, u32[]{:S(2)}, u32[]{:S(2)}) collective-permute-start(bf16[1024,128]{1,0:T(8,128)(2,1)S(1)} %collective-permute-done.4.piece_ref), channel_id=1, source_target_pairs={{0,1},{1,0},{2,3},{3,2},{4,5},{5,4},{6,7},{7,6},{8,9},{9,8},{10,11... | collective-permute-start | bytes 786440 | tf_op jit(solution)/shard_map/ppermute | solution.py:383
  14.5 4.1 %collective-permute-start.7 = (bf16[32,256]{1,0:T(8,128)(2,1)S(1)}, bf16[32,256]{1,0:T(8,128)(2,1)S(1)}, u32[]{:S(2)}, u32[]{:S(2)}) collective-permute-start(bf16[32,256]{1,0:T(8,128)(2,1)S(1)} %get-tuple-element.29), channel_id=1, source_target_pairs={{0,5},{1,4},{2,7},{3,6},{4,1},{5,0},{6,3},{7,2},{8,13},{9,12},{10,... | collective-permute-start | bytes 49160 | tf_op jit(solution)/shard_map/ppermute | solution.py:383
  15.5 0.8 %copy-start.1 = (bf16[4,2,16,256]{3,2,1,0:T(8,128)(2,1)S(1)}, bf16[4,2,16,256]{3,2,1,0:T(8,128)(2,1)}, u32[]{:S(2)}) copy-start(bf16[4,2,16,256]{3,2,1,0:T(8,128)(2,1)} %coupling_ref.1) | copy-start | bytes 196612
  15.6 0.8 %copy-start.2 = (bf16[4,2,16,128]{3,2,1,0:T(8,128)(2,1)S(1)}, bf16[4,2,16,128]{3,2,1,0:T(8,128)(2,1)}, u32[]{:S(2)}) copy-start(bf16[4,2,16,128]{3,2,1,0:T(8,128)(2,1)} %target_ref.1) | copy-start | bytes 98308
  15.6 0.8 %copy-start.4 = (s32[4,16]{1,0:T(4,128)S(1)}, s32[4,16]{1,0:T(4,128)}, u32[]{:S(2)}) copy-start(s32[4,16]{1,0:T(4,128)} %rank_ref.1) | copy-start | bytes 772

commit v7 on v6

--- a/solution.py
+++ b/solution.py
@@ -55,15 +55,8 @@
     return jnp.concatenate([-pair_lanes[:, width:], pair_lanes[:, :width]], axis=1)
 
 
-def compress_kernel(field_hbm, basis_hbm, packed_ref, field_ref, basis_ref, sems):
-    copies = [
-        pltpu.make_async_copy(field_hbm, field_ref, sems.at[0]),
-        pltpu.make_async_copy(basis_hbm, basis_ref, sems.at[1]),
-    ]
-    for copy in copies:
-        copy.start()
-    for copy in copies:
-        copy.wait()
+def compress_kernel(own_ref, basis_ref, packed_ref, field_ref):
+    field_ref[...] = own_ref[...]
     _, inc, _ = field_ref.shape
     blocks, _, rank, block = basis_ref.shape
     pieces = []
@@ -431,14 +424,10 @@
             jax.ShapeDtypeStruct((rank, blocks * 2 * inc), BF16),
             jax.ShapeDtypeStruct(surface_field.shape, BF16),
         ),
-        [ANY] * 2,
+        [VMEM] * 2,
         (VMEM, VMEM),
-        [
-            pltpu.VMEM(source_basis.shape, BF16),
-            pltpu.SemaphoreType.DMA((2,)),
-        ],
         us=0.2,
-    )(in_hbm(surface_field), in_hbm(source_basis))
+    )(surface_field, source_basis)
     payload, again = call(
         pack_kernel,
         "pack",

time: 19.6 us -> 19.6 us (level)
  waiting for transfers between devices: 3.4 us -> 4.25 us
  Pallas kernels: 5.42 us -> 4.63 us
    ppermute x5, waiting for transfers between devices: 3.34 us -> 4.24 us  [across(): return lax.ppermute(x, 'inc', [(i, i ^ bit) for i in range(inc_count)])]
    pallas_call x1, Pallas kernels: 1.07 us -> 0.27 us  [local(): call(compress_kernel, 'compress', (jax.ShapeDtypeStruct((rank, blocks * 2...]
  transfers between devices with their start and end apart: 8 -> 8, of which waited for: 4 -> 3; matrix products, arithmetic and copies ran while one was open for 0% -> 0% of each run, Pallas kernels for 24% -> 20%
where the time goes in v7:
time: 19.6 us; the launch traced here: 19.4 us
  starting transfers between devices  10.1 us (52%)
  Pallas kernels  4.63 us (24%)
  waiting for transfers between devices  4.25 us (22%)
  local copies, waits for them, and re-layouts  0.38 us (2%)
    ppermute x5, starting transfers between devices, across(): return lax.ppermute(x, 'inc', [(i, i ^ bit) for i in range(inc_count)])  6.51 us
    ppermute x5, waiting for transfers between devices, across(): return lax.ppermute(x, 'inc', [(i, i ^ bit) for i in range(inc_count)])  4.24 us
    ppermute x3, starting transfers between devices, onward(): return lax.ppermute(x, ('panel', 'inc'), pairs)  3.55 us
    pallas_call x1, Pallas kernels, local(): call(functools.partial(base_kernel, order, inc, bits, rows), 'base', (jax...  1.22 us
    pallas_call x1, Pallas kernels, local(): call(final_kernel, 'final', jax.ShapeDtypeStruct((2, inc, panels), BF16),...  0.75 us
    pallas_call x1, Pallas kernels, local(): call(functools.partial(turn_first_kernel, sizes), 'turn_first', (jax.Shap...  0.63 us
    pallas_call x1, Pallas kernels, local(): call(functools.partial(near_last_kernel, sizes), 'near_last', (near_shape...  0.54 us
    pallas_call x1, Pallas kernels, local(): call(functools.partial(near_keep_kernel, sizes, inc), 'near_keep', near_s...  0.46 us
  transfers between devices with their start and end apart: 8, of which 3 were waited for; matrix products, arithmetic and copies ran while one was open for 0% of the time, Pallas kernels for 20%

profile of v7, /device:TPU:0, one launch (start us, length us, event | category | flops | bytes accessed | tf_op | source)
XLA Modules:
  0.0 19.4 jit_solution(16270749227292882279)
XLA Ops:
  0.0 0.0 copy-start
  0.0 3.5 %collective-permute-start = (bf16[2,16,512]{2,1,0:T(8,128)(2,1)}, bf16[2,16,512]{2,1,0:T(8,128)(2,1)S(1)}, u32[]{:S(2)}, u32[]{:S(2)}) collective-permute-start(bf16[2,16,512]{2,1,0:T(8,128)(2,1)} %in_ref.1), channel_id=1, source_target_pairs={{0,5},{1,4},{2,7},{3,6},{4,1},{5,0},{6,3},{7,2},{8,13},{9,12},{10,... | collective-permute-start | bytes 98312 | tf_op jit(solution)/shard_map/ppermute | solution.py:376
  3.5 0.0 copy-done
  3.5 0.0 copy-start.2
  3.5 0.0 copy-start.3
  3.5 1.6 %collective-permute-start.4 = (bf16[1024,128]{1,0:T(8,128)(2,1)S(1)}, bf16[1024,128]{1,0:T(8,128)(2,1)S(1)}, u32[]{:S(2)}, u32[]{:S(2)}) collective-permute-start(bf16[1024,128]{1,0:T(8,128)(2,1)S(1)} %stage.1.refs_0_), channel_id=1, source_target_pairs={{0,2},{1,3},{2,0},{3,1},{4,6},{5,7},{6,4},{7,5},{8,10},{9,11},{10,... | collective-permute-start | bytes 786440 | tf_op jit(solution)/shard_map/ppermute | solution.py:376
  5.2 0.4 %collective-permute-start.3 = (bf16[1024,128]{1,0:T(8,128)(2,1)S(1)}, bf16[1024,128]{1,0:T(8,128)(2,1)S(1)}, u32[]{:S(2)}, u32[]{:S(2)}) collective-permute-start(bf16[1024,128]{1,0:T(8,128)(2,1)S(1)} %stage.1.refs_0_), channel_id=1, source_target_pairs={{0,1},{1,0},{2,3},{3,2},{4,5},{5,4},{6,7},{7,6},{8,9},{9,8},{10,11... | collective-permute-start | bytes 786440 | tf_op jit(solution)/shard_map/ppermute | solution.py:376
  5.6 0.0 copy-done.2
  5.6 0.0 copy-done.3
  5.6 0.3 %compress.1 = (bf16[16,128]{1,0:T(8,128)(2,1)S(1)}, bf16[2,16,512]{2,1,0:T(8,128)(2,1)S(1)}) custom-call(bf16[2,16,512]{2,1,0:T(8,128)(2,1)S(1)} %copy-done.3, bf16[4,2,16,128]{3,2,1,0:T(8,128)(2,1)S(1)} %copy-done.2), custom_call_target="tpu_custom_call" | custom-call | flops 200000000 | tf_op jit(solution)/shard_map/compress/pallas_call | solution.py:420
  5.8 0.0 collective-permute-done.other_ref
  5.9 0.0 copy-start.5
  5.9 1.7 %collective-permute-start.2 = (bf16[272,128]{1,0:T(8,128)(2,1)S(1)}, bf16[272,128]{1,0:T(8,128)(2,1)S(1)}, u32[]{:S(2)}, u32[]{:S(2)}) collective-permute-start(bf16[272,128]{1,0:T(8,128)(2,1)S(1)} %get-tuple-element.20.own_ref), channel_id=1, source_target_pairs={{0,8},{1,25},{2,10},{3,27},{4,12},{5,29},{6,14},{7,31},{8,0},{9,17... | collective-permute-start | bytes 208904 | tf_op jit(solution)/shard_map/ppermute | solution.py:385
  7.6 1.5 %collective-permute-start.1 = (bf16[272,128]{1,0:T(8,128)(2,1)S(1)}, bf16[272,128]{1,0:T(8,128)(2,1)S(1)}, u32[]{:S(2)}, u32[]{:S(2)}) collective-permute-start(bf16[272,128]{1,0:T(8,128)(2,1)S(1)} %get-tuple-element.20.own_ref), channel_id=1, source_target_pairs={{0,24},{1,9},{2,26},{3,11},{4,28},{5,13},{6,30},{7,15},{8,16},{9,1... | collective-permute-start | bytes 208904 | tf_op jit(solution)/shard_map/ppermute | solution.py:385
  9.1 0.3 %collective-permute-start.6 = (bf16[16,128]{1,0:T(8,128)(2,1)S(1)}, bf16[16,128]{1,0:T(8,128)(2,1)S(1)}, u32[]{:S(2)}, u32[]{:S(2)}) collective-permute-start(bf16[16,128]{1,0:T(8,128)(2,1)S(1)} %get-tuple-element.27), channel_id=1, source_target_pairs={{0,16},{1,17},{2,18},{3,19},{4,20},{5,21},{6,22},{7,23},{8,24},{9,... | collective-permute-start | bytes 12296 | tf_op jit(solution)/shard_map/ppermute | solution.py:385
  9.4 3.0 %collective-permute-done.4.piece_ref = bf16[1024,128]{1,0:T(8,128)(2,1)S(1)} collective-permute-done((bf16[1024,128]{1,0:T(8,128)(2,1)S(1)}, bf16[1024,128]{1,0:T(8,128)(2,1)S(1)}, u32[]{:S(2)}, u32[]{:S(2)}) %collective-permute-start.4) | collective-permute-done | bytes 262176 | tf_op jit(solution)/shard_map/ppermute | solution.py:376
  12.5 0.0 collective-permute-start.5
  12.5 0.0 collective-permute-done.3.refs_1_
  12.5 0.0 copy-done.5
  12.5 0.6 %turn_first.1 = (bf16[4,288,256]{2,1,0:T(8,128)(2,1)S(1)}, bf16[4,288,128]{2,1,0:T(8,128)(2,1)S(1)}, bf16[4,288,128]{2,1,0:T(8,128)(2,1)S(1)}) custom-call(s32[4,8]{1,0:T(4,128)S(1)} %copy-done.5, bf16[1024,128]{1,0:T(8,128)(2,1)S(1)} %stage.1.refs_0_, bf16[1024,128]{1,0:T(8,128)(2,1)S(1)} %collective-permute-done.3.refs_1_), custom_call_target="tpu_custom_call" | custom-call | flops 3000000000 | tf_op jit(solution)/shard_map/turn_first/pallas_call | solution.py:456
  13.1 0.3 %turn_beyond.1.refs_2_ = bf16[4,288,128]{2,1,0:T(8,128)(2,1)S(1)} custom-call(bf16[4,288,256]{2,1,0:T(8,128)(2,1)S(1)} %get-tuple-element.23.pick_ref, bf16[1024,128]{1,0:T(8,128)(2,1)S(1)} %collective-permute-done.4.piece_ref), custom_call_target="tpu_custom_call" | custom-call | flops 3000000000 | tf_op jit(solution)/shard_map/turn_beyond/pallas_call | solution.py:465
  13.4 0.0 collective-permute-done.2.above_ref.refs_1_
  13.5 0.0 collective-permute-done.1.below_ref.refs_2_
  13.5 0.4 %near_early.1 = (f32[32,256]{1,0:T(8,128)S(1)}, bf16[32,3072]{1,0:T(8,128)(2,1)S(1)}) custom-call(bf16[272,128]{1,0:T(8,128)(2,1)S(1)} %collective-permute-done.1.below_ref.refs_2_, bf16[272,128]{1,0:T(8,128)(2,1)S(1)} %get-tuple-element.20.own_ref, bf16[272,128]{1,0:T(8,128)(2,1)S(1)} %collective-permute-done.2.above_ref.refs_1_, ...), custom_call_target="tpu_custom_call" | custom-call | flops 1000000000 | tf_op jit(solution)/shard_map/near_early/pallas_call | solution.py:476
  13.9 0.1 collective-permute-done.5.last_ref
  14.0 0.5 %near_last.1 = (bf16[32,256]{1,0:T(8,128)(2,1)S(1)}, bf16[4,288,128]{2,1,0:T(8,128)(2,1)S(1)}) custom-call(bf16[4,288,256]{2,1,0:T(8,128)(2,1)S(1)} %get-tuple-element.23.pick_ref, bf16[1024,128]{1,0:T(8,128)(2,1)S(1)} %collective-permute-done.5.last_ref, bf16[32,3072]{1,0:T(8,128)(2,1)S(1)} %get-tuple-element.24.wide_ref, ...), custom_call_target="tpu_custom_call" | custom-call | flops 1000000000 | tf_op jit(solution)/shard_map/near_last/pallas_call | solution.py:484
  14.6 1.0 %collective-permute-start.7 = (bf16[32,256]{1,0:T(8,128)(2,1)S(1)}, bf16[32,256]{1,0:T(8,128)(2,1)S(1)}, u32[]{:S(2)}, u32[]{:S(2)}) collective-permute-start(bf16[32,256]{1,0:T(8,128)(2,1)S(1)} %get-tuple-element.29), channel_id=1, source_target_pairs={{0,5},{1,4},{2,7},{3,6},{4,1},{5,0},{6,3},{7,2},{8,13},{9,12},{10,... | collective-permute-start | bytes 49160 | tf_op jit(solution)/shard_map/ppermute | solution.py:376
  15.5 0.0 copy-start.1
  15.5 0.0 copy-start.4
  15.5 0.0 copy-start.6
  15.6 0.5 %near_keep.1.keep_ref = f32[32,256]{1,0:T(8,128)S(1)} custom-call(bf16[272,128]{1,0:T(8,128)(2,1)S(1)} %collective-permute-done.1.below_ref.refs_2_, bf16[272,128]{1,0:T(8,128)(2,1)S(1)} %get-tuple-element.20.own_ref, bf16[272,128]{1,0:T(8,128)(2,1)S(1)} %collective-permute-done.2.above_ref.refs_1_, bf16[4,288,128]{2,1,0:T(8,128)(2,1)S(1)} %get-tuple-element.21.refs_0_, ...), custom_call_target="tpu_custom_call" | custom-call | flops 1000000000 | tf_op jit(solution)/shard_map/near_keep/pallas_call | solution.py:491
  16.0 0.0 collective-permute-done.6.refs_3_
  16.0 0.4 %copy-done.1 = bf16[4,2,16,256]{3,2,1,0:T(8,128)(2,1)S(1)} copy-done((bf16[4,2,16,256]{3,2,1,0:T(8,128)(2,1)S(1)}, bf16[4,2,16,256]{3,2,1,0:T(8,128)(2,1)}, u32[]{:S(2)}) %copy-start.1) | copy-done | bytes 65560
  16.4 0.0 copy-done.4
  16.4 0.0 copy-done.6
  16.4 1.2 %base.1 = (f32[32,512]{1,0:T(8,128)S(1)}, bf16[128,256]{1,0:T(8,128)(2,1)S(1)}) custom-call(s32[4,8]{1,0:T(4,128)S(1)} %copy-done.5, s32[4,16]{1,0:T(4,128)S(1)} %copy-done.6, bf16[2,16,512]{2,1,0:T(8,128)(2,1)S(1)} %get-tuple-element.18.own_ref.field_ref, f32[32,256]{1,0:T(8,128)S(1)} %near_keep.1.keep_ref, bf16[4,2,16,256]{3,2,1,0:T(8,128)(2,1)S(1)} %copy-done.1, ...), custom_call_target="tpu_custom_call" | custom-call | flops 1000000000 | tf_op jit(solution)/shard_map/base/pallas_call | solution.py:521
  17.6 1.1 %collective-permute-done.7.got_ref = bf16[32,256]{1,0:T(8,128)(2,1)S(1)} collective-permute-done((bf16[32,256]{1,0:T(8,128)(2,1)S(1)}, bf16[32,256]{1,0:T(8,128)(2,1)S(1)}, u32[]{:S(2)}, u32[]{:S(2)}) %collective-permute-start.7) | collective-permute-done | bytes 16416 | tf_op jit(solution)/shard_map/ppermute | solution.py:376
  18.7 0.8 %final.1 = bf16[2,16,512]{2,1,0:T(8,128)(2,1)} custom-call(f32[32,512]{1,0:T(8,128)S(1)} %get-tuple-element.28.base_ref, bf16[32,256]{1,0:T(8,128)(2,1)S(1)} %collective-permute-done.7.got_ref, bf16[128,256]{1,0:T(8,128)(2,1)S(1)} %get-tuple-element.30.place_ref), custom_call_target="tpu_custom_call" | custom-call | flops 1000000000 | tf_op jit(solution)/shard_map/final/pallas_call | solution.py:533
  (3 shorter events, 0.0 us)
Async XLA Ops:
  0.0 3.5 %copy-start = (bf16[4,16,8,2,128]{4,3,2,1,0:T(2,128)(2,1)S(1)}, bf16[4,16,8,2,128]{4,3,2,1,0:T(2,128)(2,1)}, u32[]{:S(2)}) copy-start(bf16[4,16,8,2,128]{4,3,2,1,0:T(2,128)(2,1)} %param.8) | copy-start | bytes 786436
  0.0 5.8 %collective-permute-start = (bf16[2,16,512]{2,1,0:T(8,128)(2,1)}, bf16[2,16,512]{2,1,0:T(8,128)(2,1)S(1)}, u32[]{:S(2)}, u32[]{:S(2)}) collective-permute-start(bf16[2,16,512]{2,1,0:T(8,128)(2,1)} %in_ref.1), channel_id=1, source_target_pairs={{0,5},{1,4},{2,7},{3,6},{4,1},{5,0},{6,3},{7,2},{8,13},{9,12},{10,... | collective-permute-start | bytes 98312 | tf_op jit(solution)/shard_map/ppermute | solution.py:376
  3.5 2.1 %copy-start.2 = (bf16[4,2,16,128]{3,2,1,0:T(8,128)(2,1)S(1)}, bf16[4,2,16,128]{3,2,1,0:T(8,128)(2,1)}, u32[]{:S(2)}) copy-start(bf16[4,2,16,128]{3,2,1,0:T(8,128)(2,1)} %basis_ref.1) | copy-start | bytes 98308
  3.5 2.1 %copy-start.3 = (bf16[2,16,512]{2,1,0:T(8,128)(2,1)S(1)}, bf16[2,16,512]{2,1,0:T(8,128)(2,1)}, u32[]{:S(2)}) copy-start(bf16[2,16,512]{2,1,0:T(8,128)(2,1)} %in_ref.1) | copy-start | bytes 98308
  3.5 9.0 %collective-permute-start.4 = (bf16[1024,128]{1,0:T(8,128)(2,1)S(1)}, bf16[1024,128]{1,0:T(8,128)(2,1)S(1)}, u32[]{:S(2)}, u32[]{:S(2)}) collective-permute-start(bf16[1024,128]{1,0:T(8,128)(2,1)S(1)} %stage.1.refs_0_), channel_id=1, source_target_pairs={{0,2},{1,3},{2,0},{3,1},{4,6},{5,7},{6,4},{7,5},{8,10},{9,11},{10,... | collective-permute-start | bytes 786440 | tf_op jit(solution)/shard_map/ppermute | solution.py:376
  5.2 7.3 %collective-permute-start.3 = (bf16[1024,128]{1,0:T(8,128)(2,1)S(1)}, bf16[1024,128]{1,0:T(8,128)(2,1)S(1)}, u32[]{:S(2)}, u32[]{:S(2)}) collective-permute-start(bf16[1024,128]{1,0:T(8,128)(2,1)S(1)} %stage.1.refs_0_), channel_id=1, source_target_pairs={{0,1},{1,0},{2,3},{3,2},{4,5},{5,4},{6,7},{7,6},{8,9},{9,8},{10,11... | collective-permute-start | bytes 786440 | tf_op jit(solution)/shard_map/ppermute | solution.py:376
  5.9 6.6 %copy-start.5 = (s32[4,8]{1,0:T(4,128)S(1)}, s32[4,8]{1,0:T(4,128)}, u32[]{:S(2)}) copy-start(s32[4,8]{1,0:T(4,128)} %near_ref.3) | copy-start | bytes 388
  5.9 7.6 %collective-permute-start.2 = (bf16[272,128]{1,0:T(8,128)(2,1)S(1)}, bf16[272,128]{1,0:T(8,128)(2,1)S(1)}, u32[]{:S(2)}, u32[]{:S(2)}) collective-permute-start(bf16[272,128]{1,0:T(8,128)(2,1)S(1)} %get-tuple-element.20.own_ref), channel_id=1, source_target_pairs={{0,8},{1,25},{2,10},{3,27},{4,12},{5,29},{6,14},{7,31},{8,0},{9,17... | collective-permute-start | bytes 208904 | tf_op jit(solution)/shard_map/ppermute | solution.py:385
  7.6 5.9 %collective-permute-start.1 = (bf16[272,128]{1,0:T(8,128)(2,1)S(1)}, bf16[272,128]{1,0:T(8,128)(2,1)S(1)}, u32[]{:S(2)}, u32[]{:S(2)}) collective-permute-start(bf16[272,128]{1,0:T(8,128)(2,1)S(1)} %get-tuple-element.20.own_ref), channel_id=1, source_target_pairs={{0,24},{1,9},{2,26},{3,11},{4,28},{5,13},{6,30},{7,15},{8,16},{9,1... | collective-permute-start | bytes 208904 | tf_op jit(solution)/shard_map/ppermute | solution.py:385
  9.1 6.9 %collective-permute-start.6 = (bf16[16,128]{1,0:T(8,128)(2,1)S(1)}, bf16[16,128]{1,0:T(8,128)(2,1)S(1)}, u32[]{:S(2)}, u32[]{:S(2)}) collective-permute-start(bf16[16,128]{1,0:T(8,128)(2,1)S(1)} %get-tuple-element.27), channel_id=1, source_target_pairs={{0,16},{1,17},{2,18},{3,19},{4,20},{5,21},{6,22},{7,23},{8,24},{9,... | collective-permute-start | bytes 12296 | tf_op jit(solution)/shard_map/ppermute | solution.py:385
  12.5 1.5 %collective-permute-start.5 = (bf16[1024,128]{1,0:T(8,128)(2,1)S(1)}, bf16[1024,128]{1,0:T(8,128)(2,1)S(1)}, u32[]{:S(2)}, u32[]{:S(2)}) collective-permute-start(bf16[1024,128]{1,0:T(8,128)(2,1)S(1)} %collective-permute-done.4.piece_ref), channel_id=1, source_target_pairs={{0,1},{1,0},{2,3},{3,2},{4,5},{5,4},{6,7},{7,6},{8,9},{9,8},{10,11... | collective-permute-start | bytes 786440 | tf_op jit(solution)/shard_map/ppermute | solution.py:376
  14.6 4.1 %collective-permute-start.7 = (bf16[32,256]{1,0:T(8,128)(2,1)S(1)}, bf16[32,256]{1,0:T(8,128)(2,1)S(1)}, u32[]{:S(2)}, u32[]{:S(2)}) collective-permute-start(bf16[32,256]{1,0:T(8,128)(2,1)S(1)} %get-tuple-element.29), channel_id=1, source_target_pairs={{0,5},{1,4},{2,7},{3,6},{4,1},{5,0},{6,3},{7,2},{8,13},{9,12},{10,... | collective-permute-start | bytes 49160 | tf_op jit(solution)/shard_map/ppermute | solution.py:376
  15.5 0.8 %copy-start.1 = (bf16[4,2,16,256]{3,2,1,0:T(8,128)(2,1)S(1)}, bf16[4,2,16,256]{3,2,1,0:T(8,128)(2,1)}, u32[]{:S(2)}) copy-start(bf16[4,2,16,256]{3,2,1,0:T(8,128)(2,1)} %coupling_ref.1) | copy-start | bytes 196612
  15.5 0.8 %copy-start.4 = (bf16[4,2,16,128]{3,2,1,0:T(8,128)(2,1)S(1)}, bf16[4,2,16,128]{3,2,1,0:T(8,128)(2,1)}, u32[]{:S(2)}) copy-start(bf16[4,2,16,128]{3,2,1,0:T(8,128)(2,1)} %target_ref.1) | copy-start | bytes 98308
  15.5 0.8 %copy-start.6 = (s32[4,16]{1,0:T(4,128)S(1)}, s32[4,16]{1,0:T(4,128)}, u32[]{:S(2)}) copy-start(s32[4,16]{1,0:T(4,128)} %rank_ref.1) | copy-start | bytes 772
